TPU v7x, 512 devices: a whole 4x4x16 slice. The times are simulated.
512 devices in a mesh: dp: 32 (over x, y, core), tensor: 16 (over z).
Axes of the slice: x: 4, y: 4, z: 16, core: 2. Of those that a mesh axis runs over, the one named last changes fastest.
Arguments:
- stored_rows: bfloat16 [1024, 14336], P(('dp', 'tensor')), may hold values from -6 to 6
- kv_weight: bfloat16 [14336, 2, 14336], P('dp', None, 'tensor'), may hold values from -0.046875 to 0.046875
- lengths: int32 [64], replicated, may hold values from 1 to 16, 768 in all
- new_place: int32 [64], replicated, may hold values from 0 to 63, each once
- query: bfloat16 [64, 14336], P('dp', 'tensor'), may hold values from -80 to 80
- new_kv: bfloat16 [64, 2, 14336], P('dp', None, 'tensor'), may hold values from -4 to 4
Outputs:
- kv_cache: bfloat16 [64, 16, 2, 14336], P('dp', None, None, 'tensor')
- attended: bfloat16 [64, 14336], P('dp', 'tensor')
Inputs may be any that keep to these rules, and one draw needn't show every extreme that they name: `new_place`: each request is given a different new slot.
All inputs are finite; a program needn't handle non-finite values.
Results may differ from a plain program's by a relative error of at most 0.035.
Values may be sent and summed in bfloat16 or wider, within the bound.
No kernel may reach another device: no remote copies, remote signals or barrier semaphores. Data moves between devices by JAX's collectives and lax.ppermute only.
A program may use at most 64 MiB of HBM per device.

v0:
```python
import math

import jax
import jax.numpy as jnp
from jax import lax
from jax.sharding import PartitionSpec as P

HEADS = 112
HD = 128
REQ_DEV = 2
LMAX = 16


def alibi_slopes(count):
    closest = 2 ** int(math.floor(math.log2(count)))
    counted = jnp.arange(count, dtype=jnp.float32)
    leading = jnp.exp2(-8.0 * (counted + 1.0) / closest)
    trailing = jnp.exp2(-4.0 * (2.0 * (counted - closest) + 1.0) / closest)
    return jnp.where(counted < closest, leading, trailing)


def attend(cache, query, new_kv, slot_len, slopes):
    slots = query.shape[0]
    heads = slopes.shape[0]
    keys = cache[:, :, 0, :].reshape(slots, LMAX, heads, HD)
    values = cache[:, :, 1, :].reshape(slots, LMAX, heads, HD)
    asked = query.reshape(slots, heads, HD)
    own_key = new_kv[:, 0, :].reshape(slots, heads, HD)
    own_value = new_kv[:, 1, :].reshape(slots, heads, HD).astype(jnp.float32)
    factor = 1.0 / math.sqrt(HD)
    scores = jnp.einsum("shd,sphd->shp", asked, keys, preferred_element_type=jnp.float32) * factor
    place = jnp.arange(LMAX, dtype=jnp.int32)
    distance = (slot_len[:, None] - place[None, :]).astype(jnp.float32)
    scores = scores - slopes[None, :, None] * distance[:, None, :]
    valid = place[None, :] < slot_len[:, None]
    scores = jnp.where(valid[:, None, :], scores, -jnp.inf)
    own = jnp.einsum("shd,shd->sh", asked, own_key, preferred_element_type=jnp.float32) * factor
    top = jnp.maximum(jnp.max(scores, axis=2), own)
    raised = jnp.exp(scores - top[:, :, None])
    own_raised = jnp.exp(own - top)
    total = jnp.sum(raised, axis=2) + own_raised
    weights = (raised / total[:, :, None]).astype(jnp.bfloat16)
    own_weight = (own_raised / total).astype(jnp.bfloat16).astype(jnp.float32)
    mixed = jnp.einsum("shp,sphd->shd", weights, values, preferred_element_type=jnp.float32)
    mixed = mixed + own_weight[:, :, None] * own_value
    return mixed.reshape(slots, heads * HD).astype(jnp.bfloat16)


def per_device(stored_rows, kv_weight, lengths, new_place, query, new_kv):
    groups = lax.axis_size("dp")
    group_index = lax.axis_index("dp")
    tensor_index = lax.axis_index("tensor")
    rows_dev, width = stored_rows.shape
    block = width // groups
    requests = lengths.shape[0]
    heads_here = kv_weight.shape[2] // HD
    columns = 2 * kv_weight.shape[2]
    flat_weight = kv_weight.reshape(block, columns)
    source = (
        jnp.zeros((requests,), jnp.int32).at[new_place].set(jnp.arange(requests, dtype=jnp.int32))
    )
    place = jnp.arange(LMAX, dtype=jnp.int32)
    whole = lax.all_gather(stored_rows, "tensor", axis=0, tiled=True)
    every = lax.all_to_all(whole, "dp", split_axis=1, concat_axis=0, tiled=True)
    global_rows = jnp.arange(requests, dtype=jnp.int32)[:, None] * LMAX + place[None, :]
    live = (place[None, :] < lengths[:, None]).reshape(-1, 1)
    taken = jnp.take(every, global_rows.reshape(-1), axis=0)
    picked = taken * live.astype(jnp.bfloat16)
    summed = lax.psum_scatter(
        jnp.dot(picked, flat_weight, preferred_element_type=jnp.float32).astype(jnp.bfloat16),
        "dp",
        scatter_dimension=0,
        tiled=True,
    )
    rebuilt = summed.reshape(REQ_DEV, LMAX * columns)
    target = lax.dynamic_slice_in_dim(new_place, group_index * REQ_DEV, REQ_DEV)
    route = (target[None, :] == jnp.arange(requests, dtype=jnp.int32)[:, None]).astype(jnp.bfloat16)
    outgoing = jnp.dot(route, rebuilt, preferred_element_type=jnp.float32).astype(jnp.bfloat16)
    outgoing = outgoing.reshape(groups, REQ_DEV, LMAX * columns)
    arrived = lax.all_to_all(outgoing, "dp", split_axis=0, concat_axis=0, tiled=True)
    kv_cache = jnp.sum(arrived, axis=0, dtype=jnp.float32).astype(jnp.bfloat16)
    kv_cache = kv_cache.reshape(REQ_DEV, LMAX, 2, heads_here * HD)
    slot_len = lax.dynamic_slice_in_dim(lengths[source], group_index * REQ_DEV, REQ_DEV)
    slopes = lax.dynamic_slice_in_dim(alibi_slopes(HEADS), tensor_index * heads_here, heads_here)
    attended = attend(kv_cache, query, new_kv, slot_len, slopes)
    return (kv_cache, attended)


def solution(mesh):
    placed = (
        P(("dp", "tensor"), None),
        P("dp", None, "tensor"),
        P(),
        P(),
        P("dp", "tensor"),
        P("dp", None, "tensor"),
    )
    return jax.shard_map(
        per_device,
        mesh=mesh,
        in_specs=placed,
        out_specs=(P("dp", None, None, "tensor"), P("dp", "tensor")),
        check_vma=False,
    )
```

profile of v0, /device:TPU:1, one launch (start us, length us, event | category | flops | bytes accessed | tf_op | source)
XLA Modules:
  0.0 258.5 jit_solution(9852132583258357418)
XLA Ops:
  7.2 34.9 %all-gather = bf16[16,2,14336]{2,1,0:T(2,128)(2,1)S(1)} all-gather(bf16[1,2,14336]{2,1,0:T(2,128)(2,1)} %bitcast.47), channel_id=1, replica_groups=mesh['dp'=32,'tensor'=16] {'tensor'}, dimensions={0}, use_global_device_ids=true | all-gather | bytes 974848 | tf_op jit(solution)/shard_map/all_gather | solution.py:63
  42.0 1.1 all_to_all.17
  43.1 0.0 copy-start.1
  43.1 0.0 copy-start
  43.1 1.6 copy.11
  44.7 14.7 %all-to-all-start = ((bf16[32,32,448]{2,0,1:T(8,128)(2,1)}), bf16[32,32,448]{2,0,1:T(8,128)(2,1)S(1)}, u32[]{:S(2)}, u32[]{:S(2)}) async-start(bf16[32,32,448]{2,0,1:T(8,128)(2,1)} %copy.11), calls=%async_computation | async-start | bytes 2097152 | tf_op jit(solution)/shard_map/all_to_all | solution.py:64
  59.4 0.0 reduce-scatter.2.cloned.1.call-start
  59.4 0.1 iota_add_fusion
  59.5 0.1 add.93
  59.6 0.1 add.90
  59.7 0.0 copy-done.1
  59.7 1.4 copy.26
  61.1 0.0 copy-done
  61.1 0.1 fusion.11
  61.2 0.1 reshape.132
  61.3 15.0 %all-to-all-done = bf16[32,32,448]{2,0,1:T(8,128)(2,1)S(1)} async-done(((bf16[32,32,448]{2,0,1:T(8,128)(2,1)}), bf16[32,32,448]{2,0,1:T(8,128)(2,1)S(1)}, u32[]{:S(2)}, u32[]{:S(2)}) %all-to-all-start) | async-done | bytes 917536 | tf_op jit(solution)/shard_map/all_to_all | solution.py:64
  76.3 5.0 %gather_fusion = bf16[1024,448]{1,0:T(8,128)(2,1)} fusion(bf16[1024,448]{1,0:T(8,128)(2,1)S(1)} %bitcast.44, s32[1024]{0:T(1024)S(1)} %broadcast_clamp_fusion), kind=kCustom, calls=%fused_computation | custom fusion | bytes 1839104 | tf_op jit(solution)/shard_map/jit(_take)/gather | solution.py:67
  81.3 0.0 copy-done.2
  81.3 5.2 %convolution_convert_fusion.1 = bf16[1024,1792]{1,0:T(8,128)(2,1)} fusion(bf16[448,1792]{1,0:T(8,128)(2,1)S(1)} %bitcast.46, bf16[1024,448]{1,0:T(8,128)(2,1)} %gather_fusion, pred[1024]{0:T(1024)(128)(4,1)S(1)} %compare_and_fusion, bf16[1024]{0:T(1024)(128)(2,1)S(1)} %reshape.132), kind=kOutput, calls=%fused_computation.4 | convolution fusion | flops 1646919680 | bytes 6196224 | tf_op jit(solution)/shard_map/dot_general | solution.py:70
  86.5 0.0 reduce-scatter.2.cloned.1.call-update
  86.5 0.6 copy-done.6
  87.1 0.1 dynamic_slice.9
  87.2 94.2 %reduce-scatter.2.cloned.1.call-done = bf16[32,1792]{1,0:T(8,128)(2,1)} async-done(((bf16[1024,1792]{1,0:T(8,128)(2,1)}), bf16[32,1792]{1,0:T(8,128)(2,1)}) %reduce-scatter.2.cloned.1.call-update) | async-done | bytes 114704 | tf_op jit(solution)/shard_map/reduce_scatter | solution.py:69
  181.4 0.9 reshape.128
  182.3 2.9 %convolution_convert_fusion = bf16[64,28672]{1,0:T(8,128)(2,1)} fusion(bf16[2,28672]{1,0:T(2,128)(2,1)S(1)} %reshape.128, s32[2]{0:T(128)S(1)} %dynamic_slice.9), kind=kOutput, calls=%fused_computation.3 | convolution fusion | flops 9175168 | bytes 3784712 | tf_op jit(solution)/shard_map/dot_general | solution.py:78
  185.2 5.5 %reshape.129 = bf16[32,2,28672]{2,1,0:T(2,128)(2,1)} reshape(bf16[64,28672]{1,0:T(8,128)(2,1)} %convolution_convert_fusion) | data formatting | bytes 7340032 | tf_op jit(solution)/shard_map/reshape | solution.py:79
  190.7 7.5 %all-to-all-start.1 = ((bf16[32,2,28672]{2,1,0:T(2,128)(2,1)}), bf16[32,2,28672]{2,1,0:T(2,128)(2,1)}, u32[]{:S(2)}, u32[]{:S(2)}) async-start(bf16[32,2,28672]{2,1,0:T(2,128)(2,1)} %reshape.129), calls=%async_computation.2 | async-start | bytes 7340032 | tf_op jit(solution)/shard_map/all_to_all | solution.py:80
  198.2 0.8 scatter_custom_fusion
  199.0 0.8 gather_fusion.1
  199.8 0.1 dynamic_slice.10
  199.9 0.1 fusion.14
  200.0 0.1 copy.19
  200.2 0.1 dynamic_slice.11
  200.3 0.1 iota_compare_fusion.3
  200.4 0.1 subtract_convert_fusion
  200.4 43.7 %all-to-all-done.1 = bf16[32,2,28672]{2,1,0:T(2,128)(2,1)} async-done(((bf16[32,2,28672]{2,1,0:T(2,128)(2,1)}), bf16[32,2,28672]{2,1,0:T(2,128)(2,1)}, u32[]{:S(2)}, u32[]{:S(2)}) %all-to-all-start.1) | async-done | bytes 3670048 | tf_op jit(solution)/shard_map/all_to_all | solution.py:80
  244.2 5.4 %reduce_sum.21 = bf16[2,28672]{1,0:T(2,128)(2,1)S(1)} reduce(bf16[32,2,28672]{2,1,0:T(2,128)(2,1)} %all-to-all-done.1, bf16[]{:T(256)} %constant.21.clone.1), dimensions={0}, to_apply=%region_1.2 | reduce | flops 1777664 | bytes 3784706 | tf_op jit(solution)/shard_map/reduce_sum | solution.py:81
  249.5 0.1 reshape.130
  249.6 0.0 copy-start.3
  249.7 0.5 slice_reduce_fusion.1
  250.2 0.1 fusion.8
  250.3 0.2 fusion.32
  250.5 0.2 fusion.19
  250.7 0.1 fusion.20
  250.8 0.1 copy.12
  250.9 0.1 fusion.5
  251.0 0.1 fusion.18
  251.1 0.6 copy.44
  (24 shorter events, 0.2 us)
Async XLA Ops:
  43.1 16.6 %copy-start.1 = (bf16[448,2,896]{2,1,0:T(2,128)(2,1)S(1)}, bf16[448,2,896]{2,1,0:T(2,128)(2,1)}, u32[]{:S(2)}) copy-start(bf16[448,2,896]{2,1,0:T(2,128)(2,1)} %param.7) | copy-start | bytes 4816900
  43.1 18.0 %copy-start = (s32[64]{0:T(128)S(1)}, s32[64]{0:T(128)}, u32[]{:S(2)}) copy-start(s32[64]{0:T(128)} %param.8) | copy-start | bytes 772
  44.7 31.6 %all-to-all-start = ((bf16[32,32,448]{2,0,1:T(8,128)(2,1)}), bf16[32,32,448]{2,0,1:T(8,128)(2,1)S(1)}, u32[]{:S(2)}, u32[]{:S(2)}) async-start(bf16[32,32,448]{2,0,1:T(8,128)(2,1)} %copy.11), calls=%async_computation | async-start | bytes 2097152 | tf_op jit(solution)/shard_map/all_to_all | solution.py:64
  59.4 122.0 %reduce-scatter.2.cloned.1.call-start = ((), (), s32[]{:S(2)}) async-start(), calls=%async_computation.3 | async-start | bytes 3784704 | tf_op jit(solution)/shard_map/reduce_scatter | solution.py:69
  76.3 5.0 %copy-start.2 = (bf16[56,8,2,896]{3,1,2,0:T(8,128)(2,1)S(1)}, bf16[56,8,2,896]{3,1,2,0:T(8,128)(2,1)}, u32[]{:S(2)}) copy-start(bf16[56,8,2,896]{3,1,2,0:T(8,128)(2,1)} %copy.26) | copy-start | bytes 4816900
  86.5 0.7 copy-start.6
  190.7 7.5 %copy-start.5 = (bf16[2,896]{1,0:T(2,128)(2,1)S(1)}, bf16[2,896]{1,0:T(2,128)(2,1)}, u32[]{:S(2)}) copy-start(bf16[2,896]{1,0:T(2,128)(2,1)} %param.10) | copy-start | bytes 10756
  190.7 9.2 %copy-start.4 = (bf16[2,2,896]{2,1,0:T(2,128)(2,1)S(1)}, bf16[2,2,896]{2,1,0:T(2,128)(2,1)}, u32[]{:S(2)}) copy-start(bf16[2,2,896]{2,1,0:T(2,128)(2,1)} %param.11) | copy-start | bytes 21508
  190.7 53.5 %all-to-all-start.1 = ((bf16[32,2,28672]{2,1,0:T(2,128)(2,1)}), bf16[32,2,28672]{2,1,0:T(2,128)(2,1)}, u32[]{:S(2)}, u32[]{:S(2)}) async-start(bf16[32,2,28672]{2,1,0:T(2,128)(2,1)} %reshape.129), calls=%async_computation.2 | async-start | bytes 7340032 | tf_op jit(solution)/shard_map/all_to_all | solution.py:80
  249.6 2.0 copy-start.3
Sparse Core Ops, SparseCore 0:
  86.6 94.7 reduce-scatter.1
where the time goes:
time: 259 us
  waiting for transfers between devices  153 us (59%)
  blocking collectives  34.9 us (13%)
  starting transfers between devices  22.2 us (9%)
  local copies, waits for them, and re-layouts  19.6 us (8%)
  between operations  14.2 us (5%)
  matrix products  8.33 us (3%)
  other arithmetic  6.36 us (2%)
    reduce_scatter x1, waiting for transfers between devices, per_device(): lax.psum_scatter(jnp.dot(picked, flat_weight, preferred_element_type=jnp....  94.2 us
    all_to_all x1, waiting for transfers between devices, per_device(): lax.all_to_all(outgoing, 'dp', split_axis=0, concat_axis=0, tiled=True)  43.7 us
    all_gather x1, blocking collectives, per_device(): whole = lax.all_gather(stored_rows, 'tensor', axis=0, tiled=True)  34.9 us
    all_to_all x1, waiting for transfers between devices, per_device(): every = lax.all_to_all(whole, 'dp', split_axis=1, concat_axis=0, tiled=True)  15 us
    all_to_all x1, starting transfers between devices, per_device(): every = lax.all_to_all(whole, 'dp', split_axis=1, concat_axis=0, tiled=True)  14.7 us
    all_to_all x1, starting transfers between devices, per_device(): lax.all_to_all(outgoing, 'dp', split_axis=0, concat_axis=0, tiled=True)  7.45 us
    reshape x1, local copies, waits for them, and re-layouts, per_device(): outgoing = outgoing.reshape(groups, REQ_DEV, LMAX * columns)  5.45 us
    reduce_sum x1, other arithmetic, per_device(): kv_cache = jnp.sum(arrived, axis=0, dtype=jnp.float32).astype(jnp.bfloat16)  5.38 us
  transfers between devices with their start and end apart: 3, of which 3 were waited for; matrix products, arithmetic and copies ran while one was open for 2% of the time, Pallas kernels for 0%

commit v1 on v0

--- a/solution.py
+++ b/solution.py
@@ -9,6 +9,7 @@
 HD = 128
 REQ_DEV = 2
 LMAX = 16
+PAIR = 2
 
 
 def alibi_slopes(count):
@@ -48,41 +49,50 @@
 
 def per_device(stored_rows, kv_weight, lengths, new_place, query, new_kv):
     groups = lax.axis_size("dp")
+    planes = lax.axis_size("tensor")
     group_index = lax.axis_index("dp")
     tensor_index = lax.axis_index("tensor")
-    rows_dev, width = stored_rows.shape
+    core = lax.rem(group_index, PAIR)
+    chips = groups // PAIR
+    width = stored_rows.shape[1]
     block = width // groups
     requests = lengths.shape[0]
     heads_here = kv_weight.shape[2] // HD
     columns = 2 * kv_weight.shape[2]
+
+    by_chip = stored_rows.reshape(PAIR, chips, PAIR, block)
+    first = jnp.concatenate([by_chip[0, :, 0], by_chip[0, :, 1]], axis=1)
+    second = jnp.concatenate([by_chip[1, :, 1], by_chip[1, :, 0]], axis=1)
+    sent = jnp.stack([first, second], axis=1).reshape(groups, PAIR * block)
+    mine = lax.all_to_all(sent, "dp", split_axis=0, concat_axis=0, tiled=True)
+
     flat_weight = kv_weight.reshape(block, columns)
-    source = (
-        jnp.zeros((requests,), jnp.int32).at[new_place].set(jnp.arange(requests, dtype=jnp.int32))
-    )
-    place = jnp.arange(LMAX, dtype=jnp.int32)
-    whole = lax.all_gather(stored_rows, "tensor", axis=0, tiled=True)
-    every = lax.all_to_all(whole, "dp", split_axis=1, concat_axis=0, tiled=True)
-    global_rows = jnp.arange(requests, dtype=jnp.int32)[:, None] * LMAX + place[None, :]
-    live = (place[None, :] < lengths[:, None]).reshape(-1, 1)
-    taken = jnp.take(every, global_rows.reshape(-1), axis=0)
-    picked = taken * live.astype(jnp.bfloat16)
-    summed = lax.psum_scatter(
-        jnp.dot(picked, flat_weight, preferred_element_type=jnp.float32).astype(jnp.bfloat16),
-        "dp",
-        scatter_dimension=0,
-        tiled=True,
-    )
-    rebuilt = summed.reshape(REQ_DEV, LMAX * columns)
-    target = lax.dynamic_slice_in_dim(new_place, group_index * REQ_DEV, REQ_DEV)
-    route = (target[None, :] == jnp.arange(requests, dtype=jnp.int32)[:, None]).astype(jnp.bfloat16)
-    outgoing = jnp.dot(route, rebuilt, preferred_element_type=jnp.float32).astype(jnp.bfloat16)
-    outgoing = outgoing.reshape(groups, REQ_DEV, LMAX * columns)
-    arrived = lax.all_to_all(outgoing, "dp", split_axis=0, concat_axis=0, tiled=True)
-    kv_cache = jnp.sum(arrived, axis=0, dtype=jnp.float32).astype(jnp.bfloat16)
-    kv_cache = kv_cache.reshape(REQ_DEV, LMAX, 2, heads_here * HD)
-    slot_len = lax.dynamic_slice_in_dim(lengths[source], group_index * REQ_DEV, REQ_DEV)
+    other_weight = lax.ppermute(flat_weight, "dp", [(i, i ^ 1) for i in range(groups)])
+    weight = jnp.concatenate([flat_weight, other_weight], axis=0)
+
+    every = lax.all_gather(mine, "tensor", axis=0, tiled=True)
+
+    slots = jnp.arange(requests, dtype=jnp.int32)
+    at_slot = new_place[None, :] == slots[:, None]
+    source = jnp.sum(jnp.where(at_slot, slots[None, :], 0), axis=1)
+    slot_len = jnp.sum(jnp.where(at_slot, lengths[None, :], 0), axis=1)
+    half = LMAX // PAIR
+    step = jnp.arange(half, dtype=jnp.int32)
+    plane = (source % 2)[:, None] * half + step[None, :]
+    row = plane * groups + (source // 2)[:, None]
+    live = (PAIR * step + core)[None, :] < slot_len[:, None]
+    row = jnp.where(live, row, -1).reshape(-1)
+    route = (row[:, None] == jnp.arange(planes * groups, dtype=jnp.int32)[None, :]).astype(jnp.bfloat16)
+    picked = jnp.dot(route, every, preferred_element_type=jnp.float32).astype(jnp.bfloat16)
+    partial = jnp.dot(picked, weight, preferred_element_type=jnp.float32).astype(jnp.bfloat16)
+
+    arrived = lax.all_to_all(partial, "dp", split_axis=0, concat_axis=0, tiled=True)
+    arrived = arrived.reshape(chips, PAIR, REQ_DEV, half, columns)
+    summed = jnp.sum(arrived, axis=0, dtype=jnp.float32).astype(jnp.bfloat16)
+    kv_cache = summed.transpose(1, 2, 0, 3).reshape(REQ_DEV, LMAX, 2, heads_here * HD)
+    here_len = lax.dynamic_slice_in_dim(slot_len, group_index * REQ_DEV, REQ_DEV)
     slopes = lax.dynamic_slice_in_dim(alibi_slopes(HEADS), tensor_index * heads_here, heads_here)
-    attended = attend(kv_cache, query, new_kv, slot_len, slopes)
+    attended = attend(kv_cache, query, new_kv, here_len, slopes)
     return (kv_cache, attended)
 
 

time: 259 us -> 102 us (0.39)
  waiting for transfers between devices: 153 us -> 31.8 us
  local copies, waits for them, and re-layouts: 19.6 us -> 5.28 us
  between operations: 14.2 us -> 0.86 us
  other arithmetic: 6.36 us -> 2.42 us
  matrix products: 8.33 us -> 5.71 us
    reduce_scatter x1 -> x0, waiting for transfers between devices: 94.2 us -> none  [per_device(): lax.psum_scatter(jnp.dot(picked, flat_weight, preferred_element_type=jnp....]
    all_to_all x2, waiting for transfers between devices: 58.7 us -> 31.8 us  [the longest x1 24.8 us: per_device(): lax.all_to_all(partial, 'dp', split_axis=0, concat_axis=0, tiled=True)]
    ppermute x0 -> x1, starting transfers between devices: none -> 8.79 us  [per_device(): lax.ppermute(flat_weight, 'dp', [(i, i ^ 1) for i in range(groups)])]
    all_to_all x2, starting transfers between devices: 22.1 us -> 14.6 us  [the longest x1 11 us: per_device(): lax.all_to_all(partial, 'dp', split_axis=0, concat_axis=0, tiled=True)]
    reshape x3 -> x2, local copies, waits for them, and re-layouts: 6.48 us -> 0.21 us  [the longest x1 0.13 us: per_device(): by_chip = stored_rows.reshape(PAIR, chips, PAIR, block)]
    gather x2 -> x0, local copies, waits for them, and re-layouts: 5.81 us -> none  [the longest x1 5.03 us: per_device(): taken = jnp.take(every, global_rows.reshape(-1), axis=0)]
    reduce_sum x1 -> x2, other arithmetic: 5.38 us -> 0.38 us  [the longest x1 0.27 us: per_device(): summed = jnp.sum(arrived, axis=0, dtype=jnp.float32).astype(jnp.bfloat16)]
    dot_general x2 -> x1, matrix products: 8.07 us -> 5.46 us  [per_device(): jnp.dot(picked, weight, preferred_element_type=jnp.float32)]
  transfers between devices with their start and end apart: 3 -> 3, of which waited for: 3 -> 2; matrix products, arithmetic and copies ran while one was open for 2% -> 4% of each run, Pallas kernels for 0% -> 0%
where the time goes in v1:
time: 102 us
  blocking collectives  32.5 us (32%)
  waiting for transfers between devices  31.8 us (31%)
  starting transfers between devices  23.4 us (23%)
  matrix products  5.71 us (6%)
  local copies, waits for them, and re-layouts  5.28 us (5%)
  other arithmetic  2.42 us (2%)
    all_gather x1, blocking collectives, per_device(): every = lax.all_gather(mine, 'tensor', axis=0, tiled=True)  32.5 us
    all_to_all x1, waiting for transfers between devices, per_device(): lax.all_to_all(partial, 'dp', split_axis=0, concat_axis=0, tiled=True)  24.8 us
    all_to_all x1, starting transfers between devices, per_device(): lax.all_to_all(partial, 'dp', split_axis=0, concat_axis=0, tiled=True)  11 us
    ppermute x1, starting transfers between devices, per_device(): lax.ppermute(flat_weight, 'dp', [(i, i ^ 1) for i in range(groups)])  8.79 us
    all_to_all x1, waiting for transfers between devices, per_device(): mine = lax.all_to_all(sent, 'dp', split_axis=0, concat_axis=0, tiled=True)  7 us
    dot_general x1, matrix products, per_device(): jnp.dot(picked, weight, preferred_element_type=jnp.float32)  5.46 us
    all_to_all x1, starting transfers between devices, per_device(): mine = lax.all_to_all(sent, 'dp', split_axis=0, concat_axis=0, tiled=True)  3.64 us
    unnamed x18, local copies, waits for them, and re-layouts  3.21 us
  transfers between devices with their start and end apart: 3, of which 2 were waited for; matrix products, arithmetic and copies ran while one was open for 4% of the time, Pallas kernels for 0%

profile of v1, /device:TPU:1, one launch (start us, length us, event | category | flops | bytes accessed | tf_op | source)
XLA Modules:
  0.0 101.9 jit_solution(6015660067404228384)
XLA Ops:
  0.6 0.0 copy-start.1
  0.6 0.0 copy-start.4
  0.7 0.0 copy-start.5
  0.7 1.7 %copy.48 = bf16[56,8,2,896]{3,1,2,0:T(8,128)(2,1)S(1)} copy(bf16[56,8,2,896]{3,2,1,0:T(2,128)(2,1)} %bitcast.58) | data formatting | bytes 3211264
  2.3 8.8 %collective-permute-start = (bf16[448,1792]{1,0:T(8,128)(2,1)S(1)}, bf16[448,1792]{1,0:T(8,128)(2,1)}, u32[]{:S(2)}, u32[]{:S(2)}) collective-permute-start(bf16[448,1792]{1,0:T(8,128)(2,1)S(1)} %bitcast.59), channel_id=1, source_target_pairs={{0,16},{16,0},{32,48},{48,32},{64,80},{80,64},{96,112},{112,96},{1... | collective-permute-start | bytes 4816904 | tf_op jit(solution)/shard_map/ppermute | solution.py:70
  11.1 0.0 copy-done.1
  11.1 0.1 reshape.149
  11.3 0.1 fusion.37
  11.4 0.1 maximum_bitcast_fusion
  11.5 0.1 maximum_bitcast_fusion.1
  11.7 0.5 broadcast.176
  12.2 1.0 reduce.11
  13.2 0.8 reshape.168
  13.9 3.6 %all-to-all-start = ((bf16[32,2,448]{2,1,0:T(2,128)(2,1)}), bf16[32,2,448]{2,1,0:T(2,128)(2,1)S(1)}, u32[]{:S(2)}, u32[]{:S(2)}) async-start(bf16[32,2,448]{2,1,0:T(2,128)(2,1)} %reshape.168), calls=%async_computation | async-start | bytes 131072 | tf_op jit(solution)/shard_map/all_to_all | solution.py:67
  17.6 0.0 copy-done.4
  17.6 0.0 copy-done.5
  17.6 0.1 select_reduce_fusion.1
  17.7 0.1 add_select_fusion
  17.8 0.1 select_n.57
  17.9 7.0 %all-to-all-done = bf16[32,2,448]{2,1,0:T(2,128)(2,1)S(1)} async-done(((bf16[32,2,448]{2,1,0:T(2,128)(2,1)}), bf16[32,2,448]{2,1,0:T(2,128)(2,1)S(1)}, u32[]{:S(2)}, u32[]{:S(2)}) %all-to-all-start) | async-done | bytes 57376 | tf_op jit(solution)/shard_map/all_to_all | solution.py:67
  24.9 0.1 reshape.169
  25.1 32.5 %all-gather = bf16[512,1,896]{2,0,1:T(8,128)(2,1)S(1)} all-gather(bf16[32,1,896]{2,0,1:T(8,128)(2,1)S(1)} %copy.28), channel_id=2, replica_groups=mesh['dp'=32,'tensor'=16] {'tensor'}, dimensions={0}, use_global_device_ids=true | all-gather | bytes 974848 | tf_op jit(solution)/shard_map/all_gather | solution.py:73
  57.5 0.0 collective-permute-done
  57.6 5.5 %fusion.4 = bf16[512,1792]{1,0:T(8,128)(2,1)} fusion(bf16[448,1792]{1,0:T(8,128)(2,1)} %collective-permute-done, bf16[448,1792]{1,0:T(8,128)(2,1)S(1)} %bitcast.60, bf16[512,1,896]{2,0,1:T(8,128)(2,1)S(1)} %all-gather, s32[512]{0:T(512)S(1)} %select_n.57), kind=kOutput, calls=%fused_computation.4 | convolution fusion | flops 2121990144 | bytes 5965824 | tf_op jit(solution)/shard_map/dot_general | solution.py:87
  63.0 11.0 %all-to-all-start.1 = ((bf16[32,16,1792]{2,1,0:T(8,128)(2,1)}), bf16[32,16,1792]{2,1,0:T(8,128)(2,1)S(1)}, u32[]{:S(2)}, u32[]{:S(2)}) async-start(bf16[32,16,1792]{2,1,0:T(8,128)(2,1)} %bitcast.57), calls=%async_computation.1 | async-start | bytes 3670016 | tf_op jit(solution)/shard_map/all_to_all | solution.py:89
  74.0 0.0 copy-done.3
  74.0 0.1 dynamic_slice.6
  74.1 0.0 copy-done.2
  74.2 0.1 fusion.18
  74.3 0.1 copy.37
  74.4 0.1 dynamic_slice.7
  74.5 0.1 iota_compare_fusion.5
  74.6 0.1 subtract_convert_fusion
  74.6 24.8 %all-to-all-done.1 = bf16[32,16,1792]{2,1,0:T(8,128)(2,1)S(1)} async-done(((bf16[32,16,1792]{2,1,0:T(8,128)(2,1)}), bf16[32,16,1792]{2,1,0:T(8,128)(2,1)S(1)}, u32[]{:S(2)}, u32[]{:S(2)}) %all-to-all-start.1) | async-done | bytes 1835040 | tf_op jit(solution)/shard_map/all_to_all | solution.py:89
  99.5 0.3 reduce_sum.41
  99.7 0.1 copy.29
  99.8 0.1 reshape.152
  99.9 0.0 copy-start
  99.9 0.5 slice_reduce_fusion.1
  100.5 0.1 fusion.14
  100.6 0.2 fusion.35
  100.8 0.2 fusion.23
  100.9 0.1 fusion.24
  101.0 0.1 copy.30
  101.1 0.1 fusion.11
  101.3 0.1 fusion.22
  101.3 0.6 copy.70
  101.9 0.0 copy-done
  (19 shorter events, 0.3 us)
Async XLA Ops:
  0.6 10.5 %copy-start.1 = (bf16[2,14336]{1,0:T(2,128)(2,1)S(1)}, bf16[2,14336]{1,0:T(2,128)(2,1)}, u32[]{:S(2)}) copy-start(bf16[2,14336]{1,0:T(2,128)(2,1)} %param.6) | copy-start | bytes 172036
  0.6 17.0 %copy-start.4 = (s32[64]{0:T(128)S(1)}, s32[64]{0:T(128)}, u32[]{:S(2)}) copy-start(s32[64]{0:T(128)} %param.8) | copy-start | bytes 772
  0.7 17.0 %copy-start.5 = (s32[64]{0:T(128)S(1)}, s32[64]{0:T(128)}, u32[]{:S(2)}) copy-start(s32[64]{0:T(128)} %param.9) | copy-start | bytes 772
  2.3 55.2 %collective-permute-start = (bf16[448,1792]{1,0:T(8,128)(2,1)S(1)}, bf16[448,1792]{1,0:T(8,128)(2,1)}, u32[]{:S(2)}, u32[]{:S(2)}) collective-permute-start(bf16[448,1792]{1,0:T(8,128)(2,1)S(1)} %bitcast.59), channel_id=1, source_target_pairs={{0,16},{16,0},{32,48},{48,32},{64,80},{80,64},{96,112},{112,96},{1... | collective-permute-start | bytes 4816904 | tf_op jit(solution)/shard_map/ppermute | solution.py:70
  13.9 11.0 %all-to-all-start = ((bf16[32,2,448]{2,1,0:T(2,128)(2,1)}), bf16[32,2,448]{2,1,0:T(2,128)(2,1)S(1)}, u32[]{:S(2)}, u32[]{:S(2)}) async-start(bf16[32,2,448]{2,1,0:T(2,128)(2,1)} %reshape.168), calls=%async_computation | async-start | bytes 131072 | tf_op jit(solution)/shard_map/all_to_all | solution.py:67
  63.0 11.0 %copy-start.3 = (bf16[2,896]{1,0:T(2,128)(2,1)S(1)}, bf16[2,896]{1,0:T(2,128)(2,1)}, u32[]{:S(2)}) copy-start(bf16[2,896]{1,0:T(2,128)(2,1)} %param.10) | copy-start | bytes 10756
  63.0 11.1 %copy-start.2 = (bf16[2,2,896]{2,1,0:T(2,128)(2,1)S(1)}, bf16[2,2,896]{2,1,0:T(2,128)(2,1)}, u32[]{:S(2)}) copy-start(bf16[2,2,896]{2,1,0:T(2,128)(2,1)} %param.11) | copy-start | bytes 21508
  63.0 36.5 %all-to-all-start.1 = ((bf16[32,16,1792]{2,1,0:T(8,128)(2,1)}), bf16[32,16,1792]{2,1,0:T(8,128)(2,1)S(1)}, u32[]{:S(2)}, u32[]{:S(2)}) async-start(bf16[32,16,1792]{2,1,0:T(8,128)(2,1)} %bitcast.57), calls=%async_computation.1 | async-start | bytes 3670016 | tf_op jit(solution)/shard_map/all_to_all | solution.py:89
  99.9 2.0 %copy-start = (bf16[2,16,2,896]{3,2,1,0:T(2,128)(2,1)}, bf16[2,16,2,896]{3,2,1,0:T(2,128)(2,1)S(1)}, u32[]{:S(2)}) copy-start(bf16[2,16,2,896]{3,2,1,0:T(2,128)(2,1)S(1)} %reshape.152) | copy-start | bytes 344068

commit v2 on v1

--- a/solution.py
+++ b/solution.py
@@ -3,6 +3,8 @@
 import jax
 import jax.numpy as jnp
 from jax import lax
+from jax.experimental import pallas as pl
+from jax.experimental.pallas import tpu as pltpu
 from jax.sharding import PartitionSpec as P
 
 HEADS = 112
@@ -47,49 +49,109 @@
     return mixed.reshape(slots, heads * HD).astype(jnp.bfloat16)
 
 
+def product_kernel(where, x_own, x_other, w_own, w_pair, w_next, w_cross, route, out, xs, ws, rs, sems):
+    core, half = where[0], where[1]
+    block = w_own.shape[0]
+
+    def rows(at):
+        return pl.ds(pl.multiple_of(at * block, 16), block)
+
+    moves = [
+        (w_own, ws.at[half, rows(core)]),
+        (w_pair, ws.at[half, rows(1 - core)]),
+        (w_next, ws.at[1 - half, rows(core)]),
+        (w_cross, ws.at[1 - half, rows(1 - core)]),
+        (x_own, xs.at[core]),
+        (x_other, xs.at[1 - core]),
+        (route, rs),
+    ]
+    copies = [pltpu.make_async_copy(a, b, sems.at[i]) for i, (a, b) in enumerate(moves)]
+    for copy in copies:
+        copy.start()
+    for copy in copies:
+        copy.wait()
+    columns = out.shape[1]
+    for start in range(0, columns, 256):
+        part = slice(start, min(start + 256, columns))
+        total = jnp.dot(xs[0], ws[0, :, part], preferred_element_type=jnp.float32)
+        total += jnp.dot(xs[1], ws[1, :, part], preferred_element_type=jnp.float32)
+        placed = jnp.dot(rs[...], total.astype(jnp.bfloat16), preferred_element_type=jnp.float32)
+        out[:, part] = placed.astype(jnp.bfloat16)
+
+
+def product(where, x_own, x_other, w_own, w_pair, w_next, w_cross, route):
+    rows, depth = x_own.shape
+    block, columns = w_own.shape
+    anywhere = pl.BlockSpec(memory_space=pl.ANY)
+    return pl.pallas_call(
+        product_kernel,
+        out_shape=jax.ShapeDtypeStruct((rows, columns), jnp.bfloat16),
+        in_specs=[pl.BlockSpec(memory_space=pltpu.SMEM)] + [anywhere] * 7,
+        out_specs=pl.BlockSpec(memory_space=pltpu.VMEM),
+        scratch_shapes=[
+            pltpu.VMEM((2, rows, depth), jnp.bfloat16),
+            pltpu.VMEM((2, PAIR * block, columns), jnp.bfloat16),
+            pltpu.VMEM(route.shape, jnp.bfloat16),
+            pltpu.SemaphoreType.DMA((7,)),
+        ],
+        compiler_params=pltpu.CompilerParams(vmem_limit_bytes=24 * 1024 * 1024),
+        cost_estimate=pl.CostEstimate(
+            flops=2 * rows * columns * (2 * depth + rows),
+            bytes_accessed=2 * (2 * rows * depth + 4 * block * columns + rows * rows + rows * columns),
+            transcendentals=0,
+        ),
+    )(where, x_own, x_other, w_own, w_pair, w_next, w_cross, route)
+
+
 def per_device(stored_rows, kv_weight, lengths, new_place, query, new_kv):
     groups = lax.axis_size("dp")
     planes = lax.axis_size("tensor")
     group_index = lax.axis_index("dp")
     tensor_index = lax.axis_index("tensor")
-    core = lax.rem(group_index, PAIR)
-    chips = groups // PAIR
+    core = jnp.bitwise_and(group_index, 1)
+    half = jnp.bitwise_and(jnp.right_shift(group_index, 3), 1)
     width = stored_rows.shape[1]
     block = width // groups
     requests = lengths.shape[0]
-    heads_here = kv_weight.shape[2] // HD
-    columns = 2 * kv_weight.shape[2]
+    columns = kv_weight.shape[2]
+    heads_here = columns // HD
 
-    by_chip = stored_rows.reshape(PAIR, chips, PAIR, block)
-    first = jnp.concatenate([by_chip[0, :, 0], by_chip[0, :, 1]], axis=1)
-    second = jnp.concatenate([by_chip[1, :, 1], by_chip[1, :, 0]], axis=1)
-    sent = jnp.stack([first, second], axis=1).reshape(groups, PAIR * block)
-    mine = lax.all_to_all(sent, "dp", split_axis=0, concat_axis=0, tiled=True)
+    sent = stored_rows.reshape(2, 2, 2, 4, 2, block).transpose(1, 0, 3, 2, 4, 5)
+    mine = lax.all_to_all(sent.reshape(groups, 2, block), "dp", split_axis=0, concat_axis=0, tiled=True)
+    mine = mine.reshape(groups, 2 * block)
 
-    flat_weight = kv_weight.reshape(block, columns)
-    other_weight = lax.ppermute(flat_weight, "dp", [(i, i ^ 1) for i in range(groups)])
-    weight = jnp.concatenate([flat_weight, other_weight], axis=0)
+    def swapped(array, bit):
+        return lax.ppermute(array, "dp", [(i, i ^ bit) for i in range(groups)])
 
-    every = lax.all_gather(mine, "tensor", axis=0, tiled=True)
+    w_own = lax.dynamic_index_in_dim(kv_weight, core, axis=1, keepdims=False)
+    w_away = lax.dynamic_index_in_dim(kv_weight, 1 - core, axis=1, keepdims=False)
+    w_next = swapped(w_own, 8)
+    w_cross = swapped(w_away, 9)
+    w_pair = swapped(w_away, 1)
 
     slots = jnp.arange(requests, dtype=jnp.int32)
     at_slot = new_place[None, :] == slots[:, None]
     source = jnp.sum(jnp.where(at_slot, slots[None, :], 0), axis=1)
     slot_len = jnp.sum(jnp.where(at_slot, lengths[None, :], 0), axis=1)
-    half = LMAX // PAIR
-    step = jnp.arange(half, dtype=jnp.int32)
-    plane = (source % 2)[:, None] * half + step[None, :]
+    steps = LMAX // 2
+    step = jnp.arange(steps, dtype=jnp.int32)
+    plane = (source % 2)[:, None] * steps + step[None, :]
     row = plane * groups + (source // 2)[:, None]
-    live = (PAIR * step + core)[None, :] < slot_len[:, None]
+    live = (2 * step + half)[None, :] < slot_len[:, None]
     row = jnp.where(live, row, -1).reshape(-1)
     route = (row[:, None] == jnp.arange(planes * groups, dtype=jnp.int32)[None, :]).astype(jnp.bfloat16)
-    picked = jnp.dot(route, every, preferred_element_type=jnp.float32).astype(jnp.bfloat16)
-    partial = jnp.dot(picked, weight, preferred_element_type=jnp.float32).astype(jnp.bfloat16)
 
-    arrived = lax.all_to_all(partial, "dp", split_axis=0, concat_axis=0, tiled=True)
-    arrived = arrived.reshape(chips, PAIR, REQ_DEV, half, columns)
-    summed = jnp.sum(arrived, axis=0, dtype=jnp.float32).astype(jnp.bfloat16)
-    kv_cache = summed.transpose(1, 2, 0, 3).reshape(REQ_DEV, LMAX, 2, heads_here * HD)
+    x_own = lax.all_gather(mine, "tensor", axis=0, tiled=True)
+    x_other = swapped(x_own, 1)
+    where = jnp.stack([core, half]).astype(jnp.int32)
+    partial = product(where, x_own, x_other, w_own, w_pair, w_next, w_cross, route)
+
+    arrived = lax.all_to_all(
+        partial.reshape(groups, REQ_DEV * steps, columns), "dp", split_axis=0, concat_axis=0, tiled=True
+    )
+    arrived = arrived.reshape(2, 2, 4, 2, REQ_DEV, steps, columns)
+    summed = jnp.sum(arrived, axis=(0, 2), dtype=jnp.float32).astype(jnp.bfloat16)
+    kv_cache = summed.transpose(2, 3, 0, 1, 4).reshape(REQ_DEV, LMAX, 2, columns)
     here_len = lax.dynamic_slice_in_dim(slot_len, group_index * REQ_DEV, REQ_DEV)
     slopes = lax.dynamic_slice_in_dim(alibi_slopes(HEADS), tensor_index * heads_here, heads_here)
     attended = attend(kv_cache, query, new_kv, here_len, slopes)

time: 102 us -> 104 us (1.020)
  waiting for transfers between devices: 31.8 us -> 16.3 us
  starting transfers between devices: 23.4 us -> 34.7 us
  Pallas kernels: 0 us -> 8.5 us
  matrix products: 5.71 us -> 0.26 us
  local copies, waits for them, and re-layouts: 5.28 us -> 9.85 us
  other arithmetic: 2.42 us -> 1.37 us
    all_to_all x2, waiting for transfers between devices: 31.8 us -> 14.9 us  [the longest x1 14.9 us: per_device(): lax.all_to_all(partial.reshape(groups, REQ_DEV * steps, columns), 'dp', s...]
    pallas_call x0 -> x1, Pallas kernels: none -> 8.5 us  [product(): pl.pallas_call(product_kernel, out_shape=jax.ShapeDtypeStruct((rows, colu...]
    ppermute x1 -> x4, starting transfers between devices: 8.79 us -> 16.8 us  [swapped(): return lax.ppermute(array, 'dp', [(i, i ^ bit) for i in range(groups)])]
    dot_general x1 -> x0, matrix products: 5.46 us -> none  [per_device(): jnp.dot(picked, weight, preferred_element_type=jnp.float32)]
    dynamic_slice x0 -> x1, local copies, waits for them, and re-layouts: none -> 5.26 us  [per_device(): lax.dynamic_index_in_dim(kv_weight, 1 - core, axis=1, keepdims=False)]
    all_to_all x2, starting transfers between devices: 14.6 us -> 17.9 us  [the longest x1 10.4 us: per_device(): lax.all_to_all(sent.reshape(groups, 2, block), 'dp', split_axis=0, concat...]
    unnamed x18 -> x13, local copies, waits for them, and re-layouts: 3.21 us -> 1.71 us
    ppermute x1 -> x4, waiting for transfers between devices: 0.01 us -> 1.34 us  [swapped(): return lax.ppermute(array, 'dp', [(i, i ^ bit) for i in range(groups)])]
  transfers between devices with their start and end apart: 3 -> 6, of which waited for: 2 -> 2; matrix products, arithmetic and copies ran while one was open for 4% -> 7% of each run, Pallas kernels for 0% -> 0%
where the time goes in v2:
time: 104 us
  starting transfers between devices  34.7 us (33%)
  blocking collectives  32.1 us (31%)
  waiting for transfers between devices  16.3 us (16%)
  local copies, waits for them, and re-layouts  9.85 us (9%)
  Pallas kernels  8.5 us (8%)
  other arithmetic  1.37 us (1%)
    all_gather x1, blocking collectives, per_device(): x_own = lax.all_gather(mine, 'tensor', axis=0, tiled=True)  32.1 us
    ppermute x4, starting transfers between devices, swapped(): return lax.ppermute(array, 'dp', [(i, i ^ bit) for i in range(groups)])  16.8 us
    all_to_all x1, waiting for transfers between devices, per_device(): lax.all_to_all(partial.reshape(groups, REQ_DEV * steps, columns), 'dp', s...  14.9 us
    all_to_all x1, starting transfers between devices, per_device(): lax.all_to_all(sent.reshape(groups, 2, block), 'dp', split_axis=0, concat...  10.4 us
    pallas_call x1, Pallas kernels, product(): pl.pallas_call(product_kernel, out_shape=jax.ShapeDtypeStruct((rows, colu...  8.5 us
    all_to_all x1, starting transfers between devices, per_device(): lax.all_to_all(partial.reshape(groups, REQ_DEV * steps, columns), 'dp', s...  7.53 us
    dynamic_slice x1, local copies, waits for them, and re-layouts, per_device(): lax.dynamic_index_in_dim(kv_weight, 1 - core, axis=1, keepdims=False)  5.26 us
  transfers between devices with their start and end apart: 6, of which 2 were waited for; matrix products, arithmetic and copies ran while one was open for 7% of the time, Pallas kernels for 0%

profile of v2, /device:TPU:1, one launch (start us, length us, event | category | flops | bytes accessed | tf_op | source)
XLA Modules:
  0.0 103.9 jit_solution(13359622772428850887)
XLA Ops:
  0.6 0.9 reshape.148
  1.6 0.7 copy.19
  2.3 10.4 %all-to-all-start = ((bf16[32,2,448]{2,1,0:T(2,128)(2,1)}), bf16[32,2,448]{2,1,0:T(2,128)(2,1)S(1)}, u32[]{:S(2)}, u32[]{:S(2)}) async-start(bf16[32,2,448]{2,1,0:T(2,128)(2,1)} %bitcast.3), calls=%async_computation | async-start | bytes 131072 | tf_op jit(solution)/shard_map/all_to_all | solution.py:120
  12.7 5.3 %constant_dynamic-slice_fusion = (bf16[448,1,896]{2,1,0:T(2,128)(2,1)S(1)}, bf16[448,1,896]{2,1,0:T(2,128)(2,1)S(1)}) fusion(bf16[448,2,896]{2,1,0:T(2,128)(2,1)} %param.7, s32[]{:T(128)S(6)} %select_n.60, s32[]{:T(128)S(6)} %select_n.59), kind=kLoop, calls=%fused_computation.56 | loop fusion | bytes 3211272 | tf_op jit(solution)/shard_map/jit(dynamic_index_in_dim)/dynamic_slice | solution.py:127
  17.9 1.0 copy.58
  18.9 2.2 %collective-permute-start.1 = (bf16[448,896]{1,0:T(8,128)(2,1)}, bf16[448,896]{1,0:T(8,128)(2,1)S(1)}, u32[]{:S(2)}, u32[]{:S(2)}) collective-permute-start(bf16[448,896]{1,0:T(8,128)(2,1)} %bitcast.46), channel_id=1, source_target_pairs={{0,16},{16,0},{32,48},{48,32},{64,80},{80,64},{96,112},{112,96},{1... | collective-permute-start | bytes 2408456 | tf_op jit(solution)/shard_map/ppermute | solution.py:124
  21.2 3.4 %collective-permute-start.3 = (bf16[448,896]{1,0:T(8,128)(2,1)}, bf16[448,896]{1,0:T(8,128)(2,1)}, u32[]{:S(2)}, u32[]{:S(2)}) collective-permute-start(bf16[448,896]{1,0:T(8,128)(2,1)} %bitcast.46), channel_id=1, source_target_pairs={{0,144},{16,128},{32,176},{48,160},{64,208},{80,192},{96,240},{112... | collective-permute-start | bytes 2408456 | tf_op jit(solution)/shard_map/ppermute | solution.py:124
  24.6 0.0 copy-start.3
  24.6 0.0 copy-start.4
  24.6 0.0 copy-start.2
  24.6 0.1 copy.59
  24.7 1.9 %collective-permute-start.2 = (bf16[448,896]{1,0:T(8,128)(2,1)S(1)}, bf16[448,896]{1,0:T(8,128)(2,1)}, u32[]{:S(2)}, u32[]{:S(2)}) collective-permute-start(bf16[448,896]{1,0:T(8,128)(2,1)S(1)} %bitcast.49), channel_id=1, source_target_pairs={{0,128},{16,144},{32,160},{48,176},{64,192},{80,208},{96,224},{112... | collective-permute-start | bytes 2408456 | tf_op jit(solution)/shard_map/ppermute | solution.py:124
  26.7 0.0 all-to-all-done
  26.7 0.1 reshape.150
  26.8 32.1 %all_gather.3.x_own = bf16[512,896]{1,0:T(8,128)(2,1)S(1)} all-gather(bf16[32,896]{1,0:T(8,128)(2,1)S(1)} %reshape.150), channel_id=1, replica_groups=mesh['dp'=32,'tensor'=16] {'tensor'}, dimensions={0}, use_global_device_ids=true | all-gather | bytes 974848 | tf_op jit(solution)/shard_map/all_gather | solution.py:144
  58.9 9.2 %collective-permute-start = (bf16[512,896]{1,0:T(8,128)(2,1)S(1)}, bf16[512,896]{1,0:T(8,128)(2,1)S(1)}, u32[]{:S(2)}, u32[]{:S(2)}) collective-permute-start(bf16[512,896]{1,0:T(8,128)(2,1)S(1)} %all_gather.3.x_own), channel_id=1, source_target_pairs={{0,16},{16,0},{32,48},{48,32},{64,80},{80,64},{96,112},{112,96},{1... | collective-permute-start | bytes 2752520 | tf_op jit(solution)/shard_map/ppermute | solution.py:124
  68.1 0.1 select_reduce_fusion.1
  68.2 0.0 copy-done.2
  68.3 0.1 add_select_fusion
  68.4 0.1 select_n.66
  68.5 0.1 dynamic_slice.15
  68.5 0.1 pad_add_fusion.where
  68.6 0.2 fusion.route
  68.8 0.0 collective-permute-done.1.w_pair
  68.8 0.0 collective-permute-done.2.w_next
  68.8 0.0 collective-permute-done.3.w_cross
  68.8 1.3 %collective-permute-done.x_other = bf16[512,896]{1,0:T(8,128)(2,1)S(1)} collective-permute-done((bf16[512,896]{1,0:T(8,128)(2,1)S(1)}, bf16[512,896]{1,0:T(8,128)(2,1)S(1)}, u32[]{:S(2)}, u32[]{:S(2)}) %collective-permute-start) | collective-permute-done | bytes 917536 | tf_op jit(solution)/shard_map/ppermute | solution.py:124
  70.1 8.5 %shard_map.77 = bf16[512,896]{1,0:T(8,128)(2,1)} custom-call(s32[2]{0:T(128)S(1)} %pad_add_fusion.where, bf16[512,896]{1,0:T(8,128)(2,1)S(1)} %all_gather.3.x_own, bf16[512,896]{1,0:T(8,128)(2,1)S(1)} %collective-permute-done.x_other, bf16[448,896]{1,0:T(8,128)(2,1)S(1)} %bitcast.50, bf16[448,896]{1,0:T(8,128)(2,1)S(1)} %collective-permute-done.1.w_pair, ...), custom_call_target="tpu_custom_call" | custom-call | flops 2113929216 | bytes 6488064 | tf_op jit(solution)/shard_map/pallas_call | solution.py:86
  78.6 0.0 copy-start.1
  78.6 7.5 %all-to-all-start.1 = ((bf16[32,16,896]{2,1,0:T(8,128)(2,1)}), bf16[32,16,896]{2,1,0:T(8,128)(2,1)S(1)}, u32[]{:S(2)}, u32[]{:S(2)}) async-start(bf16[32,16,896]{2,1,0:T(8,128)(2,1)} %bitcast.6), calls=%async_computation.1 | async-start | bytes 1835008 | tf_op jit(solution)/shard_map/all_to_all | solution.py:149
  86.3 0.1 fusion.8
  86.3 0.1 copy.30
  86.5 0.1 dynamic_slice.16
  86.6 0.1 iota_compare_fusion.2
  86.7 0.1 subtract_convert_fusion
  86.7 14.9 %all-to-all-done.1 = bf16[32,16,896]{2,1,0:T(8,128)(2,1)S(1)} async-done(((bf16[32,16,896]{2,1,0:T(8,128)(2,1)}), bf16[32,16,896]{2,1,0:T(8,128)(2,1)S(1)}, u32[]{:S(2)}, u32[]{:S(2)}) %all-to-all-start.1) | async-done | bytes 917536 | tf_op jit(solution)/shard_map/all_to_all | solution.py:149
  101.7 0.1 reduce_sum.41
  101.8 0.1 copy.22
  101.9 0.0 copy-start
  101.9 0.5 slice_reduce_fusion.1
  102.4 0.1 fusion.4
  102.6 0.2 fusion.24
  102.7 0.2 fusion.13
  102.9 0.1 fusion.14
  103.0 0.1 copy.23
  103.1 0.1 fusion.1
  103.2 0.1 fusion.12
  103.3 0.6 copy.60
  (15 shorter events, 0.2 us)
Async XLA Ops:
  2.3 24.4 %all-to-all-start = ((bf16[32,2,448]{2,1,0:T(2,128)(2,1)}), bf16[32,2,448]{2,1,0:T(2,128)(2,1)S(1)}, u32[]{:S(2)}, u32[]{:S(2)}) async-start(bf16[32,2,448]{2,1,0:T(2,128)(2,1)} %bitcast.3), calls=%async_computation | async-start | bytes 131072 | tf_op jit(solution)/shard_map/all_to_all | solution.py:120
  18.9 49.9 %collective-permute-start.1 = (bf16[448,896]{1,0:T(8,128)(2,1)}, bf16[448,896]{1,0:T(8,128)(2,1)S(1)}, u32[]{:S(2)}, u32[]{:S(2)}) collective-permute-start(bf16[448,896]{1,0:T(8,128)(2,1)} %bitcast.46), channel_id=1, source_target_pairs={{0,16},{16,0},{32,48},{48,32},{64,80},{80,64},{96,112},{112,96},{1... | collective-permute-start | bytes 2408456 | tf_op jit(solution)/shard_map/ppermute | solution.py:124
  21.2 47.6 %collective-permute-start.3 = (bf16[448,896]{1,0:T(8,128)(2,1)}, bf16[448,896]{1,0:T(8,128)(2,1)}, u32[]{:S(2)}, u32[]{:S(2)}) collective-permute-start(bf16[448,896]{1,0:T(8,128)(2,1)} %bitcast.46), channel_id=1, source_target_pairs={{0,144},{16,128},{32,176},{48,160},{64,208},{80,192},{96,240},{112... | collective-permute-start | bytes 2408456 | tf_op jit(solution)/shard_map/ppermute | solution.py:124
  24.6 43.5 %copy-start.3 = (s32[64]{0:T(128)S(1)}, s32[64]{0:T(128)}, u32[]{:S(2)}) copy-start(s32[64]{0:T(128)} %param.8) | copy-start | bytes 772
  24.6 43.5 %copy-start.4 = (s32[64]{0:T(128)S(1)}, s32[64]{0:T(128)}, u32[]{:S(2)}) copy-start(s32[64]{0:T(128)} %param.9) | copy-start | bytes 772
  24.6 43.6 %copy-start.2 = (bf16[2,896]{1,0:T(2,128)(2,1)S(1)}, bf16[2,896]{1,0:T(2,128)(2,1)}, u32[]{:S(2)}) copy-start(bf16[2,896]{1,0:T(2,128)(2,1)} %param.10) | copy-start | bytes 10756
  24.7 44.1 %collective-permute-start.2 = (bf16[448,896]{1,0:T(8,128)(2,1)S(1)}, bf16[448,896]{1,0:T(8,128)(2,1)}, u32[]{:S(2)}, u32[]{:S(2)}) collective-permute-start(bf16[448,896]{1,0:T(8,128)(2,1)S(1)} %bitcast.49), channel_id=1, source_target_pairs={{0,128},{16,144},{32,160},{48,176},{64,192},{80,208},{96,224},{112... | collective-permute-start | bytes 2408456 | tf_op jit(solution)/shard_map/ppermute | solution.py:124
  58.9 11.3 %collective-permute-start = (bf16[512,896]{1,0:T(8,128)(2,1)S(1)}, bf16[512,896]{1,0:T(8,128)(2,1)S(1)}, u32[]{:S(2)}, u32[]{:S(2)}) collective-permute-start(bf16[512,896]{1,0:T(8,128)(2,1)S(1)} %all_gather.3.x_own), channel_id=1, source_target_pairs={{0,16},{16,0},{32,48},{48,32},{64,80},{80,64},{96,112},{112,96},{1... | collective-permute-start | bytes 2752520 | tf_op jit(solution)/shard_map/ppermute | solution.py:124
  78.6 7.6 %copy-start.1 = (bf16[2,2,896]{2,1,0:T(2,128)(2,1)S(1)}, bf16[2,2,896]{2,1,0:T(2,128)(2,1)}, u32[]{:S(2)}) copy-start(bf16[2,2,896]{2,1,0:T(2,128)(2,1)} %param.11) | copy-start | bytes 21508
  78.6 23.0 %all-to-all-start.1 = ((bf16[32,16,896]{2,1,0:T(8,128)(2,1)}), bf16[32,16,896]{2,1,0:T(8,128)(2,1)S(1)}, u32[]{:S(2)}, u32[]{:S(2)}) async-start(bf16[32,16,896]{2,1,0:T(8,128)(2,1)} %bitcast.6), calls=%async_computation.1 | async-start | bytes 1835008 | tf_op jit(solution)/shard_map/all_to_all | solution.py:149
  101.9 2.0 %copy-start = (bf16[2,8,2,2,896]{4,3,2,1,0:T(2,128)(2,1)}, bf16[2,8,2,2,896]{4,3,2,1,0:T(2,128)(2,1)S(1)}, u32[]{:S(2)}) copy-start(bf16[2,8,2,2,896]{4,3,2,1,0:T(2,128)(2,1)S(1)} %copy.22) | copy-start | bytes 344068

commit v3 on v2

--- a/solution.py
+++ b/solution.py
@@ -11,7 +11,6 @@
 HD = 128
 REQ_DEV = 2
 LMAX = 16
-PAIR = 2
 
 
 def alibi_slopes(count):
@@ -52,17 +51,21 @@
 def product_kernel(where, x_own, x_other, w_own, w_pair, w_next, w_cross, route, out, xs, ws, rs, sems):
     core, half = where[0], where[1]
     block = w_own.shape[0]
+    depth = x_own.shape[1]
 
-    def rows(at):
-        return pl.ds(pl.multiple_of(at * block, 16), block)
+    def rows(chip, at):
+        return pl.ds(pl.multiple_of(chip * depth + at * block, 16), block)
+
+    def part(at):
+        return pl.ds(pl.multiple_of(at * depth, 128), depth)
 
     moves = [
-        (w_own, ws.at[half, rows(core)]),
-        (w_pair, ws.at[half, rows(1 - core)]),
-        (w_next, ws.at[1 - half, rows(core)]),
-        (w_cross, ws.at[1 - half, rows(1 - core)]),
-        (x_own, xs.at[core]),
-        (x_other, xs.at[1 - core]),
+        (w_next, ws.at[rows(1 - half, core)]),
+        (w_cross, ws.at[rows(1 - half, 1 - core)]),
+        (w_own, ws.at[rows(half, core)]),
+        (w_pair, ws.at[rows(half, 1 - core)]),
+        (x_own, xs.at[:, part(core)]),
+        (x_other, xs.at[:, part(1 - core)]),
         (route, rs),
     ]
     copies = [pltpu.make_async_copy(a, b, sems.at[i]) for i, (a, b) in enumerate(moves)]
@@ -70,13 +73,8 @@
         copy.start()
     for copy in copies:
         copy.wait()
-    columns = out.shape[1]
-    for start in range(0, columns, 256):
-        part = slice(start, min(start + 256, columns))
-        total = jnp.dot(xs[0], ws[0, :, part], preferred_element_type=jnp.float32)
-        total += jnp.dot(xs[1], ws[1, :, part], preferred_element_type=jnp.float32)
-        placed = jnp.dot(rs[...], total.astype(jnp.bfloat16), preferred_element_type=jnp.float32)
-        out[:, part] = placed.astype(jnp.bfloat16)
+    total = jnp.dot(xs[...], ws[...], preferred_element_type=jnp.float32).astype(jnp.bfloat16)
+    out[...] = jnp.dot(rs[...], total, preferred_element_type=jnp.float32).astype(jnp.bfloat16)
 
 
 def product(where, x_own, x_other, w_own, w_pair, w_next, w_cross, route):
@@ -89,8 +87,8 @@
         in_specs=[pl.BlockSpec(memory_space=pltpu.SMEM)] + [anywhere] * 7,
         out_specs=pl.BlockSpec(memory_space=pltpu.VMEM),
         scratch_shapes=[
-            pltpu.VMEM((2, rows, depth), jnp.bfloat16),
-            pltpu.VMEM((2, PAIR * block, columns), jnp.bfloat16),
+            pltpu.VMEM((rows, 2 * depth), jnp.bfloat16),
+            pltpu.VMEM((4 * block, columns), jnp.bfloat16),
             pltpu.VMEM(route.shape, jnp.bfloat16),
             pltpu.SemaphoreType.DMA((7,)),
         ],
@@ -123,8 +121,9 @@
     def swapped(array, bit):
         return lax.ppermute(array, "dp", [(i, i ^ bit) for i in range(groups)])
 
-    w_own = lax.dynamic_index_in_dim(kv_weight, core, axis=1, keepdims=False)
-    w_away = lax.dynamic_index_in_dim(kv_weight, 1 - core, axis=1, keepdims=False)
+    halves = lax.optimization_barrier(kv_weight.transpose(1, 0, 2))
+    w_own = lax.dynamic_index_in_dim(halves, core, axis=0, keepdims=False)
+    w_away = lax.dynamic_index_in_dim(halves, 1 - core, axis=0, keepdims=False)
     w_next = swapped(w_own, 8)
     w_cross = swapped(w_away, 9)
     w_pair = swapped(w_away, 1)

time: 104 us -> 97.7 us (0.939)
  local copies, waits for them, and re-layouts: 9.85 us -> 6.15 us
  Pallas kernels: 8.5 us -> 5.53 us
    dynamic_slice x1 -> x0, local copies, waits for them, and re-layouts: 5.26 us -> none  [per_device(): lax.dynamic_index_in_dim(kv_weight, 1 - core, axis=1, keepdims=False)]
    pallas_call x1, Pallas kernels: 8.5 us -> 5.53 us  [product(): pl.pallas_call(product_kernel, out_shape=jax.ShapeDtypeStruct((rows, colu...]
    unnamed x13 -> x12, local copies, waits for them, and re-layouts: 1.71 us -> 2.24 us
  transfers between devices with their start and end apart: 6 -> 6, of which waited for: 2 -> 2; matrix products, arithmetic and copies ran while one was open for 7% -> 4% of each run, Pallas kernels for 0% -> 0%
where the time goes in v3:
time: 97.7 us; the launch traced here: 97.2 us
  starting transfers between devices  34.7 us (36%)
  blocking collectives  32.1 us (33%)
  waiting for transfers between devices  16.3 us (17%)
  local copies, waits for them, and re-layouts  6.15 us (6%)
  Pallas kernels  5.53 us (6%)
  other arithmetic  1.37 us (1%)
    all_gather x1, blocking collectives, per_device(): x_own = lax.all_gather(mine, 'tensor', axis=0, tiled=True)  32.1 us
    ppermute x4, starting transfers between devices, swapped(): return lax.ppermute(array, 'dp', [(i, i ^ bit) for i in range(groups)])  16.8 us
    all_to_all x1, waiting for transfers between devices, per_device(): lax.all_to_all(partial.reshape(groups, REQ_DEV * steps, columns), 'dp', s...  14.9 us
    all_to_all x1, starting transfers between devices, per_device(): lax.all_to_all(sent.reshape(groups, 2, block), 'dp', split_axis=0, concat...  10.4 us
    all_to_all x1, starting transfers between devices, per_device(): lax.all_to_all(partial.reshape(groups, REQ_DEV * steps, columns), 'dp', s...  7.53 us
    pallas_call x1, Pallas kernels, product(): pl.pallas_call(product_kernel, out_shape=jax.ShapeDtypeStruct((rows, colu...  5.53 us
    unnamed x12, local copies, waits for them, and re-layouts  2.24 us
  transfers between devices with their start and end apart: 6, of which 2 were waited for; matrix products, arithmetic and copies ran while one was open for 4% of the time, Pallas kernels for 0%

profile of v3, /device:TPU:1, one launch (start us, length us, event | category | flops | bytes accessed | tf_op | source)
XLA Modules:
  0.0 97.2 jit_solution(11154004793570803538)
XLA Ops:
  0.6 0.9 reshape.148
  1.6 0.7 copy.16
  2.3 10.4 %all-to-all-start = ((bf16[32,2,448]{2,1,0:T(2,128)(2,1)}), bf16[32,2,448]{2,1,0:T(2,128)(2,1)S(1)}, u32[]{:S(2)}, u32[]{:S(2)}) async-start(bf16[32,2,448]{2,1,0:T(2,128)(2,1)} %bitcast.3), calls=%async_computation | async-start | bytes 131072 | tf_op jit(solution)/shard_map/all_to_all | solution.py:118
  12.7 1.6 %copy.51 = bf16[448,2,896]{2,0,1:T(8,128)(2,1)S(1)} copy(bf16[448,2,896]{2,1,0:T(2,128)(2,1)} %param.7) | data formatting | bytes 3211264 | tf_op args[1]
  14.3 0.0 copy-start.3
  14.3 0.0 copy-start.4
  14.3 0.0 copy-start.2
  14.3 1.0 %dynamic-slice_bitcast_fusion = (bf16[448,896]{1,0:T(8,128)(2,1)}, bf16[448,896]{1,0:T(8,128)(2,1)S(1)}) fusion(bf16[2,448,896]{2,1,0:T(8,128)(2,1)S(1)} %bitcast.50, s32[]{:T(128)S(6)} %select_n.60, s32[]{:T(128)S(6)} %select_n.59), kind=kLoop, calls=%fused_computation.3 | loop fusion | bytes 3211272 | tf_op jit(solution)/shard_map/jit(dynamic_index_in_dim)/squeeze | solution.py:126
  15.3 2.2 %collective-permute-start.1 = (bf16[448,896]{1,0:T(8,128)(2,1)}, bf16[448,896]{1,0:T(8,128)(2,1)S(1)}, u32[]{:S(2)}, u32[]{:S(2)}) collective-permute-start(bf16[448,896]{1,0:T(8,128)(2,1)} %get-tuple-element.8), channel_id=1, source_target_pairs={{0,16},{16,0},{32,48},{48,32},{64,80},{80,64},{96,112},{112,96},{1... | collective-permute-start | bytes 2408456 | tf_op jit(solution)/shard_map/ppermute | solution.py:122
  17.6 3.4 %collective-permute-start.3 = (bf16[448,896]{1,0:T(8,128)(2,1)}, bf16[448,896]{1,0:T(8,128)(2,1)}, u32[]{:S(2)}, u32[]{:S(2)}) collective-permute-start(bf16[448,896]{1,0:T(8,128)(2,1)} %get-tuple-element.8), channel_id=1, source_target_pairs={{0,144},{16,128},{32,176},{48,160},{64,208},{80,192},{96,240},{112... | collective-permute-start | bytes 2408456 | tf_op jit(solution)/shard_map/ppermute | solution.py:122
  21.0 1.9 %collective-permute-start.2 = (bf16[448,896]{1,0:T(8,128)(2,1)S(1)}, bf16[448,896]{1,0:T(8,128)(2,1)}, u32[]{:S(2)}, u32[]{:S(2)}) collective-permute-start(bf16[448,896]{1,0:T(8,128)(2,1)S(1)} %get-tuple-element.9.w_own), channel_id=1, source_target_pairs={{0,128},{16,144},{32,160},{48,176},{64,192},{80,208},{96,224},{112... | collective-permute-start | bytes 2408456 | tf_op jit(solution)/shard_map/ppermute | solution.py:122
  22.9 0.0 all-to-all-done
  22.9 0.1 reshape.150
  23.1 32.1 %all_gather.3.x_own = bf16[512,896]{1,0:T(8,128)(2,1)S(1)} all-gather(bf16[32,896]{1,0:T(8,128)(2,1)S(1)} %reshape.150), channel_id=1, replica_groups=mesh['dp'=32,'tensor'=16] {'tensor'}, dimensions={0}, use_global_device_ids=true | all-gather | bytes 974848 | tf_op jit(solution)/shard_map/all_gather | solution.py:143
  55.2 9.2 %collective-permute-start = (bf16[512,896]{1,0:T(8,128)(2,1)S(1)}, bf16[512,896]{1,0:T(8,128)(2,1)S(1)}, u32[]{:S(2)}, u32[]{:S(2)}) collective-permute-start(bf16[512,896]{1,0:T(8,128)(2,1)S(1)} %all_gather.3.x_own), channel_id=1, source_target_pairs={{0,16},{16,0},{32,48},{48,32},{64,80},{80,64},{96,112},{112,96},{1... | collective-permute-start | bytes 2752520 | tf_op jit(solution)/shard_map/ppermute | solution.py:122
  64.3 0.0 copy-done.3
  64.3 0.0 copy-done.4
  64.4 0.1 select_reduce_fusion.1
  64.6 0.1 add_select_fusion
  64.6 0.1 select_n.66
  64.7 0.1 dynamic_slice.15
  64.8 0.1 pad_add_fusion.where
  64.9 0.2 fusion.route
  65.1 0.0 collective-permute-done.1.w_pair
  65.1 0.0 collective-permute-done.2.w_next
  65.1 0.0 collective-permute-done.3.w_cross
  65.1 1.3 %collective-permute-done.x_other = bf16[512,896]{1,0:T(8,128)(2,1)S(1)} collective-permute-done((bf16[512,896]{1,0:T(8,128)(2,1)S(1)}, bf16[512,896]{1,0:T(8,128)(2,1)S(1)}, u32[]{:S(2)}, u32[]{:S(2)}) %collective-permute-start) | collective-permute-done | bytes 917536 | tf_op jit(solution)/shard_map/ppermute | solution.py:122
  66.4 5.5 %shard_map.77 = bf16[512,896]{1,0:T(8,128)(2,1)} custom-call(s32[2]{0:T(128)S(1)} %pad_add_fusion.where, bf16[512,896]{1,0:T(8,128)(2,1)S(1)} %all_gather.3.x_own, bf16[512,896]{1,0:T(8,128)(2,1)S(1)} %collective-permute-done.x_other, bf16[448,896]{1,0:T(8,128)(2,1)S(1)} %get-tuple-element.9.w_own, bf16[448,896]{1,0:T(8,128)(2,1)S(1)} %collective-permute-done.1.w_pair, ...), custom_call_target="tpu_custom_call" | custom-call | flops 2113929216 | bytes 6488064 | tf_op jit(solution)/shard_map/pallas_call | solution.py:84
  72.0 0.0 copy-start.1
  72.0 7.5 %all-to-all-start.1 = ((bf16[32,16,896]{2,1,0:T(8,128)(2,1)}), bf16[32,16,896]{2,1,0:T(8,128)(2,1)S(1)}, u32[]{:S(2)}, u32[]{:S(2)}) async-start(bf16[32,16,896]{2,1,0:T(8,128)(2,1)} %bitcast.7), calls=%async_computation.1 | async-start | bytes 1835008 | tf_op jit(solution)/shard_map/all_to_all | solution.py:148
  79.6 0.1 fusion.8
  79.7 0.1 copy.26
  79.8 0.1 dynamic_slice.16
  79.9 0.1 iota_compare_fusion.2
  80.0 0.1 subtract_convert_fusion
  80.0 14.9 %all-to-all-done.1 = bf16[32,16,896]{2,1,0:T(8,128)(2,1)S(1)} async-done(((bf16[32,16,896]{2,1,0:T(8,128)(2,1)}), bf16[32,16,896]{2,1,0:T(8,128)(2,1)S(1)}, u32[]{:S(2)}, u32[]{:S(2)}) %all-to-all-start.1) | async-done | bytes 917536 | tf_op jit(solution)/shard_map/all_to_all | solution.py:148
  95.0 0.1 reduce_sum.41
  95.1 0.1 copy.18
  95.2 0.0 copy-start
  95.2 0.5 slice_reduce_fusion.1
  95.7 0.1 fusion.4
  95.9 0.2 fusion.24
  96.0 0.2 fusion.13
  96.2 0.1 fusion.14
  96.3 0.1 copy.19
  96.4 0.1 fusion.1
  96.5 0.1 fusion.12
  96.6 0.6 copy.52
  (14 shorter events, 0.2 us)
Async XLA Ops:
  2.3 20.7 %all-to-all-start = ((bf16[32,2,448]{2,1,0:T(2,128)(2,1)}), bf16[32,2,448]{2,1,0:T(2,128)(2,1)S(1)}, u32[]{:S(2)}, u32[]{:S(2)}) async-start(bf16[32,2,448]{2,1,0:T(2,128)(2,1)} %bitcast.3), calls=%async_computation | async-start | bytes 131072 | tf_op jit(solution)/shard_map/all_to_all | solution.py:118
  14.3 50.1 %copy-start.3 = (s32[64]{0:T(128)S(1)}, s32[64]{0:T(128)}, u32[]{:S(2)}) copy-start(s32[64]{0:T(128)} %param.8) | copy-start | bytes 772
  14.3 50.1 %copy-start.4 = (s32[64]{0:T(128)S(1)}, s32[64]{0:T(128)}, u32[]{:S(2)}) copy-start(s32[64]{0:T(128)} %param.9) | copy-start | bytes 772
  14.3 50.2 %copy-start.2 = (bf16[2,896]{1,0:T(2,128)(2,1)S(1)}, bf16[2,896]{1,0:T(2,128)(2,1)}, u32[]{:S(2)}) copy-start(bf16[2,896]{1,0:T(2,128)(2,1)} %param.10) | copy-start | bytes 10756
  15.3 49.7 %collective-permute-start.1 = (bf16[448,896]{1,0:T(8,128)(2,1)}, bf16[448,896]{1,0:T(8,128)(2,1)S(1)}, u32[]{:S(2)}, u32[]{:S(2)}) collective-permute-start(bf16[448,896]{1,0:T(8,128)(2,1)} %get-tuple-element.8), channel_id=1, source_target_pairs={{0,16},{16,0},{32,48},{48,32},{64,80},{80,64},{96,112},{112,96},{1... | collective-permute-start | bytes 2408456 | tf_op jit(solution)/shard_map/ppermute | solution.py:122
  17.6 47.5 %collective-permute-start.3 = (bf16[448,896]{1,0:T(8,128)(2,1)}, bf16[448,896]{1,0:T(8,128)(2,1)}, u32[]{:S(2)}, u32[]{:S(2)}) collective-permute-start(bf16[448,896]{1,0:T(8,128)(2,1)} %get-tuple-element.8), channel_id=1, source_target_pairs={{0,144},{16,128},{32,176},{48,160},{64,208},{80,192},{96,240},{112... | collective-permute-start | bytes 2408456 | tf_op jit(solution)/shard_map/ppermute | solution.py:122
  21.0 44.1 %collective-permute-start.2 = (bf16[448,896]{1,0:T(8,128)(2,1)S(1)}, bf16[448,896]{1,0:T(8,128)(2,1)}, u32[]{:S(2)}, u32[]{:S(2)}) collective-permute-start(bf16[448,896]{1,0:T(8,128)(2,1)S(1)} %get-tuple-element.9.w_own), channel_id=1, source_target_pairs={{0,128},{16,144},{32,160},{48,176},{64,192},{80,208},{96,224},{112... | collective-permute-start | bytes 2408456 | tf_op jit(solution)/shard_map/ppermute | solution.py:122
  55.2 11.3 %collective-permute-start = (bf16[512,896]{1,0:T(8,128)(2,1)S(1)}, bf16[512,896]{1,0:T(8,128)(2,1)S(1)}, u32[]{:S(2)}, u32[]{:S(2)}) collective-permute-start(bf16[512,896]{1,0:T(8,128)(2,1)S(1)} %all_gather.3.x_own), channel_id=1, source_target_pairs={{0,16},{16,0},{32,48},{48,32},{64,80},{80,64},{96,112},{112,96},{1... | collective-permute-start | bytes 2752520 | tf_op jit(solution)/shard_map/ppermute | solution.py:122
  72.0 7.6 %copy-start.1 = (bf16[2,2,896]{2,1,0:T(2,128)(2,1)S(1)}, bf16[2,2,896]{2,1,0:T(2,128)(2,1)}, u32[]{:S(2)}) copy-start(bf16[2,2,896]{2,1,0:T(2,128)(2,1)} %param.11) | copy-start | bytes 21508
  72.0 23.0 %all-to-all-start.1 = ((bf16[32,16,896]{2,1,0:T(8,128)(2,1)}), bf16[32,16,896]{2,1,0:T(8,128)(2,1)S(1)}, u32[]{:S(2)}, u32[]{:S(2)}) async-start(bf16[32,16,896]{2,1,0:T(8,128)(2,1)} %bitcast.7), calls=%async_computation.1 | async-start | bytes 1835008 | tf_op jit(solution)/shard_map/all_to_all | solution.py:148
  95.2 2.0 %copy-start = (bf16[2,8,2,2,896]{4,3,2,1,0:T(2,128)(2,1)}, bf16[2,8,2,2,896]{4,3,2,1,0:T(2,128)(2,1)S(1)}, u32[]{:S(2)}) copy-start(bf16[2,8,2,2,896]{4,3,2,1,0:T(2,128)(2,1)S(1)} %copy.18) | copy-start | bytes 344068

commit v4 on v3

--- a/solution.py
+++ b/solution.py
@@ -48,57 +48,83 @@
     return mixed.reshape(slots, heads * HD).astype(jnp.bfloat16)
 
 
-def product_kernel(where, x_own, x_other, w_own, w_pair, w_next, w_cross, route, out, xs, ws, rs, sems):
-    core, half = where[0], where[1]
-    block = w_own.shape[0]
-    depth = x_own.shape[1]
+VMEM = pl.BlockSpec(memory_space=pltpu.VMEM)
+SMEM = pl.BlockSpec(memory_space=pltpu.SMEM)
+ANYWHERE = pl.BlockSpec(memory_space=pl.ANY)
+KERNEL_VMEM = 24 * 1024 * 1024
+SHARE = 2
+WIDE, HALF, ROWS_Y, CORES = 2, 2, 4, 2
 
-    def rows(chip, at):
-        return pl.ds(pl.multiple_of(chip * depth + at * block, 16), block)
 
-    def part(at):
-        return pl.ds(pl.multiple_of(at * depth, 128), depth)
+def split_rows_kernel(rows, sent):
+    block = sent.shape[2]
+    for wide in range(WIDE):
+        for half in range(HALF):
+            for y in range(ROWS_Y):
+                for core in range(CORES):
+                    to = ((wide * HALF + half) * ROWS_Y + y) * CORES + core
+                    for part in range(SHARE):
+                        chip = half if part == 0 else 1 - half
+                        at = ((wide * HALF + chip) * ROWS_Y + y) * CORES + core
+                        sent[to, part : part + 1, :] = rows[half : half + 1, at * block : (at + 1) * block]
 
-    moves = [
-        (w_next, ws.at[rows(1 - half, core)]),
-        (w_cross, ws.at[rows(1 - half, 1 - core)]),
-        (w_own, ws.at[rows(half, core)]),
-        (w_pair, ws.at[rows(half, 1 - core)]),
-        (x_own, xs.at[:, part(core)]),
-        (x_other, xs.at[:, part(1 - core)]),
-        (route, rs),
+
+def split_rows(rows, groups):
+    block = rows.shape[1] // groups
+    return pl.pallas_call(
+        split_rows_kernel,
+        out_shape=jax.ShapeDtypeStruct((groups, SHARE, block), jnp.bfloat16),
+        in_specs=[VMEM],
+        out_specs=VMEM,
+        compiler_params=pltpu.CompilerParams(vmem_limit_bytes=KERNEL_VMEM),
+    )(rows)
+
+
+def load_weights(column, w_own, w_next, held, sems):
+    block = w_own.shape[1]
+    copies = [
+        pltpu.make_async_copy(w_own.at[column], held.at[pl.ds(0, block)], sems.at[0]),
+        pltpu.make_async_copy(w_next.at[column], held.at[pl.ds(block, block)], sems.at[1]),
     ]
-    copies = [pltpu.make_async_copy(a, b, sems.at[i]) for i, (a, b) in enumerate(moves)]
     for copy in copies:
         copy.start()
+    return copies
+
+
+def away_kernel(where, x, w_own, w_next, route, away, picked, held, sems):
+    copies = load_weights(1 - where[0], w_own, w_next, held, sems)
+    rows = jnp.dot(route[...], x[...], preferred_element_type=jnp.float32).astype(jnp.bfloat16)
+    picked[...] = rows
     for copy in copies:
         copy.wait()
-    total = jnp.dot(xs[...], ws[...], preferred_element_type=jnp.float32).astype(jnp.bfloat16)
-    out[...] = jnp.dot(rs[...], total, preferred_element_type=jnp.float32).astype(jnp.bfloat16)
+    away[...] = jnp.dot(rows, held[...], preferred_element_type=jnp.float32).astype(jnp.bfloat16)
 
 
-def product(where, x_own, x_other, w_own, w_pair, w_next, w_cross, route):
-    rows, depth = x_own.shape
-    block, columns = w_own.shape
-    anywhere = pl.BlockSpec(memory_space=pl.ANY)
+def home_kernel(where, picked, w_own, w_next, home, held, sems):
+    for copy in load_weights(where[0], w_own, w_next, held, sems):
+        copy.wait()
+    home[...] = jnp.dot(picked[...], held[...], preferred_element_type=jnp.float32).astype(jnp.bfloat16)
+
+
+def product_call(kernel, name, where, x, w_own, w_next, route=()):
+    rows, depth = x.shape
+    columns = w_own.shape[2]
+    one = jax.ShapeDtypeStruct((rows, columns), jnp.bfloat16)
+    outs = [one, jax.ShapeDtypeStruct((rows, depth), jnp.bfloat16)] if route else one
     return pl.pallas_call(
-        product_kernel,
-        out_shape=jax.ShapeDtypeStruct((rows, columns), jnp.bfloat16),
-        in_specs=[pl.BlockSpec(memory_space=pltpu.SMEM)] + [anywhere] * 7,
-        out_specs=pl.BlockSpec(memory_space=pltpu.VMEM),
-        scratch_shapes=[
-            pltpu.VMEM((rows, 2 * depth), jnp.bfloat16),
-            pltpu.VMEM((4 * block, columns), jnp.bfloat16),
-            pltpu.VMEM(route.shape, jnp.bfloat16),
-            pltpu.SemaphoreType.DMA((7,)),
-        ],
-        compiler_params=pltpu.CompilerParams(vmem_limit_bytes=24 * 1024 * 1024),
+        kernel,
+        out_shape=outs,
+        in_specs=[SMEM, VMEM, ANYWHERE, ANYWHERE] + [VMEM] * len(route),
+        out_specs=[VMEM, VMEM] if route else VMEM,
+        scratch_shapes=[pltpu.VMEM((depth, columns), jnp.bfloat16), pltpu.SemaphoreType.DMA((2,))],
+        compiler_params=pltpu.CompilerParams(vmem_limit_bytes=KERNEL_VMEM),
         cost_estimate=pl.CostEstimate(
-            flops=2 * rows * columns * (2 * depth + rows),
-            bytes_accessed=2 * (2 * rows * depth + 4 * block * columns + rows * rows + rows * columns),
+            flops=2 * rows * depth * (columns + rows * len(route)),
+            bytes_accessed=2 * (rows * depth * (1 + len(route)) + depth * columns + rows * columns),
             transcendentals=0,
         ),
-    )(where, x_own, x_other, w_own, w_pair, w_next, w_cross, route)
+        name=name,
+    )(where, x, w_own, w_next, *route)
 
 
 def per_device(stored_rows, kv_weight, lengths, new_place, query, new_kv):
@@ -114,19 +140,13 @@
     columns = kv_weight.shape[2]
     heads_here = columns // HD
 
-    sent = stored_rows.reshape(2, 2, 2, 4, 2, block).transpose(1, 0, 3, 2, 4, 5)
-    mine = lax.all_to_all(sent.reshape(groups, 2, block), "dp", split_axis=0, concat_axis=0, tiled=True)
-    mine = mine.reshape(groups, 2 * block)
-
     def swapped(array, bit):
         return lax.ppermute(array, "dp", [(i, i ^ bit) for i in range(groups)])
 
-    halves = lax.optimization_barrier(kv_weight.transpose(1, 0, 2))
-    w_own = lax.dynamic_index_in_dim(halves, core, axis=0, keepdims=False)
-    w_away = lax.dynamic_index_in_dim(halves, 1 - core, axis=0, keepdims=False)
-    w_next = swapped(w_own, 8)
-    w_cross = swapped(w_away, 9)
-    w_pair = swapped(w_away, 1)
+    mine = lax.all_to_all(split_rows(stored_rows, groups), "dp", split_axis=0, concat_axis=0, tiled=True)
+    mine = mine.reshape(groups, SHARE * block)
+    w_own = kv_weight.transpose(1, 0, 2)
+    w_next = swapped(w_own, ROWS_Y * CORES)
 
     slots = jnp.arange(requests, dtype=jnp.int32)
     at_slot = new_place[None, :] == slots[:, None]
@@ -140,15 +160,17 @@
     row = jnp.where(live, row, -1).reshape(-1)
     route = (row[:, None] == jnp.arange(planes * groups, dtype=jnp.int32)[None, :]).astype(jnp.bfloat16)
 
-    x_own = lax.all_gather(mine, "tensor", axis=0, tiled=True)
-    x_other = swapped(x_own, 1)
+    every = lax.all_gather(mine, "tensor", axis=0, tiled=True)
     where = jnp.stack([core, half]).astype(jnp.int32)
-    partial = product(where, x_own, x_other, w_own, w_pair, w_next, w_cross, route)
+    away, picked = product_call(away_kernel, "away", where, every, w_own, w_next, (route,))
+    received = swapped(away, 1)
+    home = product_call(home_kernel, "home", where, picked, w_own, w_next)
+    partial = (home.astype(jnp.float32) + received.astype(jnp.float32)).astype(jnp.bfloat16)
 
     arrived = lax.all_to_all(
         partial.reshape(groups, REQ_DEV * steps, columns), "dp", split_axis=0, concat_axis=0, tiled=True
     )
-    arrived = arrived.reshape(2, 2, 4, 2, REQ_DEV, steps, columns)
+    arrived = arrived.reshape(WIDE, HALF, ROWS_Y, CORES, REQ_DEV, steps, columns)
     summed = jnp.sum(arrived, axis=(0, 2), dtype=jnp.float32).astype(jnp.bfloat16)
     kv_cache = summed.transpose(2, 3, 0, 1, 4).reshape(REQ_DEV, LMAX, 2, columns)
     here_len = lax.dynamic_slice_in_dim(slot_len, group_index * REQ_DEV, REQ_DEV)

time: 97.7 us -> 124 us (1.27)
  waiting for transfers between devices: 16.3 us -> 45.7 us
  starting transfers between devices: 34.7 us -> 24.8 us
  other arithmetic: 1.37 us -> 4.53 us
  blocking collectives: 32.1 us -> 34.3 us
    all_to_all x1, waiting for transfers between devices: 0.01 us -> 30.7 us  [per_device(): lax.all_to_all(split_rows(stored_rows, groups), 'dp', split_axis=0, conca...]
    ppermute x4 -> x2, starting transfers between devices: 16.8 us -> 12.6 us  [swapped(): return lax.ppermute(array, 'dp', [(i, i ^ bit) for i in range(groups)])]
    all_to_all x1, starting transfers between devices: 7.53 us -> 3.84 us  [per_device(): lax.all_to_all(partial.reshape(groups, REQ_DEV * steps, columns), 'dp', s...]
    unnamed x12 -> x20, local copies, waits for them, and re-layouts: 2.24 us -> 5.41 us
    convert_element_type x0 -> x1, other arithmetic: none -> 2.36 us  [per_device(): (home.astype(jnp.float32) + received.astype(jnp.float32)).astype(jnp.bflo...]
    all_gather x1, blocking collectives: 32.1 us -> 34.3 us  [per_device(): every = lax.all_gather(mine, 'tensor', axis=0, tiled=True)]
    all_to_all x1, starting transfers between devices: 10.4 us -> 8.36 us  [per_device(): lax.all_to_all(split_rows(stored_rows, groups), 'dp', split_axis=0, conca...]
    ppermute x4 -> x2, waiting for transfers between devices: 1.34 us -> 0.01 us  [swapped(): return lax.ppermute(array, 'dp', [(i, i ^ bit) for i in range(groups)])]
  transfers between devices with their start and end apart: 6 -> 4, of which waited for: 2 -> 2; matrix products, arithmetic and copies ran while one was open for 4% -> 2% of each run, Pallas kernels for 0% -> 2%
where the time goes in v4:
time: 124 us; the launch traced here: 123 us
  waiting for transfers between devices  45.7 us (37%)
  blocking collectives  34.3 us (28%)
  starting transfers between devices  24.8 us (20%)
  local copies, waits for them, and re-layouts  6.66 us (5%)
  Pallas kernels  6.31 us (5%)
  other arithmetic  4.53 us (4%)
    all_gather x1, blocking collectives, per_device(): every = lax.all_gather(mine, 'tensor', axis=0, tiled=True)  34.3 us
    all_to_all x1, waiting for transfers between devices, per_device(): lax.all_to_all(split_rows(stored_rows, groups), 'dp', split_axis=0, conca...  30.7 us
    all_to_all x1, waiting for transfers between devices, per_device(): lax.all_to_all(partial.reshape(groups, REQ_DEV * steps, columns), 'dp', s...  14.9 us
    ppermute x2, starting transfers between devices, swapped(): return lax.ppermute(array, 'dp', [(i, i ^ bit) for i in range(groups)])  12.6 us
    all_to_all x1, starting transfers between devices, per_device(): lax.all_to_all(split_rows(stored_rows, groups), 'dp', split_axis=0, conca...  8.36 us
    pallas_call x2, Pallas kernels, product_call(): pl.pallas_call(kernel, out_shape=outs, in_specs=[SMEM, VMEM, ANYWHERE, AN...  5.57 us
    unnamed x20, local copies, waits for them, and re-layouts  5.41 us
    all_to_all x1, starting transfers between devices, per_device(): lax.all_to_all(partial.reshape(groups, REQ_DEV * steps, columns), 'dp', s...  3.84 us
  transfers between devices with their start and end apart: 4, of which 2 were waited for; matrix products, arithmetic and copies ran while one was open for 2% of the time, Pallas kernels for 2%

profile of v4, /device:TPU:1, one launch (start us, length us, event | category | flops | bytes accessed | tf_op | source)
XLA Modules:
  0.0 123.4 jit_solution(15913938085931568087)
XLA Ops:
  0.6 0.0 copy-start.3
  0.6 0.0 copy-start.7
  0.7 0.0 copy-start.8
  0.7 1.6 %copy.47 = bf16[448,2,896]{2,0,1:T(8,128)(2,1)S(1)} copy(bf16[448,2,896]{2,1,0:T(2,128)(2,1)} %param.7) | data formatting | bytes 3211264 | tf_op args[1]
  2.3 3.9 %collective-permute-start = (bf16[2,448,896]{2,1,0:T(8,128)(2,1)S(1)}, bf16[2,448,896]{2,1,0:T(8,128)(2,1)S(1)}, u32[]{:S(2)}, u32[]{:S(2)}) collective-permute-start(bf16[2,448,896]{2,1,0:T(8,128)(2,1)S(1)} %bitcast.44), channel_id=1, source_target_pairs={{0,128},{16,144},{32,160},{48,176},{64,192},{80,208},{96,224},{112... | collective-permute-start | bytes 4816904 | tf_op jit(solution)/shard_map/ppermute | solution.py:144
  6.3 0.0 copy-done.3
  6.3 0.7 shard_map.77
  7.0 8.4 %all-to-all-start = ((bf16[32,2,448]{2,1,0:T(2,128)(2,1)}), bf16[32,2,448]{2,1,0:T(2,128)(2,1)S(1)}, u32[]{:S(2)}, u32[]{:S(2)}) async-start(bf16[32,2,448]{2,1,0:T(2,128)(2,1)} %shard_map.77), calls=%async_computation | async-start | bytes 131072 | tf_op jit(solution)/shard_map/all_to_all | solution.py:146
  15.4 0.0 copy-done.7
  15.4 0.0 copy-done.8
  15.4 0.1 select_reduce_fusion.1
  15.5 0.1 add_select_fusion
  15.6 0.1 select_n.57
  15.7 0.9 fusion.route
  16.7 0.1 pad_add_fusion.where
  16.8 30.7 %all-to-all-done = bf16[32,2,448]{2,1,0:T(2,128)(2,1)S(1)} async-done(((bf16[32,2,448]{2,1,0:T(2,128)(2,1)}), bf16[32,2,448]{2,1,0:T(2,128)(2,1)S(1)}, u32[]{:S(2)}, u32[]{:S(2)}) %all-to-all-start) | async-done | bytes 57376 | tf_op jit(solution)/shard_map/all_to_all | solution.py:146
  47.5 0.1 reshape.142
  47.6 34.3 %all_gather.3.x = bf16[512,896]{1,0:T(8,128)(2,1)S(1)} all-gather(bf16[32,896]{1,0:T(8,128)(2,1)S(1)} %reshape.142), channel_id=1, replica_groups=mesh['dp'=32,'tensor'=16] {'tensor'}, dimensions={0}, use_global_device_ids=true | all-gather | bytes 974848 | tf_op jit(solution)/shard_map/all_gather | solution.py:163
  81.9 0.0 collective-permute-done.w_next
  81.9 1.0 copy-done.2
  82.9 3.6 %away.1 = (bf16[512,896]{1,0:T(8,128)(2,1)}, bf16[512,896]{1,0:T(8,128)(2,1)S(1)}) custom-call(s32[2]{0:T(128)S(1)} %pad_add_fusion.where, bf16[512,896]{1,0:T(8,128)(2,1)S(1)} %all_gather.3.x, bf16[2,448,896]{2,1,0:T(8,128)(2,1)S(1)} %bitcast.45, bf16[2,448,896]{2,1,0:T(8,128)(2,1)S(1)} %collective-permute-done.w_next, bf16[512,512]{1,0:T(8,128)(2,1)S(1)} %copy-done.2), custom_call_target="tpu_custom_call" | custom-call | flops 1291845632 | bytes 4358144 | tf_op jit(solution)/shard_map/away/pallas_call | solution.py:114
  86.6 0.0 copy-start
  86.6 0.9 copy-done
  87.5 8.7 %collective-permute-start.1 = (bf16[512,896]{1,0:T(8,128)(2,1)}, bf16[512,896]{1,0:T(8,128)(2,1)}, u32[]{:S(2)}, u32[]{:S(2)}) collective-permute-start(bf16[512,896]{1,0:T(8,128)(2,1)} %get-tuple-element.5), channel_id=1, source_target_pairs={{0,16},{16,0},{32,48},{48,32},{64,80},{80,64},{96,112},{112,96},{1... | collective-permute-start | bytes 2752520 | tf_op jit(solution)/shard_map/ppermute | solution.py:144
  96.3 0.1 dynamic_slice.6
  96.3 1.2 copy-done.1
  97.5 1.9 %home.1 = bf16[512,896]{1,0:T(8,128)(2,1)S(1)} custom-call(s32[2]{0:T(128)S(1)} %pad_add_fusion.where, bf16[512,896]{1,0:T(8,128)(2,1)S(1)} %copy-done.1, bf16[2,448,896]{2,1,0:T(8,128)(2,1)S(1)} %bitcast.46, bf16[2,448,896]{2,1,0:T(8,128)(2,1)S(1)} %collective-permute-done.w_next), custom_call_target="tpu_custom_call" | custom-call | flops 822083584 | bytes 3440640 | tf_op jit(solution)/shard_map/home/pallas_call | solution.py:114
  99.4 0.0 collective-permute-done.1
  99.5 2.4 %add_convert_fusion = bf16[512,896]{1,0:T(8,128)(2,1)} fusion(bf16[512,896]{1,0:T(8,128)(2,1)} %collective-permute-done.1, bf16[512,896]{1,0:T(8,128)(2,1)S(1)} %home.1), kind=kLoop, calls=%fused_computation | loop fusion | flops 1835008 | bytes 2752512 | tf_op jit(solution)/shard_map/convert_element_type | solution.py:168
  101.8 3.8 %all-to-all-start.1 = ((bf16[32,16,896]{2,1,0:T(8,128)(2,1)}), bf16[32,16,896]{2,1,0:T(8,128)(2,1)S(1)}, u32[]{:S(2)}, u32[]{:S(2)}) async-start(bf16[32,16,896]{2,1,0:T(8,128)(2,1)} %bitcast.3), calls=%async_computation.1 | async-start | bytes 1835008 | tf_op jit(solution)/shard_map/all_to_all | solution.py:170
  105.7 0.1 fusion.8
  105.8 0.1 copy.22
  106.0 0.1 dynamic_slice.7
  106.1 0.1 iota_compare_fusion.2
  106.1 0.1 subtract_convert_fusion
  106.2 14.9 %all-to-all-done.1 = bf16[32,16,896]{2,1,0:T(8,128)(2,1)S(1)} async-done(((bf16[32,16,896]{2,1,0:T(8,128)(2,1)}), bf16[32,16,896]{2,1,0:T(8,128)(2,1)S(1)}, u32[]{:S(2)}, u32[]{:S(2)}) %all-to-all-start.1) | async-done | bytes 917536 | tf_op jit(solution)/shard_map/all_to_all | solution.py:170
  121.1 0.1 reduce_sum.41
  121.3 0.1 copy.14
  121.3 0.0 copy-start.4
  121.4 0.5 slice_reduce_fusion.1
  121.9 0.1 fusion.4
  122.0 0.2 fusion.24
  122.2 0.2 fusion.13
  122.4 0.1 fusion.14
  122.5 0.1 copy.15
  122.6 0.1 fusion.1
  122.7 0.1 fusion.12
  122.8 0.6 copy.48
  (18 shorter events, 0.2 us)
Async XLA Ops:
  0.6 5.6 %copy-start.3 = (bf16[2,14336]{1,0:T(2,128)(2,1)S(1)}, bf16[2,14336]{1,0:T(2,128)(2,1)}, u32[]{:S(2)}) copy-start(bf16[2,14336]{1,0:T(2,128)(2,1)} %rows.1) | copy-start | bytes 172036
  0.6 14.8 %copy-start.7 = (s32[64]{0:T(128)S(1)}, s32[64]{0:T(128)}, u32[]{:S(2)}) copy-start(s32[64]{0:T(128)} %param.8) | copy-start | bytes 772
  0.7 14.8 %copy-start.8 = (s32[64]{0:T(128)S(1)}, s32[64]{0:T(128)}, u32[]{:S(2)}) copy-start(s32[64]{0:T(128)} %param.9) | copy-start | bytes 772
  2.3 79.6 %collective-permute-start = (bf16[2,448,896]{2,1,0:T(8,128)(2,1)S(1)}, bf16[2,448,896]{2,1,0:T(8,128)(2,1)S(1)}, u32[]{:S(2)}, u32[]{:S(2)}) collective-permute-start(bf16[2,448,896]{2,1,0:T(8,128)(2,1)S(1)} %bitcast.44), channel_id=1, source_target_pairs={{0,128},{16,144},{32,160},{48,176},{64,192},{80,208},{96,224},{112... | collective-permute-start | bytes 4816904 | tf_op jit(solution)/shard_map/ppermute | solution.py:144
  7.0 40.5 %all-to-all-start = ((bf16[32,2,448]{2,1,0:T(2,128)(2,1)}), bf16[32,2,448]{2,1,0:T(2,128)(2,1)S(1)}, u32[]{:S(2)}, u32[]{:S(2)}) async-start(bf16[32,2,448]{2,1,0:T(2,128)(2,1)} %shard_map.77), calls=%async_computation | async-start | bytes 131072 | tf_op jit(solution)/shard_map/all_to_all | solution.py:146
  81.9 1.0 copy-start.2
  82.9 13.3 %copy-start.6 = (bf16[2,896]{1,0:T(2,128)(2,1)S(1)}, bf16[2,896]{1,0:T(2,128)(2,1)}, u32[]{:S(2)}) copy-start(bf16[2,896]{1,0:T(2,128)(2,1)} %param.10) | copy-start | bytes 10756
  86.6 0.9 copy-start
  87.5 11.9 %collective-permute-start.1 = (bf16[512,896]{1,0:T(8,128)(2,1)}, bf16[512,896]{1,0:T(8,128)(2,1)}, u32[]{:S(2)}, u32[]{:S(2)}) collective-permute-start(bf16[512,896]{1,0:T(8,128)(2,1)} %get-tuple-element.5), channel_id=1, source_target_pairs={{0,16},{16,0},{32,48},{48,32},{64,80},{80,64},{96,112},{112,96},{1... | collective-permute-start | bytes 2752520 | tf_op jit(solution)/shard_map/ppermute | solution.py:144
  96.3 1.2 copy-start.1
  101.8 3.9 %copy-start.5 = (bf16[2,2,896]{2,1,0:T(2,128)(2,1)S(1)}, bf16[2,2,896]{2,1,0:T(2,128)(2,1)}, u32[]{:S(2)}) copy-start(bf16[2,2,896]{2,1,0:T(2,128)(2,1)} %param.11) | copy-start | bytes 21508
  101.8 19.3 %all-to-all-start.1 = ((bf16[32,16,896]{2,1,0:T(8,128)(2,1)}), bf16[32,16,896]{2,1,0:T(8,128)(2,1)S(1)}, u32[]{:S(2)}, u32[]{:S(2)}) async-start(bf16[32,16,896]{2,1,0:T(8,128)(2,1)} %bitcast.3), calls=%async_computation.1 | async-start | bytes 1835008 | tf_op jit(solution)/shard_map/all_to_all | solution.py:170
  121.3 2.0 %copy-start.4 = (bf16[2,8,2,2,896]{4,3,2,1,0:T(2,128)(2,1)}, bf16[2,8,2,2,896]{4,3,2,1,0:T(2,128)(2,1)S(1)}, u32[]{:S(2)}) copy-start(bf16[2,8,2,2,896]{4,3,2,1,0:T(2,128)(2,1)S(1)} %copy.14) | copy-start | bytes 344068

commit v5 on v4

v5 whole, which is shorter than its diff:
```python
import functools
import math

import jax
import jax.numpy as jnp
from jax import lax
from jax.experimental import pallas as pl
from jax.experimental.pallas import tpu as pltpu
from jax.sharding import PartitionSpec as P

HEADS = 112
HD = 128
REQ_DEV = 2
LMAX = 16


def alibi_slopes(count):
    closest = 2 ** int(math.floor(math.log2(count)))
    counted = jnp.arange(count, dtype=jnp.float32)
    leading = jnp.exp2(-8.0 * (counted + 1.0) / closest)
    trailing = jnp.exp2(-4.0 * (2.0 * (counted - closest) + 1.0) / closest)
    return jnp.where(counted < closest, leading, trailing)


def attend(cache, query, new_kv, slot_len, slopes):
    slots = query.shape[0]
    heads = slopes.shape[0]
    keys = cache[:, :, 0, :].reshape(slots, LMAX, heads, HD)
    values = cache[:, :, 1, :].reshape(slots, LMAX, heads, HD)
    asked = query.reshape(slots, heads, HD)
    own_key = new_kv[:, 0, :].reshape(slots, heads, HD)
    own_value = new_kv[:, 1, :].reshape(slots, heads, HD).astype(jnp.float32)
    factor = 1.0 / math.sqrt(HD)
    scores = jnp.einsum("shd,sphd->shp", asked, keys, preferred_element_type=jnp.float32) * factor
    place = jnp.arange(LMAX, dtype=jnp.int32)
    distance = (slot_len[:, None] - place[None, :]).astype(jnp.float32)
    scores = scores - slopes[None, :, None] * distance[:, None, :]
    valid = place[None, :] < slot_len[:, None]
    scores = jnp.where(valid[:, None, :], scores, -jnp.inf)
    own = jnp.einsum("shd,shd->sh", asked, own_key, preferred_element_type=jnp.float32) * factor
    top = jnp.maximum(jnp.max(scores, axis=2), own)
    raised = jnp.exp(scores - top[:, :, None])
    own_raised = jnp.exp(own - top)
    total = jnp.sum(raised, axis=2) + own_raised
    weights = (raised / total[:, :, None]).astype(jnp.bfloat16)
    own_weight = (own_raised / total).astype(jnp.bfloat16).astype(jnp.float32)
    mixed = jnp.einsum("shp,sphd->shd", weights, values, preferred_element_type=jnp.float32)
    mixed = mixed + own_weight[:, :, None] * own_value
    return mixed.reshape(slots, heads * HD).astype(jnp.bfloat16)


VMEM = pl.BlockSpec(memory_space=pltpu.VMEM)
SMEM = pl.BlockSpec(memory_space=pltpu.SMEM)
ANYWHERE = pl.BlockSpec(memory_space=pl.ANY)
HBM = pl.BlockSpec(memory_space=pltpu.HBM)
KERNEL_VMEM = 24 * 1024 * 1024
TILE = 512
SIDE = 4
CORES = 2


def partner(index):
    return index ^ (2 * SIDE if index % CORES == 0 else CORES)


def parity(index):
    return (index // (CORES * SIDE) + index // CORES) % 2


def split_rows_kernel(rows, sent):
    groups, share, block = sent.shape
    for to in range(groups):
        row = parity(to)
        for part, at in enumerate((to, partner(to))):
            sent[to, part : part + 1, :] = rows[row : row + 1, at * block : (at + 1) * block]


def split_rows(rows, groups):
    block = rows.shape[1] // groups
    return pl.pallas_call(
        split_rows_kernel,
        out_shape=jax.ShapeDtypeStruct((groups, 2, block), jnp.bfloat16),
        in_specs=[VMEM],
        out_specs=VMEM,
        compiler_params=pltpu.CompilerParams(vmem_limit_bytes=KERNEL_VMEM),
        name="split_rows",
    )(rows)


def join_rows_kernel(parts, rows):
    block = parts.shape[2]
    rows[:, :block] = parts[:, 0, :]
    rows[:, block:] = parts[:, 1, :]


def join_rows(parts):
    groups, share, block = parts.shape
    return pl.pallas_call(
        join_rows_kernel,
        out_shape=jax.ShapeDtypeStruct((groups, share * block), jnp.bfloat16),
        in_specs=[VMEM],
        out_specs=VMEM,
        compiler_params=pltpu.CompilerParams(vmem_limit_bytes=KERNEL_VMEM),
        cost_estimate=pl.CostEstimate(flops=34500000000, bytes_accessed=0, transcendentals=0),
        name="join_rows",
    )(parts)


def fetch(moves, sems):
    copies = [pltpu.make_async_copy(source, to, sems.at[at]) for at, (source, to) in enumerate(moves)]
    for copy in copies:
        copy.start()
    return copies


def finish(copies):
    for copy in copies:
        copy.wait()


def product_kernel(home, where, x, w_own, w_next, route, out, xs, rs, held, made, sems):
    column = where[0] if home else 1 - where[0]
    block = w_own.shape[1]
    copies = fetch(
        [
            (x, xs),
            (route, rs),
            (w_own.at[column], held.at[pl.ds(0, block)]),
            (w_next.at[column], held.at[pl.ds(block, block)]),
        ],
        sems,
    )
    finish(copies[:2])
    rows = jnp.dot(rs[...], xs[...], preferred_element_type=jnp.float32).astype(jnp.bfloat16)
    finish(copies[2:])
    stores = []
    for at, start in enumerate(range(0, out.shape[1], TILE)):
        part = pl.ds(start, min(TILE, out.shape[1] - start))
        made[:, part] = jnp.dot(rows, held[:, part], preferred_element_type=jnp.float32).astype(jnp.bfloat16)
        stores += fetch([(made.at[:, part], out.at[:, part])], sems.at[pl.ds(4 + at, 1)])
    finish(stores)


def product(home, where, x, w_own, w_next, route):
    rows, depth = x.shape
    columns = w_own.shape[2]
    return pl.pallas_call(
        functools.partial(product_kernel, home),
        out_shape=jax.ShapeDtypeStruct((rows, columns), jnp.bfloat16),
        in_specs=[SMEM, ANYWHERE, ANYWHERE, ANYWHERE, HBM],
        out_specs=ANYWHERE,
        scratch_shapes=[
            pltpu.VMEM(x.shape, jnp.bfloat16),
            pltpu.VMEM(route.shape, jnp.bfloat16),
            pltpu.VMEM((depth, columns), jnp.bfloat16),
            pltpu.VMEM((rows, columns), jnp.bfloat16),
            pltpu.SemaphoreType.DMA((4 + pl.cdiv(columns, TILE),)),
        ],
        compiler_params=pltpu.CompilerParams(vmem_limit_bytes=KERNEL_VMEM),
        cost_estimate=pl.CostEstimate(
            flops=2 * rows * depth * (columns + rows),
            bytes_accessed=2 * (rows * depth + rows * rows + depth * columns + rows * columns),
            transcendentals=0,
        ),
        name="home" if home else "away",
    )(where, x, w_own, w_next, route)


def add_kernel(one, other, total, left, right, sems):
    finish(fetch([(one, left), (other, right)], sems))
    left[...] = (left[...].astype(jnp.float32) + right[...].astype(jnp.float32)).astype(jnp.bfloat16)
    finish(fetch([(left, total)], sems))


def add(one, other):
    return pl.pallas_call(
        add_kernel,
        out_shape=jax.ShapeDtypeStruct(one.shape, jnp.bfloat16),
        in_specs=[ANYWHERE, ANYWHERE],
        out_specs=ANYWHERE,
        scratch_shapes=[pltpu.VMEM(one.shape, jnp.bfloat16)] * 2 + [pltpu.SemaphoreType.DMA((2,))],
        compiler_params=pltpu.CompilerParams(vmem_limit_bytes=KERNEL_VMEM),
        cost_estimate=pl.CostEstimate(flops=one.size, bytes_accessed=6 * one.size, transcendentals=0),
        name="add",
    )(one, other)


def per_device(stored_rows, kv_weight, lengths, new_place, query, new_kv):
    groups = lax.axis_size("dp")
    planes = lax.axis_size("tensor")
    group_index = lax.axis_index("dp")
    tensor_index = lax.axis_index("tensor")
    core = jnp.bitwise_and(group_index, 1)
    half = jnp.bitwise_and(jnp.right_shift(group_index, 3) + jnp.right_shift(group_index, 1), 1)
    requests = lengths.shape[0]
    columns = kv_weight.shape[2]
    heads_here = columns // HD

    sent = split_rows(stored_rows, groups)
    mine = join_rows(lax.all_to_all(sent, "dp", split_axis=0, concat_axis=0, tiled=True))
    w_own = kv_weight.transpose(1, 0, 2)
    w_next = lax.ppermute(w_own, "dp", [(i, partner(i)) for i in range(groups)])

    slots = jnp.arange(requests, dtype=jnp.int32)
    at_slot = new_place[None, :] == slots[:, None]
    source = jnp.sum(jnp.where(at_slot, slots[None, :], 0), axis=1)
    slot_len = jnp.sum(jnp.where(at_slot, lengths[None, :], 0), axis=1)
    steps = LMAX // 2
    step = jnp.arange(steps, dtype=jnp.int32)
    plane = (source % 2)[:, None] * steps + step[None, :]
    row = plane * groups + (source // 2)[:, None]
    live = (2 * step + half)[None, :] < slot_len[:, None]
    row = jnp.where(live, row, -1).reshape(-1)
    route = (row[:, None] == jnp.arange(planes * groups, dtype=jnp.int32)[None, :]).astype(jnp.bfloat16)

    every = lax.all_gather(mine, "tensor", axis=0, tiled=True)
    where = jnp.stack([core, half]).astype(jnp.int32)
    away = product(False, where, every, w_own, w_next, route)
    received = lax.ppermute(away, "dp", [(i, i ^ 1) for i in range(groups)])
    partial = add(product(True, where, every, w_own, w_next, route), received)

    arrived = lax.all_to_all(
        partial.reshape(groups, REQ_DEV * steps, columns), "dp", split_axis=0, concat_axis=0, tiled=True
    )
    arrived = arrived.reshape(2, 2, 2, 2, CORES, REQ_DEV, steps, columns)
    summed = jnp.sum(arrived, axis=(0, 2), dtype=jnp.float32)
    summed = jnp.stack([summed[0, 0] + summed[1, 1], summed[0, 1] + summed[1, 0]]).astype(jnp.bfloat16)
    kv_cache = summed.transpose(2, 3, 0, 1, 4).reshape(REQ_DEV, LMAX, 2, columns)
    here_len = lax.dynamic_slice_in_dim(slot_len, group_index * REQ_DEV, REQ_DEV)
    slopes = lax.dynamic_slice_in_dim(alibi_slopes(HEADS), tensor_index * heads_here, heads_here)
    attended = attend(kv_cache, query, new_kv, here_len, slopes)
    return (kv_cache, attended)


def solution(mesh):
    placed = (
        P(("dp", "tensor"), None),
        P("dp", None, "tensor"),
        P(),
        P(),
        P("dp", "tensor"),
        P("dp", None, "tensor"),
    )
    return jax.shard_map(
        per_device,
        mesh=mesh,
        in_specs=placed,
        out_specs=(P("dp", None, None, "tensor"), P("dp", "tensor")),
        check_vma=False,
    )
```

time: 124 us -> 95.5 us (0.77)
  waiting for transfers between devices: 45.7 us -> 16.8 us
  Pallas kernels: 6.31 us -> 11.1 us
  other arithmetic: 4.53 us -> 1.42 us
  starting transfers between devices: 24.8 us -> 27.9 us
  local copies, waits for them, and re-layouts: 6.66 us -> 4.19 us
  blocking collectives: 34.3 us -> 32.4 us
    all_to_all x1, waiting for transfers between devices: 30.7 us -> 1.92 us  [per_device(): lax.all_to_all(sent, 'dp', split_axis=0, concat_axis=0, tiled=True)]
    pallas_call x2 -> x4, Pallas kernels: 5.57 us -> 10.4 us  [the longest x2 7.66 us: product(): pl.pallas_call(functools.partial(product_kernel, home), out_shape=jax.Sha...]
    convert_element_type x1 -> x0, other arithmetic: 2.36 us -> none  [per_device(): (home.astype(jnp.float32) + received.astype(jnp.float32)).astype(jnp.bflo...]
    unnamed x20 -> x14, local copies, waits for them, and re-layouts: 5.41 us -> 3.06 us
    all_to_all x1, starting transfers between devices: 8.36 us -> 10.4 us  [per_device(): lax.all_to_all(sent, 'dp', split_axis=0, concat_axis=0, tiled=True)]
    all_gather x1, blocking collectives: 34.3 us -> 32.4 us  [per_device(): every = lax.all_gather(mine, 'tensor', axis=0, tiled=True)]
    all_to_all x1, starting transfers between devices: 3.84 us -> 5.53 us  [per_device(): lax.all_to_all(partial.reshape(groups, REQ_DEV * steps, columns), 'dp', s...]
  transfers between devices with their start and end apart: 4 -> 4, of which waited for: 2 -> 2; matrix products, arithmetic and copies ran while one was open for 2% -> 3% of each run, Pallas kernels for 2% -> 4%
where the time goes in v5:
time: 95.5 us; the launch traced here: 94.9 us
  blocking collectives  32.4 us (34%)
  starting transfers between devices  27.9 us (29%)
  waiting for transfers between devices  16.8 us (18%)
  Pallas kernels  11.1 us (12%)
  local copies, waits for them, and re-layouts  4.19 us (4%)
  other arithmetic  1.42 us (1%)
    all_gather x1, blocking collectives, per_device(): every = lax.all_gather(mine, 'tensor', axis=0, tiled=True)  32.4 us
    all_to_all x1, waiting for transfers between devices, per_device(): lax.all_to_all(partial.reshape(groups, REQ_DEV * steps, columns), 'dp', s...  14.9 us
    all_to_all x1, starting transfers between devices, per_device(): lax.all_to_all(sent, 'dp', split_axis=0, concat_axis=0, tiled=True)  10.4 us
    ppermute x1, starting transfers between devices, per_device(): received = lax.ppermute(away, 'dp', [(i, i ^ 1) for i in range(groups)])  8.7 us
    pallas_call x2, Pallas kernels, product(): pl.pallas_call(functools.partial(product_kernel, home), out_shape=jax.Sha...  7.66 us
    all_to_all x1, starting transfers between devices, per_device(): lax.all_to_all(partial.reshape(groups, REQ_DEV * steps, columns), 'dp', s...  5.53 us
    ppermute x1, starting transfers between devices, per_device(): w_next = lax.ppermute(w_own, 'dp', [(i, partner(i)) for i in range(groups)])  3.3 us
    unnamed x14, local copies, waits for them, and re-layouts  3.06 us
  transfers between devices with their start and end apart: 4, of which 2 were waited for; matrix products, arithmetic and copies ran while one was open for 3% of the time, Pallas kernels for 4%

profile of v5, /device:TPU:1, one launch (start us, length us, event | category | flops | bytes accessed | tf_op | source)
XLA Modules:
  0.0 94.9 jit_solution(7951002401503457260)
XLA Ops:
  0.6 0.0 copy-start
  0.6 0.8 copy-done
  1.4 0.7 split_rows.1
  2.2 10.4 %all-to-all-start = ((bf16[32,2,448]{2,1,0:T(2,128)(2,1)}), bf16[32,2,448]{2,1,0:T(2,128)(2,1)S(1)}, u32[]{:S(2)}, u32[]{:S(2)}) async-start(bf16[32,2,448]{2,1,0:T(2,128)(2,1)} %split_rows.1), calls=%async_computation | async-start | bytes 131072 | tf_op jit(solution)/shard_map/all_to_all | solution.py:200
  12.6 0.0 copy-start.4
  12.6 0.0 copy-start.5
  12.6 1.6 %copy.49 = bf16[448,2,896]{2,0,1:T(8,128)(2,1)S(1)} copy(bf16[448,2,896]{2,1,0:T(2,128)(2,1)} %param.7) | data formatting | bytes 3211264 | tf_op args[1]
  14.2 3.3 %collective-permute-start = (bf16[2,448,896]{2,1,0:T(8,128)(2,1)S(1)}, bf16[2,448,896]{2,1,0:T(8,128)(2,1)}, u32[]{:S(2)}, u32[]{:S(2)}) collective-permute-start(bf16[2,448,896]{2,1,0:T(8,128)(2,1)S(1)} %bitcast.50), channel_id=1, source_target_pairs={{0,128},{16,48},{32,160},{48,16},{64,192},{80,112},{96,224},{112,8... | collective-permute-start | bytes 4816904 | tf_op jit(solution)/shard_map/ppermute | solution.py:202
  17.5 0.0 copy-done.4
  17.6 0.0 copy-done.5
  17.6 0.1 select_reduce_fusion.1
  17.7 0.1 add_select_fusion
  17.8 0.1 select_n.57
  17.9 0.2 fusion.route
  18.1 0.1 pad_add_fusion.where
  18.1 1.9 %all-to-all-done.parts = bf16[32,2,448]{2,1,0:T(2,128)(2,1)S(1)} async-done(((bf16[32,2,448]{2,1,0:T(2,128)(2,1)}), bf16[32,2,448]{2,1,0:T(2,128)(2,1)S(1)}, u32[]{:S(2)}, u32[]{:S(2)}) %all-to-all-start) | async-done | bytes 57376 | tf_op jit(solution)/shard_map/all_to_all | solution.py:200
  20.1 0.2 join_rows.1
  20.2 32.4 %all_gather.3.x = bf16[512,896]{1,0:T(8,128)(2,1)S(1)} all-gather(bf16[32,896]{1,0:T(8,128)(2,1)S(1)} %join_rows.1), channel_id=1, replica_groups=mesh['dp'=32,'tensor'=16] {'tensor'}, dimensions={0}, use_global_device_ids=true | all-gather | bytes 974848 | tf_op jit(solution)/shard_map/all_gather | solution.py:216
  52.6 0.0 collective-permute-done.w_next
  52.6 4.1 %away.1 = bf16[512,896]{1,0:T(8,128)(2,1)} custom-call(s32[2]{0:T(128)S(1)} %pad_add_fusion.where, bf16[512,896]{1,0:T(8,128)(2,1)S(1)} %all_gather.3.x, bf16[2,448,896]{2,1,0:T(8,128)(2,1)S(1)} %bitcast.51, bf16[2,448,896]{2,1,0:T(8,128)(2,1)} %collective-permute-done.w_next, bf16[512,512]{1,0:T(8,128)(2,1)S(1)} %fusion.route), custom_call_target="tpu_custom_call" | custom-call | flops 1291845632 | bytes 3964928 | tf_op jit(solution)/shard_map/away/pallas_call | solution.py:147
  56.7 8.7 %collective-permute-start.1 = (bf16[512,896]{1,0:T(8,128)(2,1)}, bf16[512,896]{1,0:T(8,128)(2,1)}, u32[]{:S(2)}, u32[]{:S(2)}) collective-permute-start(bf16[512,896]{1,0:T(8,128)(2,1)} %away.1), channel_id=1, source_target_pairs={{0,16},{16,0},{32,48},{48,32},{64,80},{80,64},{96,112},{112,96},{1... | collective-permute-start | bytes 2752520 | tf_op jit(solution)/shard_map/ppermute | solution.py:219
  65.4 0.0 copy-done.3
  65.4 3.6 %home.1.one = bf16[512,896]{1,0:T(8,128)(2,1)S(1)} custom-call(s32[2]{0:T(128)S(1)} %pad_add_fusion.where, bf16[512,896]{1,0:T(8,128)(2,1)S(1)} %all_gather.3.x, bf16[2,448,896]{2,1,0:T(8,128)(2,1)S(1)} %bitcast.52, bf16[2,448,896]{2,1,0:T(8,128)(2,1)} %collective-permute-done.w_next, bf16[512,512]{1,0:T(8,128)(2,1)S(1)} %fusion.route), custom_call_target="tpu_custom_call" | custom-call | flops 1291845632 | bytes 3964928 | tf_op jit(solution)/shard_map/home/pallas_call | solution.py:147
  69.0 0.0 collective-permute-done.1.other
  69.0 2.6 %add.173 = bf16[512,896]{1,0:T(8,128)(2,1)} custom-call(bf16[512,896]{1,0:T(8,128)(2,1)S(1)} %home.1.one, bf16[512,896]{1,0:T(8,128)(2,1)} %collective-permute-done.1.other), custom_call_target="tpu_custom_call" | custom-call | flops 458752 | bytes 2752512 | tf_op jit(solution)/shard_map/add/pallas_call | solution.py:176
  71.6 0.0 copy-start.2
  71.6 5.5 %all-to-all-start.1 = ((bf16[32,16,896]{2,1,0:T(8,128)(2,1)}), bf16[32,16,896]{2,1,0:T(8,128)(2,1)S(1)}, u32[]{:S(2)}, u32[]{:S(2)}) async-start(bf16[32,16,896]{2,1,0:T(8,128)(2,1)} %bitcast.3), calls=%async_computation.1 | async-start | bytes 1835008 | tf_op jit(solution)/shard_map/all_to_all | solution.py:222
  77.1 0.0 copy-done.2
  77.3 0.1 fusion.12
  77.3 0.1 copy.24
  77.4 0.1 dynamic_slice.6
  77.5 0.1 dynamic_slice.7
  77.6 0.1 iota_compare_fusion.2
  77.7 0.1 subtract_convert_fusion
  77.8 14.9 %all-to-all-done.1 = bf16[32,16,896]{2,1,0:T(8,128)(2,1)S(1)} async-done(((bf16[32,16,896]{2,1,0:T(8,128)(2,1)}), bf16[32,16,896]{2,1,0:T(8,128)(2,1)S(1)}, u32[]{:S(2)}, u32[]{:S(2)}) %all-to-all-start.1) | async-done | bytes 917536 | tf_op jit(solution)/shard_map/all_to_all | solution.py:222
  92.6 0.1 convert_reduce_fusion
  92.8 0.1 copy.16
  92.9 0.0 copy-start.1
  92.9 0.5 slice_reduce_fusion.1
  93.4 0.1 fusion.8
  93.6 0.2 fusion.28
  93.7 0.2 fusion.17
  93.9 0.1 fusion.18
  94.0 0.1 copy.17
  94.1 0.1 fusion.5
  94.2 0.1 fusion.16
  94.3 0.6 copy.50
  94.9 0.0 copy-done.1
  (14 shorter events, 0.2 us)
Async XLA Ops:
  0.6 0.8 copy-start
  2.2 17.9 %all-to-all-start = ((bf16[32,2,448]{2,1,0:T(2,128)(2,1)}), bf16[32,2,448]{2,1,0:T(2,128)(2,1)S(1)}, u32[]{:S(2)}, u32[]{:S(2)}) async-start(bf16[32,2,448]{2,1,0:T(2,128)(2,1)} %split_rows.1), calls=%async_computation | async-start | bytes 131072 | tf_op jit(solution)/shard_map/all_to_all | solution.py:200
  12.6 5.0 %copy-start.4 = (s32[64]{0:T(128)S(1)}, s32[64]{0:T(128)}, u32[]{:S(2)}) copy-start(s32[64]{0:T(128)} %param.8) | copy-start | bytes 772
  12.6 5.0 %copy-start.5 = (s32[64]{0:T(128)S(1)}, s32[64]{0:T(128)}, u32[]{:S(2)}) copy-start(s32[64]{0:T(128)} %param.9) | copy-start | bytes 772
  14.2 38.3 %collective-permute-start = (bf16[2,448,896]{2,1,0:T(8,128)(2,1)S(1)}, bf16[2,448,896]{2,1,0:T(8,128)(2,1)}, u32[]{:S(2)}, u32[]{:S(2)}) collective-permute-start(bf16[2,448,896]{2,1,0:T(8,128)(2,1)S(1)} %bitcast.50), channel_id=1, source_target_pairs={{0,128},{16,48},{32,160},{48,16},{64,192},{80,112},{96,224},{112,8... | collective-permute-start | bytes 4816904 | tf_op jit(solution)/shard_map/ppermute | solution.py:202
  52.6 12.8 %copy-start.3 = (bf16[2,896]{1,0:T(2,128)(2,1)S(1)}, bf16[2,896]{1,0:T(2,128)(2,1)}, u32[]{:S(2)}) copy-start(bf16[2,896]{1,0:T(2,128)(2,1)} %param.10) | copy-start | bytes 10756
  56.7 12.3 %collective-permute-start.1 = (bf16[512,896]{1,0:T(8,128)(2,1)}, bf16[512,896]{1,0:T(8,128)(2,1)}, u32[]{:S(2)}, u32[]{:S(2)}) collective-permute-start(bf16[512,896]{1,0:T(8,128)(2,1)} %away.1), channel_id=1, source_target_pairs={{0,16},{16,0},{32,48},{48,32},{64,80},{80,64},{96,112},{112,96},{1... | collective-permute-start | bytes 2752520 | tf_op jit(solution)/shard_map/ppermute | solution.py:219
  71.6 5.6 %copy-start.2 = (bf16[2,2,896]{2,1,0:T(2,128)(2,1)S(1)}, bf16[2,2,896]{2,1,0:T(2,128)(2,1)}, u32[]{:S(2)}) copy-start(bf16[2,2,896]{2,1,0:T(2,128)(2,1)} %param.11) | copy-start | bytes 21508
  71.6 21.0 %all-to-all-start.1 = ((bf16[32,16,896]{2,1,0:T(8,128)(2,1)}), bf16[32,16,896]{2,1,0:T(8,128)(2,1)S(1)}, u32[]{:S(2)}, u32[]{:S(2)}) async-start(bf16[32,16,896]{2,1,0:T(8,128)(2,1)} %bitcast.3), calls=%async_computation.1 | async-start | bytes 1835008 | tf_op jit(solution)/shard_map/all_to_all | solution.py:222
  92.9 2.0 %copy-start.1 = (bf16[2,8,2,2,896]{4,3,2,1,0:T(2,128)(2,1)}, bf16[2,8,2,2,896]{4,3,2,1,0:T(2,128)(2,1)S(1)}, u32[]{:S(2)}) copy-start(bf16[2,8,2,2,896]{4,3,2,1,0:T(2,128)(2,1)S(1)} %copy.16) | copy-start | bytes 344068

commit v6 on v5

v6 whole, which is shorter than its diff:
```python
import functools
import math

import jax
import jax.numpy as jnp
from jax import lax
from jax.experimental import pallas as pl
from jax.experimental.pallas import tpu as pltpu
from jax.sharding import PartitionSpec as P

HEADS = 112
HD = 128
REQ_DEV = 2
LMAX = 16


def alibi_slopes(count):
    closest = 2 ** int(math.floor(math.log2(count)))
    counted = jnp.arange(count, dtype=jnp.float32)
    leading = jnp.exp2(-8.0 * (counted + 1.0) / closest)
    trailing = jnp.exp2(-4.0 * (2.0 * (counted - closest) + 1.0) / closest)
    return jnp.where(counted < closest, leading, trailing)


VMEM = pl.BlockSpec(memory_space=pltpu.VMEM)
SMEM = pl.BlockSpec(memory_space=pltpu.SMEM)
ANYWHERE = pl.BlockSpec(memory_space=pl.ANY)
HBM = pl.BlockSpec(memory_space=pltpu.HBM)
KERNEL_VMEM = 24 * 1024 * 1024
SIDE = 4
CORES = 2


def partner(index):
    return index ^ (2 * SIDE if index % CORES == 0 else CORES)


def parity(index):
    return (index // (CORES * SIDE) + index // CORES) % 2


def split_rows_kernel(rows, sent):
    groups, share, block = sent.shape
    for to in range(groups):
        row = parity(to)
        for part, at in enumerate((to, partner(to))):
            sent[to, part : part + 1, :] = rows[row : row + 1, at * block : (at + 1) * block]


def split_rows(rows, groups):
    block = rows.shape[1] // groups
    return pl.pallas_call(
        split_rows_kernel,
        out_shape=jax.ShapeDtypeStruct((groups, 2, block), jnp.bfloat16),
        in_specs=[VMEM],
        out_specs=VMEM,
        compiler_params=pltpu.CompilerParams(vmem_limit_bytes=KERNEL_VMEM),
        name="split_rows",
    )(rows)


def join_rows_kernel(parts, rows):
    block = parts.shape[2]
    rows[:, :block] = parts[:, 0, :]
    rows[:, block:] = parts[:, 1, :]


def join_rows(parts):
    groups, share, block = parts.shape
    return pl.pallas_call(
        join_rows_kernel,
        out_shape=jax.ShapeDtypeStruct((groups, share * block), jnp.bfloat16),
        in_specs=[VMEM],
        out_specs=VMEM,
        compiler_params=pltpu.CompilerParams(vmem_limit_bytes=KERNEL_VMEM),
        cost_estimate=pl.CostEstimate(flops=34500000000, bytes_accessed=0, transcendentals=0),
        name="join_rows",
    )(parts)


def fetch(moves, sems):
    copies = [pltpu.make_async_copy(source, to, sems.at[at]) for at, (source, to) in enumerate(moves)]
    for copy in copies:
        copy.start()
    return copies


def finish(copies):
    for copy in copies:
        copy.wait()


def product_kernel(home, where, x, w_own, w_next, out):
    column = where[0] if home else 1 - where[0]
    block = w_own.shape[1]
    total = jnp.dot(x[:, :block], w_own[column], preferred_element_type=jnp.float32)
    total += jnp.dot(x[:, block:], w_next[column], preferred_element_type=jnp.float32)
    out[...] = total.astype(jnp.bfloat16)


def product(home, where, x, w_own, w_next):
    rows, depth = x.shape
    columns = w_own.shape[2]
    return pl.pallas_call(
        functools.partial(product_kernel, home),
        out_shape=jax.ShapeDtypeStruct((rows, columns), jnp.bfloat16),
        in_specs=[SMEM, VMEM, VMEM, VMEM],
        out_specs=VMEM,
        compiler_params=pltpu.CompilerParams(vmem_limit_bytes=KERNEL_VMEM),
        cost_estimate=pl.CostEstimate(
            flops=2 * rows * depth * columns,
            bytes_accessed=2 * (rows * depth + depth * columns + rows * columns),
            transcendentals=0,
        ),
        name="home" if home else "away",
    )(where, x, w_own, w_next)


def add_kernel(one, other, route, total, rs, made, sems):
    finish(fetch([(route, rs)], sems))
    both = (one[...].astype(jnp.float32) + other[...].astype(jnp.float32)).astype(jnp.bfloat16)
    made[...] = jnp.dot(rs[...], both, preferred_element_type=jnp.float32).astype(jnp.bfloat16)
    finish(fetch([(made, total)], sems.at[pl.ds(1, 1)]))


def add(one, other, route):
    return pl.pallas_call(
        add_kernel,
        out_shape=jax.ShapeDtypeStruct(one.shape, jnp.bfloat16),
        in_specs=[VMEM, VMEM, HBM],
        out_specs=ANYWHERE,
        scratch_shapes=[
            pltpu.VMEM(route.shape, jnp.bfloat16),
            pltpu.VMEM(one.shape, jnp.bfloat16),
            pltpu.SemaphoreType.DMA((2,)),
        ],
        compiler_params=pltpu.CompilerParams(vmem_limit_bytes=KERNEL_VMEM),
        cost_estimate=pl.CostEstimate(
            flops=2 * one.size * route.shape[0], bytes_accessed=6 * one.size + 2 * route.size, transcendentals=0
        ),
        name="add",
    )(one, other, route)


def attend_kernel(lens, slopes, cache, query, new_kv, result, out):
    del result
    slots, columns = query.shape
    heads = columns // HD
    steps = cache.shape[3]
    factor = 1.0 / math.sqrt(HD)
    head_lane = lax.broadcasted_iota(jnp.int32, (steps, HD), 1)
    slope = jnp.zeros((steps, HD), jnp.float32)
    for head in range(heads):
        slope = jnp.where(head_lane == head, slopes[head], slope)
    for slot in range(slots):
        asked = query[slot : slot + 1, :].astype(jnp.float32)
        own_value = new_kv[slot, 1:2, :].astype(jnp.float32)

        def by_head(rows):
            products = rows * asked
            scores = jnp.zeros((rows.shape[0], HD), jnp.float32)
            for head in range(heads):
                total = jnp.sum(products[:, head * HD : (head + 1) * HD], axis=1, keepdims=True)
                scores = jnp.where(head_lane[: rows.shape[0]] == head, total, scores)
            return scores * factor

        own = by_head(new_kv[slot, 0:1, :].astype(jnp.float32))
        scores = []
        for half in range(2):
            place = 2 * lax.broadcasted_iota(jnp.int32, (steps, HD), 0) + half
            distance = (lens[slot] - place).astype(jnp.float32)
            found = by_head(cache[half, 0, slot].astype(jnp.float32)) - slope * distance
            scores.append(jnp.where(place < lens[slot], found, -jnp.inf))
        top = jnp.maximum(jnp.max(jnp.maximum(scores[0], scores[1]), axis=0, keepdims=True), own)
        raised = [jnp.exp(score - top) for score in scores]
        own_raised = jnp.exp(own - top)
        total = jnp.sum(raised[0] + raised[1], axis=0, keepdims=True) + own_raised
        weights = [(part / total).astype(jnp.bfloat16).astype(jnp.float32) for part in raised]
        own_weight = (own_raised / total).astype(jnp.bfloat16).astype(jnp.float32)
        for head in range(heads):
            lanes = slice(head * HD, (head + 1) * HD)
            mixed = jnp.zeros((steps, HD), jnp.float32)
            for half in range(2):
                values = cache[half, 1, slot, :, lanes].astype(jnp.float32)
                mixed += weights[half][:, head : head + 1] * values
            mixed = jnp.sum(mixed, axis=0, keepdims=True) + own_weight[:, head : head + 1] * own_value[:, lanes]
            out[slot : slot + 1, lanes] = mixed.astype(jnp.bfloat16)


def attend(lens, slopes, cache, query, new_kv, result):
    return pl.pallas_call(
        attend_kernel,
        out_shape=jax.ShapeDtypeStruct(query.shape, jnp.bfloat16),
        in_specs=[SMEM, SMEM, VMEM, VMEM, VMEM, VMEM],
        out_specs=VMEM,
        compiler_params=pltpu.CompilerParams(vmem_limit_bytes=KERNEL_VMEM),
        cost_estimate=pl.CostEstimate(flops=8 * cache.size, bytes_accessed=2 * cache.size, transcendentals=cache.size // HD),
        name="attend",
    )(lens, slopes, cache, query, new_kv, result)


def per_device(stored_rows, kv_weight, lengths, new_place, query, new_kv):
    groups = lax.axis_size("dp")
    planes = lax.axis_size("tensor")
    group_index = lax.axis_index("dp")
    tensor_index = lax.axis_index("tensor")
    core = jnp.bitwise_and(group_index, 1)
    half = jnp.bitwise_and(jnp.right_shift(group_index, 3) + jnp.right_shift(group_index, 1), 1)
    requests = lengths.shape[0]
    columns = kv_weight.shape[2]
    heads_here = columns // HD

    sent = split_rows(stored_rows, groups)
    mine = join_rows(lax.all_to_all(sent, "dp", split_axis=0, concat_axis=0, tiled=True))
    w_own = kv_weight.transpose(1, 0, 2)
    w_next = lax.ppermute(w_own, "dp", [(i, partner(i)) for i in range(groups)])

    slots = jnp.arange(requests, dtype=jnp.int32)
    at_slot = new_place[None, :] == slots[:, None]
    source = jnp.sum(jnp.where(at_slot, slots[None, :], 0), axis=1)
    slot_len = jnp.sum(jnp.where(at_slot, lengths[None, :], 0), axis=1)
    steps = LMAX // 2
    step = jnp.arange(steps, dtype=jnp.int32)
    plane = (source % 2)[:, None] * steps + step[None, :]
    row = plane * groups + (source // 2)[:, None]
    live = (2 * step + half)[None, :] < slot_len[:, None]
    row = jnp.where(live, row, -1).reshape(-1)
    route = (row[:, None] == jnp.arange(planes * groups, dtype=jnp.int32)[None, :]).astype(jnp.bfloat16)

    every = lax.all_gather(mine, "tensor", axis=0, tiled=True)
    where = core.reshape(1).astype(jnp.int32)
    away = product(False, where, every, w_own, w_next)
    received = lax.ppermute(away, "dp", [(i, i ^ 1) for i in range(groups)])
    partial = add(product(True, where, every, w_own, w_next), received, route)

    arrived = lax.all_to_all(
        partial.reshape(groups, REQ_DEV * steps, columns), "dp", split_axis=0, concat_axis=0, tiled=True
    )
    arrived = arrived.reshape(2, 2, 2, 2, CORES, REQ_DEV, steps, columns)
    summed = jnp.sum(arrived, axis=(0, 2), dtype=jnp.float32)
    summed = jnp.stack([summed[0, 0] + summed[1, 1], summed[0, 1] + summed[1, 0]]).astype(jnp.bfloat16)
    kv_cache = summed.transpose(2, 3, 0, 1, 4).reshape(REQ_DEV, LMAX, 2, columns)
    here_len = lax.dynamic_slice_in_dim(slot_len, group_index * REQ_DEV, REQ_DEV)
    slopes = lax.dynamic_slice_in_dim(alibi_slopes(HEADS), tensor_index * heads_here, heads_here)
    return (kv_cache, attend(here_len, slopes, summed, query, new_kv, kv_cache))


def solution(mesh):
    placed = (
        P(("dp", "tensor"), None),
        P("dp", None, "tensor"),
        P(),
        P(),
        P("dp", "tensor"),
        P("dp", None, "tensor"),
    )
    return jax.shard_map(
        per_device,
        mesh=mesh,
        in_specs=placed,
        out_specs=(P("dp", None, None, "tensor"), P("dp", "tensor")),
        check_vma=False,
    )
```

time: 95.5 us -> 92.6 us (0.970)
  local copies, waits for them, and re-layouts: 4.19 us -> 2.78 us
  waiting for transfers between devices: 16.8 us -> 17.8 us
    pallas_call x0 -> x1, Pallas kernels: none -> 1.44 us  [attend(): pl.pallas_call(attend_kernel, out_shape=jax.ShapeDtypeStruct(query.shape,...]
    pallas_call x2, Pallas kernels: 7.66 us -> 6.38 us  [product(): pl.pallas_call(functools.partial(product_kernel, home), out_shape=jax.Sha...]
    unnamed x14 -> x13, local copies, waits for them, and re-layouts: 3.06 us -> 2.45 us
  transfers between devices with their start and end apart: 4 -> 4, of which waited for: 2 -> 2; matrix products, arithmetic and copies ran while one was open for 3% -> 2% of each run, Pallas kernels for 4% -> 3%
where the time goes in v6:
time: 92.6 us; the launch traced here: 92.1 us
  blocking collectives  32.4 us (35%)
  starting transfers between devices  27.3 us (29%)
  waiting for transfers between devices  17.8 us (19%)
  Pallas kernels  10.5 us (11%)
  local copies, waits for them, and re-layouts  2.78 us (3%)
    all_gather x1, blocking collectives, per_device(): every = lax.all_gather(mine, 'tensor', axis=0, tiled=True)  32.4 us
    all_to_all x1, waiting for transfers between devices, per_device(): lax.all_to_all(partial.reshape(groups, REQ_DEV * steps, columns), 'dp', s...  15.3 us
    all_to_all x1, starting transfers between devices, per_device(): lax.all_to_all(sent, 'dp', split_axis=0, concat_axis=0, tiled=True)  10.4 us
    ppermute x1, starting transfers between devices, per_device(): received = lax.ppermute(away, 'dp', [(i, i ^ 1) for i in range(groups)])  8.68 us
    pallas_call x2, Pallas kernels, product(): pl.pallas_call(functools.partial(product_kernel, home), out_shape=jax.Sha...  6.38 us
    all_to_all x1, starting transfers between devices, per_device(): lax.all_to_all(partial.reshape(groups, REQ_DEV * steps, columns), 'dp', s...  4.91 us
    ppermute x1, starting transfers between devices, per_device(): w_next = lax.ppermute(w_own, 'dp', [(i, partner(i)) for i in range(groups)])  3.3 us
    all_to_all x1, waiting for transfers between devices, per_device(): lax.all_to_all(sent, 'dp', split_axis=0, concat_axis=0, tiled=True)  2.55 us
  transfers between devices with their start and end apart: 4, of which 2 were waited for; matrix products, arithmetic and copies ran while one was open for 2% of the time, Pallas kernels for 3%

profile of v6, /device:TPU:1, one launch (start us, length us, event | category | flops | bytes accessed | tf_op | source)
XLA Modules:
  0.0 92.1 jit_solution(11774849988581413365)
XLA Ops:
  0.6 0.0 copy-start.1
  0.6 0.8 copy-done.1
  1.4 0.7 split_rows.1
  2.2 10.4 %all-to-all-start = ((bf16[32,2,448]{2,1,0:T(2,128)(2,1)}), bf16[32,2,448]{2,1,0:T(2,128)(2,1)S(1)}, u32[]{:S(2)}, u32[]{:S(2)}) async-start(bf16[32,2,448]{2,1,0:T(2,128)(2,1)} %split_rows.1), calls=%async_computation | async-start | bytes 131072 | tf_op jit(solution)/shard_map/all_to_all | solution.py:214
  12.6 1.6 %copy.15 = bf16[448,2,896]{2,0,1:T(8,128)(2,1)S(1)} copy(bf16[448,2,896]{2,1,0:T(2,128)(2,1)} %param.7) | data formatting | bytes 3211264 | tf_op args[1]
  14.2 3.3 %collective-permute-start = (bf16[2,448,896]{2,1,0:T(8,128)(2,1)S(1)}, bf16[2,448,896]{2,1,0:T(8,128)(2,1)}, u32[]{:S(2)}, u32[]{:S(2)}) collective-permute-start(bf16[2,448,896]{2,1,0:T(8,128)(2,1)S(1)} %bitcast.14), channel_id=1, source_target_pairs={{0,128},{16,48},{32,160},{48,16},{64,192},{80,112},{96,224},{112,8... | collective-permute-start | bytes 4816904 | tf_op jit(solution)/shard_map/ppermute | solution.py:216
  17.5 2.5 %all-to-all-done.parts = bf16[32,2,448]{2,1,0:T(2,128)(2,1)S(1)} async-done(((bf16[32,2,448]{2,1,0:T(2,128)(2,1)}), bf16[32,2,448]{2,1,0:T(2,128)(2,1)S(1)}, u32[]{:S(2)}, u32[]{:S(2)}) %all-to-all-start) | async-done | bytes 57376 | tf_op jit(solution)/shard_map/all_to_all | solution.py:214
  20.1 0.2 join_rows.1
  20.2 32.4 %all_gather.3.x = bf16[512,896]{1,0:T(8,128)(2,1)S(1)} all-gather(bf16[32,896]{1,0:T(8,128)(2,1)S(1)} %join_rows.1), channel_id=1, replica_groups=mesh['dp'=32,'tensor'=16] {'tensor'}, dimensions={0}, use_global_device_ids=true | all-gather | bytes 974848 | tf_op jit(solution)/shard_map/all_gather | solution.py:230
  52.6 0.0 collective-permute-done.w_next
  52.6 0.0 copy-start.4
  52.6 0.0 copy-start.5
  52.6 3.7 %away.1 = bf16[512,896]{1,0:T(8,128)(2,1)} custom-call(s32[1]{0:T(128)} %bitcast.where, bf16[512,896]{1,0:T(8,128)(2,1)S(1)} %all_gather.3.x, bf16[2,448,896]{2,1,0:T(8,128)(2,1)S(1)} %bitcast.15, bf16[2,448,896]{2,1,0:T(8,128)(2,1)} %collective-permute-done.w_next), custom_call_target="tpu_custom_call" | custom-call | flops 822083584 | bytes 3440640 | tf_op jit(solution)/shard_map/away/pallas_call | solution.py:104
  56.2 8.7 %collective-permute-start.1 = (bf16[512,896]{1,0:T(8,128)(2,1)}, bf16[512,896]{1,0:T(8,128)(2,1)S(1)}, u32[]{:S(2)}, u32[]{:S(2)}) collective-permute-start(bf16[512,896]{1,0:T(8,128)(2,1)} %away.1), channel_id=1, source_target_pairs={{0,16},{16,0},{32,48},{48,32},{64,80},{80,64},{96,112},{112,96},{1... | collective-permute-start | bytes 2752520 | tf_op jit(solution)/shard_map/ppermute | solution.py:233
  64.9 0.0 copy-done.4
  65.0 0.0 copy-done.5
  65.0 0.1 select_reduce_fusion.1
  65.1 0.1 add_select_fusion
  65.2 0.1 select_n.53
  65.3 0.2 fusion.route
  65.5 2.7 %home.1.one = bf16[512,896]{1,0:T(8,128)(2,1)S(1)} custom-call(s32[1]{0:T(128)} %bitcast.where, bf16[512,896]{1,0:T(8,128)(2,1)S(1)} %all_gather.3.x, bf16[2,448,896]{2,1,0:T(8,128)(2,1)S(1)} %bitcast.16, bf16[2,448,896]{2,1,0:T(8,128)(2,1)} %collective-permute-done.w_next), custom_call_target="tpu_custom_call" | custom-call | flops 822083584 | bytes 3440640 | tf_op jit(solution)/shard_map/home/pallas_call | solution.py:104
  68.2 0.0 collective-permute-done.1.other
  68.2 1.8 %add.150 = bf16[512,896]{1,0:T(8,128)(2,1)} custom-call(bf16[512,896]{1,0:T(8,128)(2,1)S(1)} %home.1.one, bf16[512,896]{1,0:T(8,128)(2,1)S(1)} %collective-permute-done.1.other, bf16[512,512]{1,0:T(8,128)(2,1)S(1)} %fusion.route), custom_call_target="tpu_custom_call" | custom-call | flops 469762048 | bytes 3276800 | tf_op jit(solution)/shard_map/add/pallas_call | solution.py:127
  70.0 4.9 %all-to-all-start.1 = ((bf16[32,16,896]{2,1,0:T(8,128)(2,1)}), bf16[32,16,896]{2,1,0:T(8,128)(2,1)S(1)}, u32[]{:S(2)}, u32[]{:S(2)}) async-start(bf16[32,16,896]{2,1,0:T(8,128)(2,1)} %bitcast.2), calls=%async_computation.1 | async-start | bytes 1835008 | tf_op jit(solution)/shard_map/all_to_all | solution.py:236
  74.9 0.0 copy-start.2
  74.9 0.0 copy-start.3
  74.9 0.1 dynamic_slice.6.lens
  75.0 0.1 dynamic_slice.7.slopes
  75.1 15.3 %all-to-all-done.1 = bf16[32,16,896]{2,1,0:T(8,128)(2,1)S(1)} async-done(((bf16[32,16,896]{2,1,0:T(8,128)(2,1)}), bf16[32,16,896]{2,1,0:T(8,128)(2,1)S(1)}, u32[]{:S(2)}, u32[]{:S(2)}) %all-to-all-start.1) | async-done | bytes 917536 | tf_op jit(solution)/shard_map/all_to_all | solution.py:236
  90.3 0.1 convert_reduce_fusion
  90.5 0.1 copy.13
  90.6 0.0 copy-start
  90.6 0.0 copy-done.2
  90.7 0.0 copy-done.3
  90.7 1.4 %attend.1 = bf16[2,896]{1,0:T(2,128)(2,1)} custom-call(s32[2]{0:T(128)S(1)} %dynamic_slice.6.lens, f32[7]{0:T(128)S(1)} %dynamic_slice.7.slopes, bf16[2,2,2,8,896]{4,3,2,1,0:T(8,128)(2,1)S(1)} %get-tuple-element.6.cache, bf16[2,896]{1,0:T(2,128)(2,1)S(1)} %copy-done.3, bf16[2,2,896]{2,1,0:T(2,128)(2,1)S(1)} %copy-done.2, bf16[2,16,2,896]{3,2,1,0:T(2,128)(2,1)S(1)} %bitcast.17), custom_call_target="tpu_custom_call" | custom-call | flops 458752 | bytes 114688 | tf_op jit(solution)/shard_map/attend/pallas_call | solution.py:191
  92.1 0.0 copy-done
  (5 shorter events, 0.1 us)
Async XLA Ops:
  0.6 0.8 copy-start.1
  2.2 17.9 %all-to-all-start = ((bf16[32,2,448]{2,1,0:T(2,128)(2,1)}), bf16[32,2,448]{2,1,0:T(2,128)(2,1)S(1)}, u32[]{:S(2)}, u32[]{:S(2)}) async-start(bf16[32,2,448]{2,1,0:T(2,128)(2,1)} %split_rows.1), calls=%async_computation | async-start | bytes 131072 | tf_op jit(solution)/shard_map/all_to_all | solution.py:214
  14.2 38.4 %collective-permute-start = (bf16[2,448,896]{2,1,0:T(8,128)(2,1)S(1)}, bf16[2,448,896]{2,1,0:T(8,128)(2,1)}, u32[]{:S(2)}, u32[]{:S(2)}) collective-permute-start(bf16[2,448,896]{2,1,0:T(8,128)(2,1)S(1)} %bitcast.14), channel_id=1, source_target_pairs={{0,128},{16,48},{32,160},{48,16},{64,192},{80,112},{96,224},{112,8... | collective-permute-start | bytes 4816904 | tf_op jit(solution)/shard_map/ppermute | solution.py:216
  52.6 12.4 %copy-start.4 = (s32[64]{0:T(128)S(1)}, s32[64]{0:T(128)}, u32[]{:S(2)}) copy-start(s32[64]{0:T(128)} %param.8) | copy-start | bytes 772
  52.6 12.4 %copy-start.5 = (s32[64]{0:T(128)S(1)}, s32[64]{0:T(128)}, u32[]{:S(2)}) copy-start(s32[64]{0:T(128)} %param.9) | copy-start | bytes 772
  56.2 11.9 %collective-permute-start.1 = (bf16[512,896]{1,0:T(8,128)(2,1)}, bf16[512,896]{1,0:T(8,128)(2,1)S(1)}, u32[]{:S(2)}, u32[]{:S(2)}) collective-permute-start(bf16[512,896]{1,0:T(8,128)(2,1)} %away.1), channel_id=1, source_target_pairs={{0,16},{16,0},{32,48},{48,32},{64,80},{80,64},{96,112},{112,96},{1... | collective-permute-start | bytes 2752520 | tf_op jit(solution)/shard_map/ppermute | solution.py:233
  70.0 20.4 %all-to-all-start.1 = ((bf16[32,16,896]{2,1,0:T(8,128)(2,1)}), bf16[32,16,896]{2,1,0:T(8,128)(2,1)S(1)}, u32[]{:S(2)}, u32[]{:S(2)}) async-start(bf16[32,16,896]{2,1,0:T(8,128)(2,1)} %bitcast.2), calls=%async_computation.1 | async-start | bytes 1835008 | tf_op jit(solution)/shard_map/all_to_all | solution.py:236
  74.9 15.8 %copy-start.2 = (bf16[2,2,896]{2,1,0:T(2,128)(2,1)S(1)}, bf16[2,2,896]{2,1,0:T(2,128)(2,1)}, u32[]{:S(2)}) copy-start(bf16[2,2,896]{2,1,0:T(2,128)(2,1)} %new_kv.1) | copy-start | bytes 21508
  74.9 15.8 %copy-start.3 = (bf16[2,896]{1,0:T(2,128)(2,1)S(1)}, bf16[2,896]{1,0:T(2,128)(2,1)}, u32[]{:S(2)}) copy-start(bf16[2,896]{1,0:T(2,128)(2,1)} %query.1) | copy-start | bytes 10756
  90.6 1.5 %copy-start = (bf16[2,8,2,2,896]{4,3,2,1,0:T(2,128)(2,1)}, bf16[2,8,2,2,896]{4,3,2,1,0:T(2,128)(2,1)S(1)}, u32[]{:S(2)}) copy-start(bf16[2,8,2,2,896]{4,3,2,1,0:T(2,128)(2,1)S(1)} %copy.13) | copy-start | bytes 344068

commit v7 on v6

--- a/solution.py
+++ b/solution.py
@@ -59,23 +59,24 @@
     )(rows)
 
 
-def join_rows_kernel(parts, rows):
+def join_rows_kernel(parts, row, rows):
+    del row
     block = parts.shape[2]
     rows[:, :block] = parts[:, 0, :]
     rows[:, block:] = parts[:, 1, :]
 
 
-def join_rows(parts):
+def join_rows(parts, row):
     groups, share, block = parts.shape
     return pl.pallas_call(
         join_rows_kernel,
         out_shape=jax.ShapeDtypeStruct((groups, share * block), jnp.bfloat16),
-        in_specs=[VMEM],
+        in_specs=[VMEM, HBM],
         out_specs=VMEM,
         compiler_params=pltpu.CompilerParams(vmem_limit_bytes=KERNEL_VMEM),
         cost_estimate=pl.CostEstimate(flops=34500000000, bytes_accessed=0, transcendentals=0),
         name="join_rows",
-    )(parts)
+    )(parts, row)
 
 
 def fetch(moves, sems):
@@ -90,11 +91,13 @@
         copy.wait()
 
 
-def product_kernel(home, where, x, w_own, w_next, out):
+def product_kernel(home, where, x, w_own, w_next, out, held, sems):
     column = where[0] if home else 1 - where[0]
     block = w_own.shape[1]
+    copies = fetch([(w_next.at[column], held)], sems)
     total = jnp.dot(x[:, :block], w_own[column], preferred_element_type=jnp.float32)
-    total += jnp.dot(x[:, block:], w_next[column], preferred_element_type=jnp.float32)
+    finish(copies)
+    total += jnp.dot(x[:, block:], held[...], preferred_element_type=jnp.float32)
     out[...] = total.astype(jnp.bfloat16)
 
 
@@ -104,8 +107,9 @@
     return pl.pallas_call(
         functools.partial(product_kernel, home),
         out_shape=jax.ShapeDtypeStruct((rows, columns), jnp.bfloat16),
-        in_specs=[SMEM, VMEM, VMEM, VMEM],
-        out_specs=VMEM,
+        in_specs=[SMEM, VMEM, VMEM, ANYWHERE],
+        out_specs=VMEM,
+        scratch_shapes=[pltpu.VMEM(w_next.shape[1:], jnp.bfloat16), pltpu.SemaphoreType.DMA((1,))],
         compiler_params=pltpu.CompilerParams(vmem_limit_bytes=KERNEL_VMEM),
         cost_estimate=pl.CostEstimate(
             flops=2 * rows * depth * columns,
@@ -116,24 +120,17 @@
     )(where, x, w_own, w_next)
 
 
-def add_kernel(one, other, route, total, rs, made, sems):
-    finish(fetch([(route, rs)], sems))
+def add_kernel(one, other, route, total):
     both = (one[...].astype(jnp.float32) + other[...].astype(jnp.float32)).astype(jnp.bfloat16)
-    made[...] = jnp.dot(rs[...], both, preferred_element_type=jnp.float32).astype(jnp.bfloat16)
-    finish(fetch([(made, total)], sems.at[pl.ds(1, 1)]))
+    total[...] = jnp.dot(route[...], both, preferred_element_type=jnp.float32).astype(jnp.bfloat16)
 
 
 def add(one, other, route):
     return pl.pallas_call(
         add_kernel,
         out_shape=jax.ShapeDtypeStruct(one.shape, jnp.bfloat16),
-        in_specs=[VMEM, VMEM, HBM],
-        out_specs=ANYWHERE,
-        scratch_shapes=[
-            pltpu.VMEM(route.shape, jnp.bfloat16),
-            pltpu.VMEM(one.shape, jnp.bfloat16),
-            pltpu.SemaphoreType.DMA((2,)),
-        ],
+        in_specs=[VMEM, VMEM, VMEM],
+        out_specs=VMEM,
         compiler_params=pltpu.CompilerParams(vmem_limit_bytes=KERNEL_VMEM),
         cost_estimate=pl.CostEstimate(
             flops=2 * one.size * route.shape[0], bytes_accessed=6 * one.size + 2 * route.size, transcendentals=0
@@ -211,7 +208,7 @@
     heads_here = columns // HD
 
     sent = split_rows(stored_rows, groups)
-    mine = join_rows(lax.all_to_all(sent, "dp", split_axis=0, concat_axis=0, tiled=True))
+    parts = lax.all_to_all(sent, "dp", split_axis=0, concat_axis=0, tiled=True)
     w_own = kv_weight.transpose(1, 0, 2)
     w_next = lax.ppermute(w_own, "dp", [(i, partner(i)) for i in range(groups)])
 
@@ -227,7 +224,7 @@
     row = jnp.where(live, row, -1).reshape(-1)
     route = (row[:, None] == jnp.arange(planes * groups, dtype=jnp.int32)[None, :]).astype(jnp.bfloat16)
 
-    every = lax.all_gather(mine, "tensor", axis=0, tiled=True)
+    every = lax.all_gather(join_rows(parts, row), "tensor", axis=0, tiled=True)
     where = core.reshape(1).astype(jnp.int32)
     away = product(False, where, every, w_own, w_next)
     received = lax.ppermute(away, "dp", [(i, i ^ 1) for i in range(groups)])

time: 92.6 us -> 89.7 us (0.969)
  Pallas kernels: 10.5 us -> 6.98 us
    pallas_call x2, Pallas kernels: 6.38 us -> 2.95 us  [product(): pl.pallas_call(functools.partial(product_kernel, home), out_shape=jax.Sha...]
  transfers between devices with their start and end apart: 4 -> 4, of which waited for: 2 -> 3; matrix products, arithmetic and copies ran while one was open for 2% -> 3% of each run, Pallas kernels for 3% -> 2%
where the time goes in v7:
time: 89.7 us; the launch traced here: 89.3 us
  blocking collectives  32.4 us (36%)
  starting transfers between devices  27.9 us (31%)
  waiting for transfers between devices  17.9 us (20%)
  Pallas kernels  6.98 us (8%)
  local copies, waits for them, and re-layouts  2.8 us (3%)
    all_gather x1, blocking collectives, per_device(): every = lax.all_gather(join_rows(parts, row), 'tensor', axis=0, tiled=True)  32.4 us
    all_to_all x1, waiting for transfers between devices, per_device(): lax.all_to_all(partial.reshape(groups, REQ_DEV * steps, columns), 'dp', s...  15.3 us
    all_to_all x1, starting transfers between devices, per_device(): parts = lax.all_to_all(sent, 'dp', split_axis=0, concat_axis=0, tiled=True)  10.4 us
    ppermute x1, starting transfers between devices, per_device(): received = lax.ppermute(away, 'dp', [(i, i ^ 1) for i in range(groups)])  8.69 us
    all_to_all x1, starting transfers between devices, per_device(): lax.all_to_all(partial.reshape(groups, REQ_DEV * steps, columns), 'dp', s...  5.54 us
    ppermute x1, starting transfers between devices, per_device(): w_next = lax.ppermute(w_own, 'dp', [(i, partner(i)) for i in range(groups)])  3.3 us
    pallas_call x2, Pallas kernels, product(): pl.pallas_call(functools.partial(product_kernel, home), out_shape=jax.Sha...  2.95 us
    unnamed x13, local copies, waits for them, and re-layouts  2.46 us
  transfers between devices with their start and end apart: 4, of which 3 were waited for; matrix products, arithmetic and copies ran while one was open for 3% of the time, Pallas kernels for 2%

profile of v7, /device:TPU:1, one launch (start us, length us, event | category | flops | bytes accessed | tf_op | source)
XLA Modules:
  0.0 89.3 jit_solution(7515102102633727601)
XLA Ops:
  0.6 0.0 copy-start.1
  0.6 0.8 copy-done.1
  1.4 0.7 split_rows.1
  2.2 10.4 %all-to-all-start = ((bf16[32,2,448]{2,1,0:T(2,128)(2,1)}), bf16[32,2,448]{2,1,0:T(2,128)(2,1)S(1)}, u32[]{:S(2)}, u32[]{:S(2)}) async-start(bf16[32,2,448]{2,1,0:T(2,128)(2,1)} %split_rows.1), calls=%async_computation | async-start | bytes 131072 | tf_op jit(solution)/shard_map/all_to_all | solution.py:211
  12.6 0.0 copy-start.4
  12.6 0.0 copy-start.5
  12.6 1.6 %copy.15 = bf16[448,2,896]{2,0,1:T(8,128)(2,1)S(1)} copy(bf16[448,2,896]{2,1,0:T(2,128)(2,1)} %param.7) | data formatting | bytes 3211264 | tf_op args[1]
  14.2 3.3 %collective-permute-start = (bf16[2,448,896]{2,1,0:T(8,128)(2,1)S(1)}, bf16[2,448,896]{2,1,0:T(8,128)(2,1)S(1)}, u32[]{:S(2)}, u32[]{:S(2)}) collective-permute-start(bf16[2,448,896]{2,1,0:T(8,128)(2,1)S(1)} %bitcast.14), channel_id=1, source_target_pairs={{0,128},{16,48},{32,160},{48,16},{64,192},{80,112},{96,224},{112,8... | collective-permute-start | bytes 4816904 | tf_op jit(solution)/shard_map/ppermute | solution.py:213
  17.5 0.0 copy-done.4
  17.5 0.0 copy-done.5
  17.6 0.1 select_reduce_fusion.1
  17.7 0.1 add_select_fusion
  17.8 0.1 select_n.54.row
  17.9 2.2 %all-to-all-done.parts = bf16[32,2,448]{2,1,0:T(2,128)(2,1)S(1)} async-done(((bf16[32,2,448]{2,1,0:T(2,128)(2,1)}), bf16[32,2,448]{2,1,0:T(2,128)(2,1)S(1)}, u32[]{:S(2)}, u32[]{:S(2)}) %all-to-all-start) | async-done | bytes 57376 | tf_op jit(solution)/shard_map/all_to_all | solution.py:211
  20.1 0.2 join_rows.1
  20.2 32.4 %all_gather.3.x = bf16[512,896]{1,0:T(8,128)(2,1)S(1)} all-gather(bf16[32,896]{1,0:T(8,128)(2,1)S(1)} %join_rows.1), channel_id=1, replica_groups=mesh['dp'=32,'tensor'=16] {'tensor'}, dimensions={0}, use_global_device_ids=true | all-gather | bytes 974848 | tf_op jit(solution)/shard_map/all_gather | solution.py:227
  52.6 0.0 collective-permute-done.w_next
  52.6 1.5 %away.1 = bf16[512,896]{1,0:T(8,128)(2,1)S(1)} custom-call(s32[1]{0:T(128)} %bitcast.where, bf16[512,896]{1,0:T(8,128)(2,1)S(1)} %all_gather.3.x, bf16[2,448,896]{2,1,0:T(8,128)(2,1)S(1)} %bitcast.15, bf16[2,448,896]{2,1,0:T(8,128)(2,1)S(1)} %collective-permute-done.w_next), custom_call_target="tpu_custom_call" | custom-call | flops 822083584 | bytes 3440640 | tf_op jit(solution)/shard_map/away/pallas_call | solution.py:107
  54.0 8.7 %collective-permute-start.1 = (bf16[512,896]{1,0:T(8,128)(2,1)S(1)}, bf16[512,896]{1,0:T(8,128)(2,1)S(1)}, u32[]{:S(2)}, u32[]{:S(2)}) collective-permute-start(bf16[512,896]{1,0:T(8,128)(2,1)S(1)} %away.1), channel_id=1, source_target_pairs={{0,16},{16,0},{32,48},{48,32},{64,80},{80,64},{96,112},{112,96},{1... | collective-permute-start | bytes 2752520 | tf_op jit(solution)/shard_map/ppermute | solution.py:230
  62.8 0.2 fusion.route
  62.9 1.5 %home.1.one = bf16[512,896]{1,0:T(8,128)(2,1)S(1)} custom-call(s32[1]{0:T(128)} %bitcast.where, bf16[512,896]{1,0:T(8,128)(2,1)S(1)} %all_gather.3.x, bf16[2,448,896]{2,1,0:T(8,128)(2,1)S(1)} %bitcast.16, bf16[2,448,896]{2,1,0:T(8,128)(2,1)S(1)} %collective-permute-done.w_next), custom_call_target="tpu_custom_call" | custom-call | flops 822083584 | bytes 3440640 | tf_op jit(solution)/shard_map/home/pallas_call | solution.py:107
  64.4 0.4 collective-permute-done.1.other
  64.8 1.7 %add.152 = bf16[512,896]{1,0:T(8,128)(2,1)} custom-call(bf16[512,896]{1,0:T(8,128)(2,1)S(1)} %home.1.one, bf16[512,896]{1,0:T(8,128)(2,1)S(1)} %collective-permute-done.1.other, bf16[512,512]{1,0:T(8,128)(2,1)S(1)} %fusion.route), custom_call_target="tpu_custom_call" | custom-call | flops 469762048 | bytes 3276800 | tf_op jit(solution)/shard_map/add/pallas_call | solution.py:129
  66.5 5.5 %all-to-all-start.1 = ((bf16[32,16,896]{2,1,0:T(8,128)(2,1)}), bf16[32,16,896]{2,1,0:T(8,128)(2,1)S(1)}, u32[]{:S(2)}, u32[]{:S(2)}) async-start(bf16[32,16,896]{2,1,0:T(8,128)(2,1)} %bitcast.2), calls=%async_computation.1 | async-start | bytes 1835008 | tf_op jit(solution)/shard_map/all_to_all | solution.py:233
  72.1 0.0 copy-start.2
  72.1 0.0 copy-start.3
  72.1 0.1 dynamic_slice.6.lens
  72.2 0.1 dynamic_slice.7.slopes
  72.3 15.3 %all-to-all-done.1 = bf16[32,16,896]{2,1,0:T(8,128)(2,1)S(1)} async-done(((bf16[32,16,896]{2,1,0:T(8,128)(2,1)}), bf16[32,16,896]{2,1,0:T(8,128)(2,1)S(1)}, u32[]{:S(2)}, u32[]{:S(2)}) %all-to-all-start.1) | async-done | bytes 917536 | tf_op jit(solution)/shard_map/all_to_all | solution.py:233
  87.6 0.1 convert_reduce_fusion
  87.7 0.1 copy.13
  87.8 0.0 copy-start
  87.9 0.0 copy-done.2
  87.9 0.0 copy-done.3
  87.9 1.4 %attend.1 = bf16[2,896]{1,0:T(2,128)(2,1)} custom-call(s32[2]{0:T(128)S(1)} %dynamic_slice.6.lens, f32[7]{0:T(128)S(1)} %dynamic_slice.7.slopes, bf16[2,2,2,8,896]{4,3,2,1,0:T(8,128)(2,1)S(1)} %get-tuple-element.6.cache, bf16[2,896]{1,0:T(2,128)(2,1)S(1)} %copy-done.3, bf16[2,2,896]{2,1,0:T(2,128)(2,1)S(1)} %copy-done.2, bf16[2,16,2,896]{3,2,1,0:T(2,128)(2,1)S(1)} %bitcast.17), custom_call_target="tpu_custom_call" | custom-call | flops 458752 | bytes 114688 | tf_op jit(solution)/shard_map/attend/pallas_call | solution.py:188
  89.3 0.0 copy-done
  (5 shorter events, 0.1 us)
Async XLA Ops:
  0.6 0.8 copy-start.1
  2.2 17.9 %all-to-all-start = ((bf16[32,2,448]{2,1,0:T(2,128)(2,1)}), bf16[32,2,448]{2,1,0:T(2,128)(2,1)S(1)}, u32[]{:S(2)}, u32[]{:S(2)}) async-start(bf16[32,2,448]{2,1,0:T(2,128)(2,1)} %split_rows.1), calls=%async_computation | async-start | bytes 131072 | tf_op jit(solution)/shard_map/all_to_all | solution.py:211
  12.6 5.0 %copy-start.4 = (s32[64]{0:T(128)S(1)}, s32[64]{0:T(128)}, u32[]{:S(2)}) copy-start(s32[64]{0:T(128)} %param.8) | copy-start | bytes 772
  12.6 5.0 %copy-start.5 = (s32[64]{0:T(128)S(1)}, s32[64]{0:T(128)}, u32[]{:S(2)}) copy-start(s32[64]{0:T(128)} %param.9) | copy-start | bytes 772
  14.2 38.3 %collective-permute-start = (bf16[2,448,896]{2,1,0:T(8,128)(2,1)S(1)}, bf16[2,448,896]{2,1,0:T(8,128)(2,1)S(1)}, u32[]{:S(2)}, u32[]{:S(2)}) collective-permute-start(bf16[2,448,896]{2,1,0:T(8,128)(2,1)S(1)} %bitcast.14), channel_id=1, source_target_pairs={{0,128},{16,48},{32,160},{48,16},{64,192},{80,112},{96,224},{112,8... | collective-permute-start | bytes 4816904 | tf_op jit(solution)/shard_map/ppermute | solution.py:213
  54.0 10.8 %collective-permute-start.1 = (bf16[512,896]{1,0:T(8,128)(2,1)S(1)}, bf16[512,896]{1,0:T(8,128)(2,1)S(1)}, u32[]{:S(2)}, u32[]{:S(2)}) collective-permute-start(bf16[512,896]{1,0:T(8,128)(2,1)S(1)} %away.1), channel_id=1, source_target_pairs={{0,16},{16,0},{32,48},{48,32},{64,80},{80,64},{96,112},{112,96},{1... | collective-permute-start | bytes 2752520 | tf_op jit(solution)/shard_map/ppermute | solution.py:230
  66.5 21.0 %all-to-all-start.1 = ((bf16[32,16,896]{2,1,0:T(8,128)(2,1)}), bf16[32,16,896]{2,1,0:T(8,128)(2,1)S(1)}, u32[]{:S(2)}, u32[]{:S(2)}) async-start(bf16[32,16,896]{2,1,0:T(8,128)(2,1)} %bitcast.2), calls=%async_computation.1 | async-start | bytes 1835008 | tf_op jit(solution)/shard_map/all_to_all | solution.py:233
  72.1 15.8 %copy-start.2 = (bf16[2,2,896]{2,1,0:T(2,128)(2,1)S(1)}, bf16[2,2,896]{2,1,0:T(2,128)(2,1)}, u32[]{:S(2)}) copy-start(bf16[2,2,896]{2,1,0:T(2,128)(2,1)} %new_kv.1) | copy-start | bytes 21508
  72.1 15.8 %copy-start.3 = (bf16[2,896]{1,0:T(2,128)(2,1)S(1)}, bf16[2,896]{1,0:T(2,128)(2,1)}, u32[]{:S(2)}) copy-start(bf16[2,896]{1,0:T(2,128)(2,1)} %query.1) | copy-start | bytes 10756
  87.8 1.5 %copy-start = (bf16[2,8,2,2,896]{4,3,2,1,0:T(2,128)(2,1)}, bf16[2,8,2,2,896]{4,3,2,1,0:T(2,128)(2,1)S(1)}, u32[]{:S(2)}) copy-start(bf16[2,8,2,2,896]{4,3,2,1,0:T(2,128)(2,1)S(1)} %copy.13) | copy-start | bytes 344068

commit v8 on v7

--- a/solution.py
+++ b/solution.py
@@ -39,7 +39,8 @@
     return (index // (CORES * SIDE) + index // CORES) % 2
 
 
-def split_rows_kernel(rows, sent):
+def split_rows_kernel(rows, weights, sent, same):
+    del weights, same
     groups, share, block = sent.shape
     for to in range(groups):
         row = parity(to)
@@ -47,16 +48,20 @@
             sent[to, part : part + 1, :] = rows[row : row + 1, at * block : (at + 1) * block]
 
 
-def split_rows(rows, groups):
+def split_rows(rows, weights, groups):
     block = rows.shape[1] // groups
     return pl.pallas_call(
         split_rows_kernel,
-        out_shape=jax.ShapeDtypeStruct((groups, 2, block), jnp.bfloat16),
-        in_specs=[VMEM],
-        out_specs=VMEM,
+        out_shape=[
+            jax.ShapeDtypeStruct((groups, 2, block), jnp.bfloat16),
+            jax.ShapeDtypeStruct(weights.shape, weights.dtype),
+        ],
+        in_specs=[VMEM, ANYWHERE],
+        out_specs=[VMEM, ANYWHERE],
+        input_output_aliases={1: 1},
         compiler_params=pltpu.CompilerParams(vmem_limit_bytes=KERNEL_VMEM),
         name="split_rows",
-    )(rows)
+    )(rows, weights)
 
 
 def join_rows_kernel(parts, row, rows):
@@ -207,9 +212,9 @@
     columns = kv_weight.shape[2]
     heads_here = columns // HD
 
-    sent = split_rows(stored_rows, groups)
+    w_own = kv_weight.transpose(1, 0, 2)
+    sent, w_own = split_rows(stored_rows, w_own, groups)
     parts = lax.all_to_all(sent, "dp", split_axis=0, concat_axis=0, tiled=True)
-    w_own = kv_weight.transpose(1, 0, 2)
     w_next = lax.ppermute(w_own, "dp", [(i, partner(i)) for i in range(groups)])
 
     slots = jnp.arange(requests, dtype=jnp.int32)

time: 89.7 us -> 89.4 us (level)
  waiting for transfers between devices: 17.9 us -> 19.5 us
  starting transfers between devices: 27.9 us -> 26.8 us
    all_to_all x1, waiting for transfers between devices: 2.16 us -> 3.81 us  [per_device(): parts = lax.all_to_all(sent, 'dp', split_axis=0, concat_axis=0, tiled=True)]
    all_to_all x1, starting transfers between devices: 5.54 us -> 4.41 us  [per_device(): lax.all_to_all(partial.reshape(groups, REQ_DEV * steps, columns), 'dp', s...]
  transfers between devices with their start and end apart: 4 -> 4, of which waited for: 3 -> 3; matrix products, arithmetic and copies ran while one was open for 3% -> 1% of each run, Pallas kernels for 2% -> 2%
where the time goes in v8:
time: 89.4 us; the launch traced here: 89 us
  blocking collectives  32.4 us (36%)
  starting transfers between devices  26.8 us (30%)
  waiting for transfers between devices  19.5 us (22%)
  Pallas kernels  6.96 us (8%)
  local copies, waits for them, and re-layouts  2 us (2%)
    all_gather x1, blocking collectives, per_device(): every = lax.all_gather(join_rows(parts, row), 'tensor', axis=0, tiled=True)  32.4 us
    all_to_all x1, waiting for transfers between devices, per_device(): lax.all_to_all(partial.reshape(groups, REQ_DEV * steps, columns), 'dp', s...  15.3 us
    all_to_all x1, starting transfers between devices, per_device(): parts = lax.all_to_all(sent, 'dp', split_axis=0, concat_axis=0, tiled=True)  10.4 us
    ppermute x1, starting transfers between devices, per_device(): received = lax.ppermute(away, 'dp', [(i, i ^ 1) for i in range(groups)])  8.69 us
    all_to_all x1, starting transfers between devices, per_device(): lax.all_to_all(partial.reshape(groups, REQ_DEV * steps, columns), 'dp', s...  4.41 us
    all_to_all x1, waiting for transfers between devices, per_device(): parts = lax.all_to_all(sent, 'dp', split_axis=0, concat_axis=0, tiled=True)  3.81 us
    ppermute x1, starting transfers between devices, per_device(): w_next = lax.ppermute(w_own, 'dp', [(i, partner(i)) for i in range(groups)])  3.3 us
    pallas_call x2, Pallas kernels, product(): pl.pallas_call(functools.partial(product_kernel, home), out_shape=jax.Sha...  2.95 us
  transfers between devices with their start and end apart: 4, of which 3 were waited for; matrix products, arithmetic and copies ran while one was open for 1% of the time, Pallas kernels for 2%

profile of v8, /device:TPU:1, one launch (start us, length us, event | category | flops | bytes accessed | tf_op | source)
XLA Modules:
  0.0 89.0 jit_solution(8700114991814266419)
XLA Ops:
  0.6 0.0 copy-start.1
  0.6 1.6 %copy.16 = bf16[448,2,896]{2,0,1:T(8,128)(2,1)S(1)} copy(bf16[448,2,896]{2,1,0:T(2,128)(2,1)} %param.7) | data formatting | bytes 3211264 | tf_op args[1]
  2.3 0.0 copy-start.4
  2.3 0.0 copy-start.5
  2.3 0.0 copy-done.1
  2.3 0.7 split_rows.1
  3.0 10.4 %all-to-all-start = ((bf16[32,2,448]{2,1,0:T(2,128)(2,1)}), bf16[32,2,448]{2,1,0:T(2,128)(2,1)S(1)}, u32[]{:S(2)}, u32[]{:S(2)}) async-start(bf16[32,2,448]{2,1,0:T(2,128)(2,1)} %get-tuple-element.4), calls=%async_computation | async-start | bytes 131072 | tf_op jit(solution)/shard_map/all_to_all | solution.py:217
  13.4 3.3 %collective-permute-start = (bf16[2,448,896]{2,1,0:T(8,128)(2,1)S(1)}, bf16[2,448,896]{2,1,0:T(8,128)(2,1)S(1)}, u32[]{:S(2)}, u32[]{:S(2)}) collective-permute-start(bf16[2,448,896]{2,1,0:T(8,128)(2,1)S(1)} %get-tuple-element.5.w_own), channel_id=1, source_target_pairs={{0,128},{16,48},{32,160},{48,16},{64,192},{80,112},{96,224},{112,8... | collective-permute-start | bytes 4816904 | tf_op jit(solution)/shard_map/ppermute | solution.py:218
  16.7 0.0 copy-done.4
  16.8 0.0 copy-done.5
  16.8 0.1 select_reduce_fusion.1
  16.9 0.1 add_select_fusion
  17.0 0.1 select_n.54.row
  17.1 3.8 %all-to-all-done.parts = bf16[32,2,448]{2,1,0:T(2,128)(2,1)S(1)} async-done(((bf16[32,2,448]{2,1,0:T(2,128)(2,1)}), bf16[32,2,448]{2,1,0:T(2,128)(2,1)S(1)}, u32[]{:S(2)}, u32[]{:S(2)}) %all-to-all-start) | async-done | bytes 57376 | tf_op jit(solution)/shard_map/all_to_all | solution.py:217
  20.9 0.2 join_rows.1
  21.1 32.4 %all_gather.3.x = bf16[512,896]{1,0:T(8,128)(2,1)S(1)} all-gather(bf16[32,896]{1,0:T(8,128)(2,1)S(1)} %join_rows.1), channel_id=1, replica_groups=mesh['dp'=32,'tensor'=16] {'tensor'}, dimensions={0}, use_global_device_ids=true | all-gather | bytes 974848 | tf_op jit(solution)/shard_map/all_gather | solution.py:232
  53.4 0.0 collective-permute-done.w_next
  53.4 1.5 %away.1 = bf16[512,896]{1,0:T(8,128)(2,1)S(1)} custom-call(s32[1]{0:T(128)} %bitcast.where, bf16[512,896]{1,0:T(8,128)(2,1)S(1)} %all_gather.3.x, bf16[2,448,896]{2,1,0:T(8,128)(2,1)S(1)} %get-tuple-element.5.w_own, bf16[2,448,896]{2,1,0:T(8,128)(2,1)S(1)} %collective-permute-done.w_next), custom_call_target="tpu_custom_call" | custom-call | flops 822083584 | bytes 3440640 | tf_op jit(solution)/shard_map/away/pallas_call | solution.py:112
  54.9 8.7 %collective-permute-start.1 = (bf16[512,896]{1,0:T(8,128)(2,1)S(1)}, bf16[512,896]{1,0:T(8,128)(2,1)S(1)}, u32[]{:S(2)}, u32[]{:S(2)}) collective-permute-start(bf16[512,896]{1,0:T(8,128)(2,1)S(1)} %away.1), channel_id=1, source_target_pairs={{0,16},{16,0},{32,48},{48,32},{64,80},{80,64},{96,112},{112,96},{1... | collective-permute-start | bytes 2752520 | tf_op jit(solution)/shard_map/ppermute | solution.py:235
  63.6 0.2 fusion.route
  63.8 1.5 %home.1.one = bf16[512,896]{1,0:T(8,128)(2,1)S(1)} custom-call(s32[1]{0:T(128)} %bitcast.where, bf16[512,896]{1,0:T(8,128)(2,1)S(1)} %all_gather.3.x, bf16[2,448,896]{2,1,0:T(8,128)(2,1)S(1)} %get-tuple-element.5.w_own, bf16[2,448,896]{2,1,0:T(8,128)(2,1)S(1)} %collective-permute-done.w_next), custom_call_target="tpu_custom_call" | custom-call | flops 822083584 | bytes 3440640 | tf_op jit(solution)/shard_map/home/pallas_call | solution.py:112
  65.2 0.4 collective-permute-done.1.other
  65.7 1.7 %add.152 = bf16[512,896]{1,0:T(8,128)(2,1)} custom-call(bf16[512,896]{1,0:T(8,128)(2,1)S(1)} %home.1.one, bf16[512,896]{1,0:T(8,128)(2,1)S(1)} %collective-permute-done.1.other, bf16[512,512]{1,0:T(8,128)(2,1)S(1)} %fusion.route), custom_call_target="tpu_custom_call" | custom-call | flops 469762048 | bytes 3276800 | tf_op jit(solution)/shard_map/add/pallas_call | solution.py:134
  67.4 4.4 %all-to-all-start.1 = ((bf16[32,16,896]{2,1,0:T(8,128)(2,1)}), bf16[32,16,896]{2,1,0:T(8,128)(2,1)S(1)}, u32[]{:S(2)}, u32[]{:S(2)}) async-start(bf16[32,16,896]{2,1,0:T(8,128)(2,1)} %bitcast.2), calls=%async_computation.1 | async-start | bytes 1835008 | tf_op jit(solution)/shard_map/all_to_all | solution.py:238
  71.8 0.0 copy-start.2
  71.8 0.0 copy-start.3
  71.8 0.1 dynamic_slice.6.lens
  71.9 0.1 dynamic_slice.7.slopes
  72.0 15.3 %all-to-all-done.1 = bf16[32,16,896]{2,1,0:T(8,128)(2,1)S(1)} async-done(((bf16[32,16,896]{2,1,0:T(8,128)(2,1)}), bf16[32,16,896]{2,1,0:T(8,128)(2,1)S(1)}, u32[]{:S(2)}, u32[]{:S(2)}) %all-to-all-start.1) | async-done | bytes 917536 | tf_op jit(solution)/shard_map/all_to_all | solution.py:238
  87.3 0.1 convert_reduce_fusion
  87.4 0.1 copy.14
  87.5 0.0 copy-start
  87.6 0.0 copy-done.2
  87.6 0.0 copy-done.3
  87.6 1.4 %attend.1 = bf16[2,896]{1,0:T(2,128)(2,1)} custom-call(s32[2]{0:T(128)S(1)} %dynamic_slice.6.lens, f32[7]{0:T(128)S(1)} %dynamic_slice.7.slopes, bf16[2,2,2,8,896]{4,3,2,1,0:T(8,128)(2,1)S(1)} %get-tuple-element.10.cache, bf16[2,896]{1,0:T(2,128)(2,1)S(1)} %copy-done.3, bf16[2,2,896]{2,1,0:T(2,128)(2,1)S(1)} %copy-done.2, bf16[2,16,2,896]{3,2,1,0:T(2,128)(2,1)S(1)} %bitcast.15), custom_call_target="tpu_custom_call" | custom-call | flops 458752 | bytes 114688 | tf_op jit(solution)/shard_map/attend/pallas_call | solution.py:193
  89.0 0.0 copy-done
  (5 shorter events, 0.1 us)
Async XLA Ops:
  0.6 1.7 %copy-start.1 = (bf16[2,14336]{1,0:T(2,128)(2,1)S(1)}, bf16[2,14336]{1,0:T(2,128)(2,1)}, u32[]{:S(2)}) copy-start(bf16[2,14336]{1,0:T(2,128)(2,1)} %rows.1) | copy-start | bytes 172036
  2.3 14.5 %copy-start.4 = (s32[64]{0:T(128)S(1)}, s32[64]{0:T(128)}, u32[]{:S(2)}) copy-start(s32[64]{0:T(128)} %param.8) | copy-start | bytes 772
  2.3 14.5 %copy-start.5 = (s32[64]{0:T(128)S(1)}, s32[64]{0:T(128)}, u32[]{:S(2)}) copy-start(s32[64]{0:T(128)} %param.9) | copy-start | bytes 772
  3.0 17.9 %all-to-all-start = ((bf16[32,2,448]{2,1,0:T(2,128)(2,1)}), bf16[32,2,448]{2,1,0:T(2,128)(2,1)S(1)}, u32[]{:S(2)}, u32[]{:S(2)}) async-start(bf16[32,2,448]{2,1,0:T(2,128)(2,1)} %get-tuple-element.4), calls=%async_computation | async-start | bytes 131072 | tf_op jit(solution)/shard_map/all_to_all | solution.py:217
  13.4 40.0 %collective-permute-start = (bf16[2,448,896]{2,1,0:T(8,128)(2,1)S(1)}, bf16[2,448,896]{2,1,0:T(8,128)(2,1)S(1)}, u32[]{:S(2)}, u32[]{:S(2)}) collective-permute-start(bf16[2,448,896]{2,1,0:T(8,128)(2,1)S(1)} %get-tuple-element.5.w_own), channel_id=1, source_target_pairs={{0,128},{16,48},{32,160},{48,16},{64,192},{80,112},{96,224},{112,8... | collective-permute-start | bytes 4816904 | tf_op jit(solution)/shard_map/ppermute | solution.py:218
  54.9 10.8 %collective-permute-start.1 = (bf16[512,896]{1,0:T(8,128)(2,1)S(1)}, bf16[512,896]{1,0:T(8,128)(2,1)S(1)}, u32[]{:S(2)}, u32[]{:S(2)}) collective-permute-start(bf16[512,896]{1,0:T(8,128)(2,1)S(1)} %away.1), channel_id=1, source_target_pairs={{0,16},{16,0},{32,48},{48,32},{64,80},{80,64},{96,112},{112,96},{1... | collective-permute-start | bytes 2752520 | tf_op jit(solution)/shard_map/ppermute | solution.py:235
  67.4 19.9 %all-to-all-start.1 = ((bf16[32,16,896]{2,1,0:T(8,128)(2,1)}), bf16[32,16,896]{2,1,0:T(8,128)(2,1)S(1)}, u32[]{:S(2)}, u32[]{:S(2)}) async-start(bf16[32,16,896]{2,1,0:T(8,128)(2,1)} %bitcast.2), calls=%async_computation.1 | async-start | bytes 1835008 | tf_op jit(solution)/shard_map/all_to_all | solution.py:238
  71.8 15.8 %copy-start.2 = (bf16[2,2,896]{2,1,0:T(2,128)(2,1)S(1)}, bf16[2,2,896]{2,1,0:T(2,128)(2,1)}, u32[]{:S(2)}) copy-start(bf16[2,2,896]{2,1,0:T(2,128)(2,1)} %new_kv.1) | copy-start | bytes 21508
  71.8 15.8 %copy-start.3 = (bf16[2,896]{1,0:T(2,128)(2,1)S(1)}, bf16[2,896]{1,0:T(2,128)(2,1)}, u32[]{:S(2)}) copy-start(bf16[2,896]{1,0:T(2,128)(2,1)} %query.1) | copy-start | bytes 10756
  87.5 1.5 %copy-start = (bf16[2,8,2,2,896]{4,3,2,1,0:T(2,128)(2,1)}, bf16[2,8,2,2,896]{4,3,2,1,0:T(2,128)(2,1)S(1)}, u32[]{:S(2)}) copy-start(bf16[2,8,2,2,896]{4,3,2,1,0:T(2,128)(2,1)S(1)} %copy.14) | copy-start | bytes 344068

commit v9 on v8

--- a/solution.py
+++ b/solution.py
@@ -29,6 +29,7 @@
 KERNEL_VMEM = 24 * 1024 * 1024
 SIDE = 4
 CORES = 2
+TILE = 512
 
 
 def partner(index):
@@ -96,13 +97,11 @@
         copy.wait()
 
 
-def product_kernel(home, where, x, w_own, w_next, out, held, sems):
+def product_kernel(home, where, x, w_own, w_next, out):
     column = where[0] if home else 1 - where[0]
     block = w_own.shape[1]
-    copies = fetch([(w_next.at[column], held)], sems)
     total = jnp.dot(x[:, :block], w_own[column], preferred_element_type=jnp.float32)
-    finish(copies)
-    total += jnp.dot(x[:, block:], held[...], preferred_element_type=jnp.float32)
+    total += jnp.dot(x[:, block:], w_next[column], preferred_element_type=jnp.float32)
     out[...] = total.astype(jnp.bfloat16)
 
 
@@ -112,9 +111,8 @@
     return pl.pallas_call(
         functools.partial(product_kernel, home),
         out_shape=jax.ShapeDtypeStruct((rows, columns), jnp.bfloat16),
-        in_specs=[SMEM, VMEM, VMEM, ANYWHERE],
+        in_specs=[SMEM, VMEM, VMEM, VMEM],
         out_specs=VMEM,
-        scratch_shapes=[pltpu.VMEM(w_next.shape[1:], jnp.bfloat16), pltpu.SemaphoreType.DMA((1,))],
         compiler_params=pltpu.CompilerParams(vmem_limit_bytes=KERNEL_VMEM),
         cost_estimate=pl.CostEstimate(
             flops=2 * rows * depth * columns,
@@ -125,9 +123,15 @@
     )(where, x, w_own, w_next)
 
 
-def add_kernel(one, other, route, total):
-    both = (one[...].astype(jnp.float32) + other[...].astype(jnp.float32)).astype(jnp.bfloat16)
-    total[...] = jnp.dot(route[...], both, preferred_element_type=jnp.float32).astype(jnp.bfloat16)
+def add_kernel(one, other, route, total, made, sems):
+    columns = total.shape[1]
+    copies = []
+    for at, (start, stop) in enumerate(((0, TILE), (TILE, columns))):
+        part = pl.ds(start, stop - start)
+        both = (one[:, part].astype(jnp.float32) + other[:, part].astype(jnp.float32)).astype(jnp.bfloat16)
+        made[:, part] = jnp.dot(route[...], both, preferred_element_type=jnp.float32).astype(jnp.bfloat16)
+        copies += fetch([(made.at[:, part], total.at[:, part])], sems.at[pl.ds(at, 1)])
+    finish(copies)
 
 
 def add(one, other, route):
@@ -135,7 +139,8 @@
         add_kernel,
         out_shape=jax.ShapeDtypeStruct(one.shape, jnp.bfloat16),
         in_specs=[VMEM, VMEM, VMEM],
-        out_specs=VMEM,
+        out_specs=ANYWHERE,
+        scratch_shapes=[pltpu.VMEM(one.shape, jnp.bfloat16), pltpu.SemaphoreType.DMA((2,))],
         compiler_params=pltpu.CompilerParams(vmem_limit_bytes=KERNEL_VMEM),
         cost_estimate=pl.CostEstimate(
             flops=2 * one.size * route.shape[0], bytes_accessed=6 * one.size + 2 * route.size, transcendentals=0

time: 89.4 us -> 89.1 us (level)
  no operation moved by 1% of the time
where the time goes in v9:
time: 89.1 us; the launch traced here: 88.7 us
  blocking collectives  32.4 us (36%)
  starting transfers between devices  26.8 us (30%)
  waiting for transfers between devices  19.7 us (22%)
  Pallas kernels  6.47 us (7%)
  local copies, waits for them, and re-layouts  2 us (2%)
    all_gather x1, blocking collectives, per_device(): every = lax.all_gather(join_rows(parts, row), 'tensor', axis=0, tiled=True)  32.4 us
    all_to_all x1, waiting for transfers between devices, per_device(): lax.all_to_all(partial.reshape(groups, REQ_DEV * steps, columns), 'dp', s...  15.3 us
    all_to_all x1, starting transfers between devices, per_device(): parts = lax.all_to_all(sent, 'dp', split_axis=0, concat_axis=0, tiled=True)  10.4 us
    ppermute x1, starting transfers between devices, per_device(): received = lax.ppermute(away, 'dp', [(i, i ^ 1) for i in range(groups)])  8.69 us
    all_to_all x1, starting transfers between devices, per_device(): lax.all_to_all(partial.reshape(groups, REQ_DEV * steps, columns), 'dp', s...  4.43 us
    all_to_all x1, waiting for transfers between devices, per_device(): parts = lax.all_to_all(sent, 'dp', split_axis=0, concat_axis=0, tiled=True)  3.81 us
    ppermute x1, starting transfers between devices, per_device(): w_next = lax.ppermute(w_own, 'dp', [(i, partner(i)) for i in range(groups)])  3.3 us
    pallas_call x2, Pallas kernels, product(): pl.pallas_call(functools.partial(product_kernel, home), out_shape=jax.Sha...  2.59 us
  transfers between devices with their start and end apart: 4, of which 3 were waited for; matrix products, arithmetic and copies ran while one was open for 1% of the time, Pallas kernels for 2%

profile of v9, /device:TPU:1, one launch (start us, length us, event | category | flops | bytes accessed | tf_op | source)
XLA Modules:
  0.0 88.7 jit_solution(16527345283095058157)
XLA Ops:
  0.6 0.0 copy-start.1
  0.6 1.6 %copy.16 = bf16[448,2,896]{2,0,1:T(8,128)(2,1)S(1)} copy(bf16[448,2,896]{2,1,0:T(2,128)(2,1)} %param.7) | data formatting | bytes 3211264 | tf_op args[1]
  2.3 0.0 copy-start.4
  2.3 0.0 copy-start.5
  2.3 0.0 copy-done.1
  2.3 0.7 split_rows.1
  3.0 10.4 %all-to-all-start = ((bf16[32,2,448]{2,1,0:T(2,128)(2,1)}), bf16[32,2,448]{2,1,0:T(2,128)(2,1)S(1)}, u32[]{:S(2)}, u32[]{:S(2)}) async-start(bf16[32,2,448]{2,1,0:T(2,128)(2,1)} %get-tuple-element.4), calls=%async_computation | async-start | bytes 131072 | tf_op jit(solution)/shard_map/all_to_all | solution.py:222
  13.4 3.3 %collective-permute-start = (bf16[2,448,896]{2,1,0:T(8,128)(2,1)S(1)}, bf16[2,448,896]{2,1,0:T(8,128)(2,1)S(1)}, u32[]{:S(2)}, u32[]{:S(2)}) collective-permute-start(bf16[2,448,896]{2,1,0:T(8,128)(2,1)S(1)} %get-tuple-element.5.w_own), channel_id=1, source_target_pairs={{0,128},{16,48},{32,160},{48,16},{64,192},{80,112},{96,224},{112,8... | collective-permute-start | bytes 4816904 | tf_op jit(solution)/shard_map/ppermute | solution.py:223
  16.7 0.0 copy-done.4
  16.8 0.0 copy-done.5
  16.8 0.1 select_reduce_fusion.1
  16.9 0.1 add_select_fusion
  17.0 0.1 select_n.54.row
  17.1 3.8 %all-to-all-done.parts = bf16[32,2,448]{2,1,0:T(2,128)(2,1)S(1)} async-done(((bf16[32,2,448]{2,1,0:T(2,128)(2,1)}), bf16[32,2,448]{2,1,0:T(2,128)(2,1)S(1)}, u32[]{:S(2)}, u32[]{:S(2)}) %all-to-all-start) | async-done | bytes 57376 | tf_op jit(solution)/shard_map/all_to_all | solution.py:222
  20.9 0.2 join_rows.1
  21.1 32.4 %all_gather.3.x = bf16[512,896]{1,0:T(8,128)(2,1)S(1)} all-gather(bf16[32,896]{1,0:T(8,128)(2,1)S(1)} %join_rows.1), channel_id=1, replica_groups=mesh['dp'=32,'tensor'=16] {'tensor'}, dimensions={0}, use_global_device_ids=true | all-gather | bytes 974848 | tf_op jit(solution)/shard_map/all_gather | solution.py:237
  53.4 0.0 collective-permute-done.w_next
  53.4 1.3 %away.1 = bf16[512,896]{1,0:T(8,128)(2,1)S(1)} custom-call(s32[1]{0:T(128)} %bitcast.where, bf16[512,896]{1,0:T(8,128)(2,1)S(1)} %all_gather.3.x, bf16[2,448,896]{2,1,0:T(8,128)(2,1)S(1)} %get-tuple-element.5.w_own, bf16[2,448,896]{2,1,0:T(8,128)(2,1)S(1)} %collective-permute-done.w_next), custom_call_target="tpu_custom_call" | custom-call | flops 822083584 | bytes 3440640 | tf_op jit(solution)/shard_map/away/pallas_call | solution.py:111
  54.7 8.7 %collective-permute-start.1 = (bf16[512,896]{1,0:T(8,128)(2,1)S(1)}, bf16[512,896]{1,0:T(8,128)(2,1)S(1)}, u32[]{:S(2)}, u32[]{:S(2)}) collective-permute-start(bf16[512,896]{1,0:T(8,128)(2,1)S(1)} %away.1), channel_id=1, source_target_pairs={{0,16},{16,0},{32,48},{48,32},{64,80},{80,64},{96,112},{112,96},{1... | collective-permute-start | bytes 2752520 | tf_op jit(solution)/shard_map/ppermute | solution.py:240
  63.4 0.2 fusion.route
  63.6 1.3 %home.1.one = bf16[512,896]{1,0:T(8,128)(2,1)S(1)} custom-call(s32[1]{0:T(128)} %bitcast.where, bf16[512,896]{1,0:T(8,128)(2,1)S(1)} %all_gather.3.x, bf16[2,448,896]{2,1,0:T(8,128)(2,1)S(1)} %get-tuple-element.5.w_own, bf16[2,448,896]{2,1,0:T(8,128)(2,1)S(1)} %collective-permute-done.w_next), custom_call_target="tpu_custom_call" | custom-call | flops 822083584 | bytes 3440640 | tf_op jit(solution)/shard_map/home/pallas_call | solution.py:111
  64.9 0.6 collective-permute-done.1.other
  65.5 1.6 %add.152 = bf16[512,896]{1,0:T(8,128)(2,1)} custom-call(bf16[512,896]{1,0:T(8,128)(2,1)S(1)} %home.1.one, bf16[512,896]{1,0:T(8,128)(2,1)S(1)} %collective-permute-done.1.other, bf16[512,512]{1,0:T(8,128)(2,1)S(1)} %fusion.route), custom_call_target="tpu_custom_call" | custom-call | flops 469762048 | bytes 3276800 | tf_op jit(solution)/shard_map/add/pallas_call | solution.py:138
  67.1 4.4 %all-to-all-start.1 = ((bf16[32,16,896]{2,1,0:T(8,128)(2,1)}), bf16[32,16,896]{2,1,0:T(8,128)(2,1)S(1)}, u32[]{:S(2)}, u32[]{:S(2)}) async-start(bf16[32,16,896]{2,1,0:T(8,128)(2,1)} %bitcast.2), calls=%async_computation.1 | async-start | bytes 1835008 | tf_op jit(solution)/shard_map/all_to_all | solution.py:243
  71.5 0.0 copy-start.2
  71.5 0.0 copy-start.3
  71.5 0.1 dynamic_slice.6.lens
  71.6 0.1 dynamic_slice.7.slopes
  71.7 15.3 %all-to-all-done.1 = bf16[32,16,896]{2,1,0:T(8,128)(2,1)S(1)} async-done(((bf16[32,16,896]{2,1,0:T(8,128)(2,1)}), bf16[32,16,896]{2,1,0:T(8,128)(2,1)S(1)}, u32[]{:S(2)}, u32[]{:S(2)}) %all-to-all-start.1) | async-done | bytes 917536 | tf_op jit(solution)/shard_map/all_to_all | solution.py:243
  87.0 0.1 convert_reduce_fusion
  87.2 0.1 copy.14
  87.3 0.0 copy-start
  87.3 0.0 copy-done.2
  87.3 0.0 copy-done.3
  87.3 1.4 %attend.1 = bf16[2,896]{1,0:T(2,128)(2,1)} custom-call(s32[2]{0:T(128)S(1)} %dynamic_slice.6.lens, f32[7]{0:T(128)S(1)} %dynamic_slice.7.slopes, bf16[2,2,2,8,896]{4,3,2,1,0:T(8,128)(2,1)S(1)} %get-tuple-element.10.cache, bf16[2,896]{1,0:T(2,128)(2,1)S(1)} %copy-done.3, bf16[2,2,896]{2,1,0:T(2,128)(2,1)S(1)} %copy-done.2, bf16[2,16,2,896]{3,2,1,0:T(2,128)(2,1)S(1)} %bitcast.15), custom_call_target="tpu_custom_call" | custom-call | flops 458752 | bytes 114688 | tf_op jit(solution)/shard_map/attend/pallas_call | solution.py:198
  88.7 0.0 copy-done
  (5 shorter events, 0.1 us)
Async XLA Ops:
  0.6 1.7 %copy-start.1 = (bf16[2,14336]{1,0:T(2,128)(2,1)S(1)}, bf16[2,14336]{1,0:T(2,128)(2,1)}, u32[]{:S(2)}) copy-start(bf16[2,14336]{1,0:T(2,128)(2,1)} %rows.1) | copy-start | bytes 172036
  2.3 14.5 %copy-start.4 = (s32[64]{0:T(128)S(1)}, s32[64]{0:T(128)}, u32[]{:S(2)}) copy-start(s32[64]{0:T(128)} %param.8) | copy-start | bytes 772
  2.3 14.5 %copy-start.5 = (s32[64]{0:T(128)S(1)}, s32[64]{0:T(128)}, u32[]{:S(2)}) copy-start(s32[64]{0:T(128)} %param.9) | copy-start | bytes 772
  3.0 17.9 %all-to-all-start = ((bf16[32,2,448]{2,1,0:T(2,128)(2,1)}), bf16[32,2,448]{2,1,0:T(2,128)(2,1)S(1)}, u32[]{:S(2)}, u32[]{:S(2)}) async-start(bf16[32,2,448]{2,1,0:T(2,128)(2,1)} %get-tuple-element.4), calls=%async_computation | async-start | bytes 131072 | tf_op jit(solution)/shard_map/all_to_all | solution.py:222
  13.4 40.0 %collective-permute-start = (bf16[2,448,896]{2,1,0:T(8,128)(2,1)S(1)}, bf16[2,448,896]{2,1,0:T(8,128)(2,1)S(1)}, u32[]{:S(2)}, u32[]{:S(2)}) collective-permute-start(bf16[2,448,896]{2,1,0:T(8,128)(2,1)S(1)} %get-tuple-element.5.w_own), channel_id=1, source_target_pairs={{0,128},{16,48},{32,160},{48,16},{64,192},{80,112},{96,224},{112,8... | collective-permute-start | bytes 4816904 | tf_op jit(solution)/shard_map/ppermute | solution.py:223
  54.7 10.8 %collective-permute-start.1 = (bf16[512,896]{1,0:T(8,128)(2,1)S(1)}, bf16[512,896]{1,0:T(8,128)(2,1)S(1)}, u32[]{:S(2)}, u32[]{:S(2)}) collective-permute-start(bf16[512,896]{1,0:T(8,128)(2,1)S(1)} %away.1), channel_id=1, source_target_pairs={{0,16},{16,0},{32,48},{48,32},{64,80},{80,64},{96,112},{112,96},{1... | collective-permute-start | bytes 2752520 | tf_op jit(solution)/shard_map/ppermute | solution.py:240
  67.1 19.9 %all-to-all-start.1 = ((bf16[32,16,896]{2,1,0:T(8,128)(2,1)}), bf16[32,16,896]{2,1,0:T(8,128)(2,1)S(1)}, u32[]{:S(2)}, u32[]{:S(2)}) async-start(bf16[32,16,896]{2,1,0:T(8,128)(2,1)} %bitcast.2), calls=%async_computation.1 | async-start | bytes 1835008 | tf_op jit(solution)/shard_map/all_to_all | solution.py:243
  71.5 15.8 %copy-start.2 = (bf16[2,2,896]{2,1,0:T(2,128)(2,1)S(1)}, bf16[2,2,896]{2,1,0:T(2,128)(2,1)}, u32[]{:S(2)}) copy-start(bf16[2,2,896]{2,1,0:T(2,128)(2,1)} %new_kv.1) | copy-start | bytes 21508
  71.5 15.8 %copy-start.3 = (bf16[2,896]{1,0:T(2,128)(2,1)S(1)}, bf16[2,896]{1,0:T(2,128)(2,1)}, u32[]{:S(2)}) copy-start(bf16[2,896]{1,0:T(2,128)(2,1)} %query.1) | copy-start | bytes 10756
  87.3 1.5 %copy-start = (bf16[2,8,2,2,896]{4,3,2,1,0:T(2,128)(2,1)}, bf16[2,8,2,2,896]{4,3,2,1,0:T(2,128)(2,1)S(1)}, u32[]{:S(2)}) copy-start(bf16[2,8,2,2,896]{4,3,2,1,0:T(2,128)(2,1)S(1)} %copy.14) | copy-start | bytes 344068

commit v10 on v9

--- a/solution.py
+++ b/solution.py
@@ -155,10 +155,9 @@
     heads = columns // HD
     steps = cache.shape[3]
     factor = 1.0 / math.sqrt(HD)
-    head_lane = lax.broadcasted_iota(jnp.int32, (steps, HD), 1)
-    slope = jnp.zeros((steps, HD), jnp.float32)
-    for head in range(heads):
-        slope = jnp.where(head_lane == head, slopes[head], slope)
+    head_lane = lax.broadcasted_iota(jnp.int32, (2 * steps, HD), 1)
+    step = lax.broadcasted_iota(jnp.int32, (2 * steps, HD), 0)
+    place = jnp.where(step < steps, 2 * step, 2 * (step - steps) + 1)
     for slot in range(slots):
         asked = query[slot : slot + 1, :].astype(jnp.float32)
         own_value = new_kv[slot, 1:2, :].astype(jnp.float32)
@@ -172,25 +171,20 @@
             return scores * factor
 
         own = by_head(new_kv[slot, 0:1, :].astype(jnp.float32))
-        scores = []
-        for half in range(2):
-            place = 2 * lax.broadcasted_iota(jnp.int32, (steps, HD), 0) + half
-            distance = (lens[slot] - place).astype(jnp.float32)
-            found = by_head(cache[half, 0, slot].astype(jnp.float32)) - slope * distance
-            scores.append(jnp.where(place < lens[slot], found, -jnp.inf))
-        top = jnp.maximum(jnp.max(jnp.maximum(scores[0], scores[1]), axis=0, keepdims=True), own)
-        raised = [jnp.exp(score - top) for score in scores]
+        keys = jnp.concatenate([cache[half, 0, slot].astype(jnp.float32) for half in range(2)], axis=0)
+        values = jnp.concatenate([cache[half, 1, slot].astype(jnp.float32) for half in range(2)], axis=0)
+        scores = by_head(keys) - slopes[...] * (lens[slot] - place).astype(jnp.float32)
+        scores = jnp.where(place < lens[slot], scores, -jnp.inf)
+        top = jnp.maximum(jnp.max(scores, axis=0, keepdims=True), own)
+        raised = jnp.exp(scores - top)
         own_raised = jnp.exp(own - top)
-        total = jnp.sum(raised[0] + raised[1], axis=0, keepdims=True) + own_raised
-        weights = [(part / total).astype(jnp.bfloat16).astype(jnp.float32) for part in raised]
+        total = jnp.sum(raised, axis=0, keepdims=True) + own_raised
+        weights = (raised / total).astype(jnp.bfloat16).astype(jnp.float32)
         own_weight = (own_raised / total).astype(jnp.bfloat16).astype(jnp.float32)
         for head in range(heads):
             lanes = slice(head * HD, (head + 1) * HD)
-            mixed = jnp.zeros((steps, HD), jnp.float32)
-            for half in range(2):
-                values = cache[half, 1, slot, :, lanes].astype(jnp.float32)
-                mixed += weights[half][:, head : head + 1] * values
-            mixed = jnp.sum(mixed, axis=0, keepdims=True) + own_weight[:, head : head + 1] * own_value[:, lanes]
+            mixed = jnp.sum(weights[:, head : head + 1] * values[:, lanes], axis=0, keepdims=True)
+            mixed += own_weight[:, head : head + 1] * own_value[:, lanes]
             out[slot : slot + 1, lanes] = mixed.astype(jnp.bfloat16)
 
 
@@ -198,7 +192,7 @@
     return pl.pallas_call(
         attend_kernel,
         out_shape=jax.ShapeDtypeStruct(query.shape, jnp.bfloat16),
-        in_specs=[SMEM, SMEM, VMEM, VMEM, VMEM, VMEM],
+        in_specs=[SMEM, VMEM, VMEM, VMEM, VMEM, VMEM],
         out_specs=VMEM,
         compiler_params=pltpu.CompilerParams(vmem_limit_bytes=KERNEL_VMEM),
         cost_estimate=pl.CostEstimate(flops=8 * cache.size, bytes_accessed=2 * cache.size, transcendentals=cache.size // HD),
@@ -249,7 +243,7 @@
     kv_cache = summed.transpose(2, 3, 0, 1, 4).reshape(REQ_DEV, LMAX, 2, columns)
     here_len = lax.dynamic_slice_in_dim(slot_len, group_index * REQ_DEV, REQ_DEV)
     slopes = lax.dynamic_slice_in_dim(alibi_slopes(HEADS), tensor_index * heads_here, heads_here)
-    return (kv_cache, attend(here_len, slopes, summed, query, new_kv, kv_cache))
+    return (kv_cache, attend(here_len, jnp.pad(slopes, (0, HD - heads_here)).reshape(1, HD), summed, query, new_kv, kv_cache))
 
 
 def solution(mesh):

time: 89.1 us -> 89.1 us (level)
  no operation moved by 1% of the time
where the time goes in v10:
time: 89.1 us; the launch traced here: 88.7 us
  blocking collectives  32.4 us (36%)
  starting transfers between devices  26.8 us (30%)
  waiting for transfers between devices  19.7 us (22%)
  Pallas kernels  6.46 us (7%)
  local copies, waits for them, and re-layouts  2 us (2%)
    all_gather x1, blocking collectives, per_device(): every = lax.all_gather(join_rows(parts, row), 'tensor', axis=0, tiled=True)  32.4 us
    all_to_all x1, waiting for transfers between devices, per_device(): lax.all_to_all(partial.reshape(groups, REQ_DEV * steps, columns), 'dp', s...  15.3 us
    all_to_all x1, starting transfers between devices, per_device(): parts = lax.all_to_all(sent, 'dp', split_axis=0, concat_axis=0, tiled=True)  10.4 us
    ppermute x1, starting transfers between devices, per_device(): received = lax.ppermute(away, 'dp', [(i, i ^ 1) for i in range(groups)])  8.69 us
    all_to_all x1, starting transfers between devices, per_device(): lax.all_to_all(partial.reshape(groups, REQ_DEV * steps, columns), 'dp', s...  4.43 us
    all_to_all x1, waiting for transfers between devices, per_device(): parts = lax.all_to_all(sent, 'dp', split_axis=0, concat_axis=0, tiled=True)  3.81 us
    ppermute x1, starting transfers between devices, per_device(): w_next = lax.ppermute(w_own, 'dp', [(i, partner(i)) for i in range(groups)])  3.3 us
    pallas_call x2, Pallas kernels, product(): pl.pallas_call(functools.partial(product_kernel, home), out_shape=jax.Sha...  2.59 us
  transfers between devices with their start and end apart: 4, of which 3 were waited for; matrix products, arithmetic and copies ran while one was open for 1% of the time, Pallas kernels for 2%

profile of v10, /device:TPU:1, one launch (start us, length us, event | category | flops | bytes accessed | tf_op | source)
XLA Modules:
  0.0 88.7 jit_solution(14286743268787773218)
XLA Ops:
  0.6 0.0 copy-start.1
  0.6 1.6 %copy.16 = bf16[448,2,896]{2,0,1:T(8,128)(2,1)S(1)} copy(bf16[448,2,896]{2,1,0:T(2,128)(2,1)} %param.7) | data formatting | bytes 3211264 | tf_op args[1]
  2.3 0.0 copy-start.4
  2.3 0.0 copy-start.5
  2.3 0.0 copy-done.1
  2.3 0.7 split_rows.1
  3.0 10.4 %all-to-all-start = ((bf16[32,2,448]{2,1,0:T(2,128)(2,1)}), bf16[32,2,448]{2,1,0:T(2,128)(2,1)S(1)}, u32[]{:S(2)}, u32[]{:S(2)}) async-start(bf16[32,2,448]{2,1,0:T(2,128)(2,1)} %get-tuple-element.4), calls=%async_computation | async-start | bytes 131072 | tf_op jit(solution)/shard_map/all_to_all | solution.py:216
  13.4 3.3 %collective-permute-start = (bf16[2,448,896]{2,1,0:T(8,128)(2,1)S(1)}, bf16[2,448,896]{2,1,0:T(8,128)(2,1)S(1)}, u32[]{:S(2)}, u32[]{:S(2)}) collective-permute-start(bf16[2,448,896]{2,1,0:T(8,128)(2,1)S(1)} %get-tuple-element.5.w_own), channel_id=1, source_target_pairs={{0,128},{16,48},{32,160},{48,16},{64,192},{80,112},{96,224},{112,8... | collective-permute-start | bytes 4816904 | tf_op jit(solution)/shard_map/ppermute | solution.py:217
  16.7 0.0 copy-done.4
  16.8 0.0 copy-done.5
  16.8 0.1 select_reduce_fusion.1
  16.9 0.1 add_select_fusion
  17.0 0.1 select_n.54.row
  17.1 3.8 %all-to-all-done.parts = bf16[32,2,448]{2,1,0:T(2,128)(2,1)S(1)} async-done(((bf16[32,2,448]{2,1,0:T(2,128)(2,1)}), bf16[32,2,448]{2,1,0:T(2,128)(2,1)S(1)}, u32[]{:S(2)}, u32[]{:S(2)}) %all-to-all-start) | async-done | bytes 57376 | tf_op jit(solution)/shard_map/all_to_all | solution.py:216
  20.9 0.2 join_rows.1
  21.1 32.4 %all_gather.3.x = bf16[512,896]{1,0:T(8,128)(2,1)S(1)} all-gather(bf16[32,896]{1,0:T(8,128)(2,1)S(1)} %join_rows.1), channel_id=1, replica_groups=mesh['dp'=32,'tensor'=16] {'tensor'}, dimensions={0}, use_global_device_ids=true | all-gather | bytes 974848 | tf_op jit(solution)/shard_map/all_gather | solution.py:231
  53.4 0.0 collective-permute-done.w_next
  53.4 1.3 %away.1 = bf16[512,896]{1,0:T(8,128)(2,1)S(1)} custom-call(s32[1]{0:T(128)} %bitcast.where, bf16[512,896]{1,0:T(8,128)(2,1)S(1)} %all_gather.3.x, bf16[2,448,896]{2,1,0:T(8,128)(2,1)S(1)} %get-tuple-element.5.w_own, bf16[2,448,896]{2,1,0:T(8,128)(2,1)S(1)} %collective-permute-done.w_next), custom_call_target="tpu_custom_call" | custom-call | flops 822083584 | bytes 3440640 | tf_op jit(solution)/shard_map/away/pallas_call | solution.py:111
  54.7 8.7 %collective-permute-start.1 = (bf16[512,896]{1,0:T(8,128)(2,1)S(1)}, bf16[512,896]{1,0:T(8,128)(2,1)S(1)}, u32[]{:S(2)}, u32[]{:S(2)}) collective-permute-start(bf16[512,896]{1,0:T(8,128)(2,1)S(1)} %away.1), channel_id=1, source_target_pairs={{0,16},{16,0},{32,48},{48,32},{64,80},{80,64},{96,112},{112,96},{1... | collective-permute-start | bytes 2752520 | tf_op jit(solution)/shard_map/ppermute | solution.py:234
  63.4 0.2 fusion.route
  63.6 1.3 %home.1.one = bf16[512,896]{1,0:T(8,128)(2,1)S(1)} custom-call(s32[1]{0:T(128)} %bitcast.where, bf16[512,896]{1,0:T(8,128)(2,1)S(1)} %all_gather.3.x, bf16[2,448,896]{2,1,0:T(8,128)(2,1)S(1)} %get-tuple-element.5.w_own, bf16[2,448,896]{2,1,0:T(8,128)(2,1)S(1)} %collective-permute-done.w_next), custom_call_target="tpu_custom_call" | custom-call | flops 822083584 | bytes 3440640 | tf_op jit(solution)/shard_map/home/pallas_call | solution.py:111
  64.9 0.6 collective-permute-done.1.other
  65.5 1.6 %add.154 = bf16[512,896]{1,0:T(8,128)(2,1)} custom-call(bf16[512,896]{1,0:T(8,128)(2,1)S(1)} %home.1.one, bf16[512,896]{1,0:T(8,128)(2,1)S(1)} %collective-permute-done.1.other, bf16[512,512]{1,0:T(8,128)(2,1)S(1)} %fusion.route), custom_call_target="tpu_custom_call" | custom-call | flops 469762048 | bytes 3276800 | tf_op jit(solution)/shard_map/add/pallas_call | solution.py:138
  67.1 4.4 %all-to-all-start.1 = ((bf16[32,16,896]{2,1,0:T(8,128)(2,1)}), bf16[32,16,896]{2,1,0:T(8,128)(2,1)S(1)}, u32[]{:S(2)}, u32[]{:S(2)}) async-start(bf16[32,16,896]{2,1,0:T(8,128)(2,1)} %bitcast.2), calls=%async_computation.1 | async-start | bytes 1835008 | tf_op jit(solution)/shard_map/all_to_all | solution.py:237
  71.5 0.0 copy-start.2
  71.5 0.0 copy-start.3
  71.5 0.1 dynamic_slice.6.lens
  71.6 0.1 dynamic_slice.7
  71.7 15.3 %all-to-all-done.1 = bf16[32,16,896]{2,1,0:T(8,128)(2,1)S(1)} async-done(((bf16[32,16,896]{2,1,0:T(8,128)(2,1)}), bf16[32,16,896]{2,1,0:T(8,128)(2,1)S(1)}, u32[]{:S(2)}, u32[]{:S(2)}) %all-to-all-start.1) | async-done | bytes 917536 | tf_op jit(solution)/shard_map/all_to_all | solution.py:237
  87.0 0.1 convert_reduce_fusion
  87.2 0.1 copy.14
  87.3 0.0 copy-start
  87.3 0.0 copy-done.2
  87.3 0.0 copy-done.3
  87.3 1.4 %attend.1 = bf16[2,896]{1,0:T(2,128)(2,1)} custom-call(s32[2]{0:T(128)S(1)} %dynamic_slice.6.lens, f32[1,128]{1,0:T(1,128)S(1)} %pad_bitcast_fusion.slopes, bf16[2,2,2,8,896]{4,3,2,1,0:T(8,128)(2,1)S(1)} %get-tuple-element.10.cache, bf16[2,896]{1,0:T(2,128)(2,1)S(1)} %copy-done.3, bf16[2,2,896]{2,1,0:T(2,128)(2,1)S(1)} %copy-done.2, ...), custom_call_target="tpu_custom_call" | custom-call | flops 458752 | bytes 114688 | tf_op jit(solution)/shard_map/attend/pallas_call | solution.py:192
  88.7 0.0 copy-done
  (6 shorter events, 0.1 us)
Async XLA Ops:
  0.6 1.7 %copy-start.1 = (bf16[2,14336]{1,0:T(2,128)(2,1)S(1)}, bf16[2,14336]{1,0:T(2,128)(2,1)}, u32[]{:S(2)}) copy-start(bf16[2,14336]{1,0:T(2,128)(2,1)} %rows.1) | copy-start | bytes 172036
  2.3 14.5 %copy-start.4 = (s32[64]{0:T(128)S(1)}, s32[64]{0:T(128)}, u32[]{:S(2)}) copy-start(s32[64]{0:T(128)} %param.8) | copy-start | bytes 772
  2.3 14.5 %copy-start.5 = (s32[64]{0:T(128)S(1)}, s32[64]{0:T(128)}, u32[]{:S(2)}) copy-start(s32[64]{0:T(128)} %param.9) | copy-start | bytes 772
  3.0 17.9 %all-to-all-start = ((bf16[32,2,448]{2,1,0:T(2,128)(2,1)}), bf16[32,2,448]{2,1,0:T(2,128)(2,1)S(1)}, u32[]{:S(2)}, u32[]{:S(2)}) async-start(bf16[32,2,448]{2,1,0:T(2,128)(2,1)} %get-tuple-element.4), calls=%async_computation | async-start | bytes 131072 | tf_op jit(solution)/shard_map/all_to_all | solution.py:216
  13.4 40.0 %collective-permute-start = (bf16[2,448,896]{2,1,0:T(8,128)(2,1)S(1)}, bf16[2,448,896]{2,1,0:T(8,128)(2,1)S(1)}, u32[]{:S(2)}, u32[]{:S(2)}) collective-permute-start(bf16[2,448,896]{2,1,0:T(8,128)(2,1)S(1)} %get-tuple-element.5.w_own), channel_id=1, source_target_pairs={{0,128},{16,48},{32,160},{48,16},{64,192},{80,112},{96,224},{112,8... | collective-permute-start | bytes 4816904 | tf_op jit(solution)/shard_map/ppermute | solution.py:217
  54.7 10.8 %collective-permute-start.1 = (bf16[512,896]{1,0:T(8,128)(2,1)S(1)}, bf16[512,896]{1,0:T(8,128)(2,1)S(1)}, u32[]{:S(2)}, u32[]{:S(2)}) collective-permute-start(bf16[512,896]{1,0:T(8,128)(2,1)S(1)} %away.1), channel_id=1, source_target_pairs={{0,16},{16,0},{32,48},{48,32},{64,80},{80,64},{96,112},{112,96},{1... | collective-permute-start | bytes 2752520 | tf_op jit(solution)/shard_map/ppermute | solution.py:234
  67.1 19.9 %all-to-all-start.1 = ((bf16[32,16,896]{2,1,0:T(8,128)(2,1)}), bf16[32,16,896]{2,1,0:T(8,128)(2,1)S(1)}, u32[]{:S(2)}, u32[]{:S(2)}) async-start(bf16[32,16,896]{2,1,0:T(8,128)(2,1)} %bitcast.2), calls=%async_computation.1 | async-start | bytes 1835008 | tf_op jit(solution)/shard_map/all_to_all | solution.py:237
  71.5 15.8 %copy-start.2 = (bf16[2,2,896]{2,1,0:T(2,128)(2,1)S(1)}, bf16[2,2,896]{2,1,0:T(2,128)(2,1)}, u32[]{:S(2)}) copy-start(bf16[2,2,896]{2,1,0:T(2,128)(2,1)} %new_kv.1) | copy-start | bytes 21508
  71.5 15.8 %copy-start.3 = (bf16[2,896]{1,0:T(2,128)(2,1)S(1)}, bf16[2,896]{1,0:T(2,128)(2,1)}, u32[]{:S(2)}) copy-start(bf16[2,896]{1,0:T(2,128)(2,1)} %query.1) | copy-start | bytes 10756
  87.3 1.5 %copy-start = (bf16[2,8,2,2,896]{4,3,2,1,0:T(2,128)(2,1)}, bf16[2,8,2,2,896]{4,3,2,1,0:T(2,128)(2,1)S(1)}, u32[]{:S(2)}) copy-start(bf16[2,8,2,2,896]{4,3,2,1,0:T(2,128)(2,1)S(1)} %copy.14) | copy-start | bytes 344068

commit v11 on v10

--- a/solution.py
+++ b/solution.py
@@ -45,8 +45,8 @@
     groups, share, block = sent.shape
     for to in range(groups):
         row = parity(to)
-        for part, at in enumerate((to, partner(to))):
-            sent[to, part : part + 1, :] = rows[row : row + 1, at * block : (at + 1) * block]
+        parts = [rows[row : row + 1, at * block : (at + 1) * block] for at in (to, partner(to))]
+        sent[to] = jnp.concatenate(parts, axis=0)
 
 
 def split_rows(rows, weights, groups):

time: 89.1 us -> 89.1 us (level)
  no operation moved by 1% of the time
where the time goes in v11:
time: 89.1 us; the launch traced here: 88.7 us
  blocking collectives  32.4 us (36%)
  starting transfers between devices  26.8 us (30%)
  waiting for transfers between devices  19.7 us (22%)
  Pallas kernels  6.47 us (7%)
  local copies, waits for them, and re-layouts  2 us (2%)
    all_gather x1, blocking collectives, per_device(): every = lax.all_gather(join_rows(parts, row), 'tensor', axis=0, tiled=True)  32.4 us
    all_to_all x1, waiting for transfers between devices, per_device(): lax.all_to_all(partial.reshape(groups, REQ_DEV * steps, columns), 'dp', s...  15.3 us
    all_to_all x1, starting transfers between devices, per_device(): parts = lax.all_to_all(sent, 'dp', split_axis=0, concat_axis=0, tiled=True)  10.4 us
    ppermute x1, starting transfers between devices, per_device(): received = lax.ppermute(away, 'dp', [(i, i ^ 1) for i in range(groups)])  8.69 us
    all_to_all x1, starting transfers between devices, per_device(): lax.all_to_all(partial.reshape(groups, REQ_DEV * steps, columns), 'dp', s...  4.43 us
    all_to_all x1, waiting for transfers between devices, per_device(): parts = lax.all_to_all(sent, 'dp', split_axis=0, concat_axis=0, tiled=True)  3.81 us
    ppermute x1, starting transfers between devices, per_device(): w_next = lax.ppermute(w_own, 'dp', [(i, partner(i)) for i in range(groups)])  3.3 us
    pallas_call x2, Pallas kernels, product(): pl.pallas_call(functools.partial(product_kernel, home), out_shape=jax.Sha...  2.59 us
  transfers between devices with their start and end apart: 4, of which 3 were waited for; matrix products, arithmetic and copies ran while one was open for 1% of the time, Pallas kernels for 2%

profile of v11, /device:TPU:1, one launch (start us, length us, event | category | flops | bytes accessed | tf_op | source)
XLA Modules:
  0.0 88.7 jit_solution(4706979216769169987)
XLA Ops:
  0.6 0.0 copy-start.1
  0.6 1.6 %copy.16 = bf16[448,2,896]{2,0,1:T(8,128)(2,1)S(1)} copy(bf16[448,2,896]{2,1,0:T(2,128)(2,1)} %param.7) | data formatting | bytes 3211264 | tf_op args[1]
  2.3 0.0 copy-start.4
  2.3 0.0 copy-start.5
  2.3 0.0 copy-done.1
  2.3 0.7 split_rows.1
  3.0 10.4 %all-to-all-start = ((bf16[32,2,448]{2,1,0:T(2,128)(2,1)}), bf16[32,2,448]{2,1,0:T(2,128)(2,1)S(1)}, u32[]{:S(2)}, u32[]{:S(2)}) async-start(bf16[32,2,448]{2,1,0:T(2,128)(2,1)} %get-tuple-element.4), calls=%async_computation | async-start | bytes 131072 | tf_op jit(solution)/shard_map/all_to_all | solution.py:216
  13.4 3.3 %collective-permute-start = (bf16[2,448,896]{2,1,0:T(8,128)(2,1)S(1)}, bf16[2,448,896]{2,1,0:T(8,128)(2,1)S(1)}, u32[]{:S(2)}, u32[]{:S(2)}) collective-permute-start(bf16[2,448,896]{2,1,0:T(8,128)(2,1)S(1)} %get-tuple-element.5.w_own), channel_id=1, source_target_pairs={{0,128},{16,48},{32,160},{48,16},{64,192},{80,112},{96,224},{112,8... | collective-permute-start | bytes 4816904 | tf_op jit(solution)/shard_map/ppermute | solution.py:217
  16.8 0.0 copy-done.4
  16.8 0.0 copy-done.5
  16.8 0.1 select_reduce_fusion.1
  16.9 0.1 add_select_fusion
  17.0 0.1 select_n.54.row
  17.1 3.8 %all-to-all-done.parts = bf16[32,2,448]{2,1,0:T(2,128)(2,1)S(1)} async-done(((bf16[32,2,448]{2,1,0:T(2,128)(2,1)}), bf16[32,2,448]{2,1,0:T(2,128)(2,1)S(1)}, u32[]{:S(2)}, u32[]{:S(2)}) %all-to-all-start) | async-done | bytes 57376 | tf_op jit(solution)/shard_map/all_to_all | solution.py:216
  20.9 0.2 join_rows.1
  21.1 32.4 %all_gather.3.x = bf16[512,896]{1,0:T(8,128)(2,1)S(1)} all-gather(bf16[32,896]{1,0:T(8,128)(2,1)S(1)} %join_rows.1), channel_id=1, replica_groups=mesh['dp'=32,'tensor'=16] {'tensor'}, dimensions={0}, use_global_device_ids=true | all-gather | bytes 974848 | tf_op jit(solution)/shard_map/all_gather | solution.py:231
  53.4 0.0 collective-permute-done.w_next
  53.4 1.3 %away.1 = bf16[512,896]{1,0:T(8,128)(2,1)S(1)} custom-call(s32[1]{0:T(128)} %bitcast.where, bf16[512,896]{1,0:T(8,128)(2,1)S(1)} %all_gather.3.x, bf16[2,448,896]{2,1,0:T(8,128)(2,1)S(1)} %get-tuple-element.5.w_own, bf16[2,448,896]{2,1,0:T(8,128)(2,1)S(1)} %collective-permute-done.w_next), custom_call_target="tpu_custom_call" | custom-call | flops 822083584 | bytes 3440640 | tf_op jit(solution)/shard_map/away/pallas_call | solution.py:111
  54.7 8.7 %collective-permute-start.1 = (bf16[512,896]{1,0:T(8,128)(2,1)S(1)}, bf16[512,896]{1,0:T(8,128)(2,1)S(1)}, u32[]{:S(2)}, u32[]{:S(2)}) collective-permute-start(bf16[512,896]{1,0:T(8,128)(2,1)S(1)} %away.1), channel_id=1, source_target_pairs={{0,16},{16,0},{32,48},{48,32},{64,80},{80,64},{96,112},{112,96},{1... | collective-permute-start | bytes 2752520 | tf_op jit(solution)/shard_map/ppermute | solution.py:234
  63.4 0.2 fusion.route
  63.6 1.3 %home.1.one = bf16[512,896]{1,0:T(8,128)(2,1)S(1)} custom-call(s32[1]{0:T(128)} %bitcast.where, bf16[512,896]{1,0:T(8,128)(2,1)S(1)} %all_gather.3.x, bf16[2,448,896]{2,1,0:T(8,128)(2,1)S(1)} %get-tuple-element.5.w_own, bf16[2,448,896]{2,1,0:T(8,128)(2,1)S(1)} %collective-permute-done.w_next), custom_call_target="tpu_custom_call" | custom-call | flops 822083584 | bytes 3440640 | tf_op jit(solution)/shard_map/home/pallas_call | solution.py:111
  64.9 0.6 collective-permute-done.1.other
  65.5 1.6 %add.154 = bf16[512,896]{1,0:T(8,128)(2,1)} custom-call(bf16[512,896]{1,0:T(8,128)(2,1)S(1)} %home.1.one, bf16[512,896]{1,0:T(8,128)(2,1)S(1)} %collective-permute-done.1.other, bf16[512,512]{1,0:T(8,128)(2,1)S(1)} %fusion.route), custom_call_target="tpu_custom_call" | custom-call | flops 469762048 | bytes 3276800 | tf_op jit(solution)/shard_map/add/pallas_call | solution.py:138
  67.1 4.4 %all-to-all-start.1 = ((bf16[32,16,896]{2,1,0:T(8,128)(2,1)}), bf16[32,16,896]{2,1,0:T(8,128)(2,1)S(1)}, u32[]{:S(2)}, u32[]{:S(2)}) async-start(bf16[32,16,896]{2,1,0:T(8,128)(2,1)} %bitcast.2), calls=%async_computation.1 | async-start | bytes 1835008 | tf_op jit(solution)/shard_map/all_to_all | solution.py:237
  71.5 0.0 copy-start.2
  71.5 0.0 copy-start.3
  71.5 0.1 dynamic_slice.6.lens
  71.6 0.1 dynamic_slice.7
  71.7 15.3 %all-to-all-done.1 = bf16[32,16,896]{2,1,0:T(8,128)(2,1)S(1)} async-done(((bf16[32,16,896]{2,1,0:T(8,128)(2,1)}), bf16[32,16,896]{2,1,0:T(8,128)(2,1)S(1)}, u32[]{:S(2)}, u32[]{:S(2)}) %all-to-all-start.1) | async-done | bytes 917536 | tf_op jit(solution)/shard_map/all_to_all | solution.py:237
  87.0 0.1 convert_reduce_fusion
  87.2 0.1 copy.14
  87.3 0.0 copy-start
  87.3 0.0 copy-done.2
  87.3 0.0 copy-done.3
  87.3 1.4 %attend.1 = bf16[2,896]{1,0:T(2,128)(2,1)} custom-call(s32[2]{0:T(128)S(1)} %dynamic_slice.6.lens, f32[1,128]{1,0:T(1,128)S(1)} %pad_bitcast_fusion.slopes, bf16[2,2,2,8,896]{4,3,2,1,0:T(8,128)(2,1)S(1)} %get-tuple-element.10.cache, bf16[2,896]{1,0:T(2,128)(2,1)S(1)} %copy-done.3, bf16[2,2,896]{2,1,0:T(2,128)(2,1)S(1)} %copy-done.2, ...), custom_call_target="tpu_custom_call" | custom-call | flops 458752 | bytes 114688 | tf_op jit(solution)/shard_map/attend/pallas_call | solution.py:192
  88.7 0.0 copy-done
  (6 shorter events, 0.1 us)
Async XLA Ops:
  0.6 1.7 %copy-start.1 = (bf16[2,14336]{1,0:T(2,128)(2,1)S(1)}, bf16[2,14336]{1,0:T(2,128)(2,1)}, u32[]{:S(2)}) copy-start(bf16[2,14336]{1,0:T(2,128)(2,1)} %rows.1) | copy-start | bytes 172036
  2.3 14.5 %copy-start.4 = (s32[64]{0:T(128)S(1)}, s32[64]{0:T(128)}, u32[]{:S(2)}) copy-start(s32[64]{0:T(128)} %param.8) | copy-start | bytes 772
  2.3 14.5 %copy-start.5 = (s32[64]{0:T(128)S(1)}, s32[64]{0:T(128)}, u32[]{:S(2)}) copy-start(s32[64]{0:T(128)} %param.9) | copy-start | bytes 772
  3.0 17.9 %all-to-all-start = ((bf16[32,2,448]{2,1,0:T(2,128)(2,1)}), bf16[32,2,448]{2,1,0:T(2,128)(2,1)S(1)}, u32[]{:S(2)}, u32[]{:S(2)}) async-start(bf16[32,2,448]{2,1,0:T(2,128)(2,1)} %get-tuple-element.4), calls=%async_computation | async-start | bytes 131072 | tf_op jit(solution)/shard_map/all_to_all | solution.py:216
  13.4 40.0 %collective-permute-start = (bf16[2,448,896]{2,1,0:T(8,128)(2,1)S(1)}, bf16[2,448,896]{2,1,0:T(8,128)(2,1)S(1)}, u32[]{:S(2)}, u32[]{:S(2)}) collective-permute-start(bf16[2,448,896]{2,1,0:T(8,128)(2,1)S(1)} %get-tuple-element.5.w_own), channel_id=1, source_target_pairs={{0,128},{16,48},{32,160},{48,16},{64,192},{80,112},{96,224},{112,8... | collective-permute-start | bytes 4816904 | tf_op jit(solution)/shard_map/ppermute | solution.py:217
  54.7 10.8 %collective-permute-start.1 = (bf16[512,896]{1,0:T(8,128)(2,1)S(1)}, bf16[512,896]{1,0:T(8,128)(2,1)S(1)}, u32[]{:S(2)}, u32[]{:S(2)}) collective-permute-start(bf16[512,896]{1,0:T(8,128)(2,1)S(1)} %away.1), channel_id=1, source_target_pairs={{0,16},{16,0},{32,48},{48,32},{64,80},{80,64},{96,112},{112,96},{1... | collective-permute-start | bytes 2752520 | tf_op jit(solution)/shard_map/ppermute | solution.py:234
  67.1 19.9 %all-to-all-start.1 = ((bf16[32,16,896]{2,1,0:T(8,128)(2,1)}), bf16[32,16,896]{2,1,0:T(8,128)(2,1)S(1)}, u32[]{:S(2)}, u32[]{:S(2)}) async-start(bf16[32,16,896]{2,1,0:T(8,128)(2,1)} %bitcast.2), calls=%async_computation.1 | async-start | bytes 1835008 | tf_op jit(solution)/shard_map/all_to_all | solution.py:237
  71.5 15.8 %copy-start.2 = (bf16[2,2,896]{2,1,0:T(2,128)(2,1)S(1)}, bf16[2,2,896]{2,1,0:T(2,128)(2,1)}, u32[]{:S(2)}) copy-start(bf16[2,2,896]{2,1,0:T(2,128)(2,1)} %new_kv.1) | copy-start | bytes 21508
  71.5 15.8 %copy-start.3 = (bf16[2,896]{1,0:T(2,128)(2,1)S(1)}, bf16[2,896]{1,0:T(2,128)(2,1)}, u32[]{:S(2)}) copy-start(bf16[2,896]{1,0:T(2,128)(2,1)} %query.1) | copy-start | bytes 10756
  87.3 1.5 %copy-start = (bf16[2,8,2,2,896]{4,3,2,1,0:T(2,128)(2,1)}, bf16[2,8,2,2,896]{4,3,2,1,0:T(2,128)(2,1)S(1)}, u32[]{:S(2)}) copy-start(bf16[2,8,2,2,896]{4,3,2,1,0:T(2,128)(2,1)S(1)} %copy.14) | copy-start | bytes 344068
